TPU v7x, 32 devices: a whole 2x2x4 slice. The times are simulated.
32 devices in a mesh: row: 8 (over z, y), col: 4 (over x, core).
Axes of the slice: x: 2, y: 2, z: 4, core: 2. Of those that a mesh axis runs over, the one named last changes fastest.
Arguments:
- volume: bfloat16 [48, 32, 128, 32], P(None, ('row', 'col')), may hold values from -6 to 6
- norm_gain: float32 [2, 48], replicated, may hold values from 0.1 to 1.9
- in_proj: bfloat16 [2, 320, 48], replicated, may hold values from -0.875 to 0.875
- dt_proj: bfloat16 [2, 3, 48], replicated, may hold values from -0.875 to 0.875
- dt_bias: float32 [2, 3], replicated, may hold values from -2 to 1
- decay_rate: float32 [2, 3], replicated, may hold values from 2e-07 to 0.05
- conv_weight: float32 [2, 224, 4], replicated, may hold values from -3 to 3
- conv_bias: float32 [2, 224], replicated, may hold values from -3 to 3
- skip_gain: float32 [2, 3], replicated, may hold values from 0.5 to 1.5
- out_gain: float32 [2, 96], replicated, may hold values from 0.1 to 1.9
- out_proj: bfloat16 [2, 48, 96], replicated, may hold values from -0.625 to 0.625
- head_weight: bfloat16 [14, 48], replicated, may hold values from -2.6875 to 2.6875
- head_bias: float32 [14], replicated, may hold values from -6 to 6
- labels: int32 [32, 32, 128], P(('row', 'col')), may hold values from 0 to 13
- distance: int32 [14, 32, 32, 128], P(None, ('row', 'col')), may hold values from -16384 to 16384
Outputs:
- features: bfloat16 [48, 32, 32, 128], P(None, ('row', 'col'))
- logit_grad: float32 [14, 32, 32, 128], P(None, ('row', 'col'))
- total_loss: float32 [], replicated
All inputs are finite; a program needn't handle non-finite values.
Results may differ from a plain program's by a relative error of at most 0.006.
The roundings to bfloat16 on the way count: a program that leaves them out, or rounds other values in their place, can miss the bound.
Values may be sent and summed in bfloat16 or wider, within the bound.
No kernel may reach another device: no remote copies, remote signals or barrier semaphores. Data moves between devices by JAX's collectives and lax.ppermute only.
A program may use at most 192 MiB of HBM per device.

v0:
```python
import functools

import jax
import jax.numpy as jnp
from jax import lax
from jax.experimental import pallas as pl
from jax.experimental.pallas import tpu as pltpu
from jax.sharding import PartitionSpec as P

SCAN_BLOCK = 128
LANES = 128

eps = 1e-05
dist_unit = 4096.0
axes = ("row", "col")
f32, bf16 = jnp.float32, jnp.bfloat16
vmem_bytes = 48 * 1024 * 1024


def silu(v):
    return 0.5 * v * (1.0 + jnp.tanh(0.5 * v))


def rounded(v):
    return v.astype(bf16).astype(f32)


def normalise(hidden, gain_col):
    values = hidden.astype(f32)
    mean_sq = jnp.mean(values * values, axis=0, keepdims=True)
    return (values * lax.rsqrt(mean_sq + eps) * gain_col).astype(bf16)


def project(weight, normed):
    return jnp.dot(weight, normed, preferred_element_type=f32)


def contract(a, b, dim):
    return lax.dot_general(a, b, (((dim,), (dim,)), ((), ())), preferred_element_type=f32)


def spread(rows, first, count, height):
    return jnp.concatenate(
        [jnp.broadcast_to(rows[first + h : first + h + 1], (height, rows.shape[1])) for h in range(count)], axis=0
    )


def taps(conv_in, moved_ref, cols, first):
    rows = conv_in.shape[0]
    lane = lax.broadcasted_iota(jnp.int32, (rows, SCAN_BLOCK), 1)
    tap_count = moved_ref.shape[0] + 1
    total = cols[first : first + rows, tap_count : tap_count + 1] + jnp.zeros((rows, SCAN_BLOCK), f32)
    for offset in range(tap_count):
        lag = tap_count - 1 - offset
        if lag:
            now = pltpu.roll(conv_in, lag, 1)
            shifted = jnp.where(lane < lag, moved_ref[lag - 1], now)
            moved_ref[lag - 1] = now
        else:
            shifted = conv_in
        total = total + cols[first : first + rows, offset : offset + 1] * shifted
    return total


def keep_tail(tail_in, moved_ref):
    for lag in range(1, moved_ref.shape[0] + 1):
        moved_ref[lag - 1] = pltpu.roll(tail_in, lag, 1)


def state_kernel(
    heads, hid_ref, tail_ref, weight_ref, dt_ref, cols_ref, gain_ref, head_ref, tri_ref,
    inner_ref, write_ref, dec_ref, state_ref, total_ref, moved_ref, carry_ref,
):
    group = hid_ref.shape[0]
    inner = inner_ref.shape[1]
    width = inner // heads
    state = write_ref.shape[1]
    weight = weight_ref[...]
    gain_col = gain_ref[...]
    cols = cols_ref[...]
    head_cols = head_ref[...]

    @pl.when(pl.program_id(0) == 0)
    def _():
        carry_ref[...] = jnp.zeros_like(carry_ref)
        tail_in = rounded(project(weight, normalise(tail_ref[...], gain_col)))
        keep_tail(tail_in, moved_ref)

    lane = lax.broadcasted_iota(jnp.int32, (1, LANES), 1)
    normed = [normalise(hid_ref[u], gain_col) for u in range(group)]
    dt_raw = [project(dt_ref[...], n) for n in normed]
    step = [v + head_cols[:, 0:1] for v in dt_raw]
    step = [jnp.maximum(v, 0.0) + jnp.log1p(jnp.exp(-jnp.abs(v))) for v in step]
    log_decay = jnp.concatenate([head_cols[:, 1:2] * v for v in step], axis=0)
    high = log_decay.astype(bf16)
    rest = log_decay - high.astype(f32)
    middle = rest.astype(bf16)
    low = (rest - middle.astype(f32)).astype(bf16)
    tri = tri_ref[...]
    cum_all = project(low, tri) + project(middle, tri) + project(high, tri)
    for u in range(group):
        cum = cum_all[8 * u : 8 * u + 8]
        last = jnp.broadcast_to(cum[:, SCAN_BLOCK - 1 :], cum.shape)
        carry_weight = jnp.exp(last - cum) * step[u]
        dec_ref[u, 0:8, :] = cum
        dec_ref[u, 8:16, :] = step[u]
        conv_in = rounded(project(weight, normed[u]))
        conv_out = silu(taps(conv_in, moved_ref, cols, 0)).astype(bf16)
        inner_values = conv_out[:inner]
        write = conv_out[inner:]
        inner_ref[u] = inner_values
        write_ref[u] = write
        scaled = inner_values.astype(f32) * spread(carry_weight, 0, heads, width)
        scaled = jnp.concatenate([scaled, jnp.zeros((LANES - inner, SCAN_BLOCK), f32)], axis=0)
        block_state = contract(write, scaled.astype(bf16), 1)
        decay_row = last[heads - 1 : heads]
        for h in range(heads - 2, -1, -1):
            decay_row = jnp.where(lane < (h + 1) * width, last[h : h + 1], decay_row)
        state_ref[u] = carry_ref[...]
        carry_ref[0:state, :] = jnp.exp(decay_row) * carry_ref[0:state, :] + block_state
        carry_ref[state:, :] = carry_ref[state:, :] + decay_row
    total_ref[...] = carry_ref[...]


def local_kernel(
    heads, hid_ref, tail_ref, weight_ref, cols_ref, gain_ref, head_ref, inner_ref, write_ref, dec_ref,
    local_ref, gate_ref, read_ref, moved_ref,
):
    group = hid_ref.shape[0]
    inner = inner_ref.shape[1]
    width = inner // heads
    weight = weight_ref[...]
    gain_col = gain_ref[...]
    cols = cols_ref[...]
    head_cols = head_ref[...]
    conv_first = cols.shape[0] - read_ref.shape[1]

    @pl.when(pl.program_id(0) == 0)
    def _():
        tail_in = rounded(project(weight[inner:], normalise(tail_ref[...], gain_col)))
        keep_tail(tail_in, moved_ref)

    source = lax.broadcasted_iota(jnp.int32, (SCAN_BLOCK, SCAN_BLOCK), 0)
    target = lax.broadcasted_iota(jnp.int32, (SCAN_BLOCK, SCAN_BLOCK), 1)
    causal = source <= target
    for u in range(group):
        normed = normalise(hid_ref[u], gain_col)
        projected = rounded(project(weight, normed))
        gate_ref[u] = silu(projected[:inner])
        read = silu(taps(projected[inner:], moved_ref, cols, conv_first)).astype(bf16)
        read_ref[u] = read
        scores = contract(write_ref[u], read, 0)
        cum = dec_ref[u, 0:8, :]
        step = dec_ref[u, 8:16, :]
        source_cols = jnp.transpose(cum - jnp.log(step), (1, 0))
        for h in range(heads):
            gap = jnp.where(causal, cum[h : h + 1] - source_cols[:, h : h + 1], -jnp.inf)
            weights = (scores * jnp.exp(gap)).astype(bf16)
            values = inner_ref[u, h * width : (h + 1) * width, :]
            local_ref[u, h * width : (h + 1) * width, :] = (
                project(values, weights) + head_cols[h : h + 1, 2:3] * values.astype(f32)
            )


def finished(u, heads, enter, hid_ref, local_ref, gate_ref, read_ref, dec_ref, state_ref, out_gain, out_proj):
    inner = local_ref.shape[1]
    width = inner // heads
    state = read_ref.shape[1]
    entering = jnp.exp(state_ref[u, state : state + 1, :]) * enter + state_ref[u, 0:state, :]
    inter = contract(entering.astype(bf16), read_ref[u], 0)[:inner]
    scan_out = local_ref[u] + spread(jnp.exp(dec_ref[u, 0:8, :]), 0, heads, width) * inter
    gated = scan_out * gate_ref[u]
    mean_sq = jnp.mean(gated * gated, axis=0, keepdims=True)
    gated = (gated * lax.rsqrt(mean_sq + eps) * out_gain).astype(bf16)
    return (hid_ref[u].astype(f32) + project(out_proj, gated)).astype(bf16)


def finish_kernel(
    heads, enter_ref, hid_ref, local_ref, gate_ref, read_ref, dec_ref, state_ref, gain_ref, proj_ref, out_ref
):
    enter = enter_ref[0 : read_ref.shape[1], :]
    for u in range(hid_ref.shape[0]):
        out_ref[u] = finished(
            u, heads, enter, hid_ref, local_ref, gate_ref, read_ref, dec_ref, state_ref, gain_ref[...], proj_ref[...]
        )


def head_kernel(
    heads, enter_ref, hid_ref, local_ref, gate_ref, read_ref, dec_ref, state_ref, gain_ref, proj_ref,
    head_ref, bias_ref, labels_ref, distance_ref, features_ref, grad_ref, loss_ref, feature_scr, logit_scr,
):
    group = hid_ref.shape[0]
    classes = distance_ref.shape[0]
    enter = enter_ref[0 : read_ref.shape[1], :]

    @pl.when(pl.program_id(0) == 0)
    def _():
        loss_ref[...] = jnp.zeros_like(loss_ref)

    for u in range(group):
        result = finished(
            u, heads, enter, hid_ref, local_ref, gate_ref, read_ref, dec_ref, state_ref, gain_ref[...], proj_ref[...]
        )
        logits = project(head_ref[...], result) + bias_ref[...]
        feature_scr[pl.ds(u, result.shape[0], stride=group), :] = result.astype(f32)
        logit_scr[pl.ds(u, logits.shape[0], stride=group), :] = logits
    features = feature_scr[...].reshape(-1, group, SCAN_BLOCK)
    features_ref[...] = features.astype(bf16)
    logits = logit_scr[...].reshape(-1, group, SCAN_BLOCK)[:classes]
    labels = labels_ref[...]
    peak = jnp.max(logits, axis=0)
    shifted = jnp.exp(logits - peak[None])
    partition = jnp.sum(shifted, axis=0)
    probability = shifted / partition[None]
    distance_map = distance_ref[...].astype(f32) * (1.0 / dist_unit)
    weighted = probability * distance_map
    expect = jnp.sum(weighted, axis=0)
    hot = labels[None] == lax.broadcasted_iota(jnp.int32, logits.shape, 0)
    chosen = jnp.sum(jnp.where(hot, logits, 0.0), axis=0)
    loss = peak + jnp.log(partition) - chosen + expect
    grad_ref[...] = probability - jnp.where(hot, 1.0, 0.0) + weighted - probability * expect[None]
    loss_ref[...] += jnp.sum(loss.reshape(-1, 8, SCAN_BLOCK), axis=0)


def whole(shape):
    return pl.BlockSpec(shape, lambda g: (0,) * len(shape))


def blocks(group, *rest):
    return pl.BlockSpec((group,) + rest, lambda g: (g,) + (0,) * len(rest))


def params():
    return pltpu.CompilerParams(vmem_limit_bytes=vmem_bytes)


def prefix_state(total):
    size = lax.axis_size(axes)
    me = lax.axis_index(axes)
    rows = total.shape[0] - 8

    def combine(earlier, latter):
        log = latter[rows : rows + 1]
        return jnp.concatenate(
            [jnp.exp(log) * earlier[:rows] + latter[:rows], earlier[rows:] + latter[rows:]], axis=0
        )

    before = jnp.zeros_like(total)
    reach = 1
    while reach < size:
        other = lax.ppermute(total, axes, [(i, i ^ reach) for i in range(size)])
        upper = (me & reach) != 0
        before = jnp.where(upper, combine(other, before), before)
        if 2 * reach < size:
            total = combine(jnp.where(upper, other, total), jnp.where(upper, total, other))
        reach *= 2
    return before


def layer_start(hidden, tail, prep, group):
    count, model, _ = hidden.shape
    heads, inner, state = prep["heads"], prep["inner"], prep["state"]
    steps = count // group
    conv_cols = prep["cols"]
    tile = lambda rows, kind: jax.ShapeDtypeStruct((count, rows, SCAN_BLOCK), kind)
    first_rows = inner + state
    inner_values, write, dec, states, total = pl.pallas_call(
        functools.partial(state_kernel, heads),
        grid=(steps,),
        in_specs=[
            blocks(group, model, SCAN_BLOCK),
            whole((model, SCAN_BLOCK)),
            whole((first_rows, model)),
            whole((8, model)),
            whole(conv_cols.shape),
            whole((model, 1)),
            whole((8, 8)),
            whole((SCAN_BLOCK, SCAN_BLOCK)),
        ],
        out_specs=[
            blocks(group, inner, SCAN_BLOCK),
            blocks(group, state, SCAN_BLOCK),
            blocks(group, 16, SCAN_BLOCK),
            blocks(group, state + 8, LANES),
            whole((state + 8, LANES)),
        ],
        out_shape=[
            tile(inner, bf16),
            tile(state, bf16),
            tile(16, f32),
            tile(state + 8, f32),
            jax.ShapeDtypeStruct((state + 8, LANES), f32),
        ],
        scratch_shapes=[
            pltpu.VMEM((prep["taps"] - 1, first_rows, SCAN_BLOCK), f32),
            pltpu.VMEM((state + 8, LANES), f32),
        ],
        compiler_params=params(),
        name="states",
    )(
        hidden, tail, prep["in_first"], prep["dt_proj"], conv_cols, prep["gain"], prep["head_cols"], prep["tri"]
    )
    local, gate, read = pl.pallas_call(
        functools.partial(local_kernel, heads),
        grid=(steps,),
        in_specs=[
            blocks(group, model, SCAN_BLOCK),
            whole((model, SCAN_BLOCK)),
            whole((first_rows, model)),
            whole(conv_cols.shape),
            whole((model, 1)),
            whole((8, 8)),
            blocks(group, inner, SCAN_BLOCK),
            blocks(group, state, SCAN_BLOCK),
            blocks(group, 16, SCAN_BLOCK),
        ],
        out_specs=[
            blocks(group, inner, SCAN_BLOCK),
            blocks(group, inner, SCAN_BLOCK),
            blocks(group, state, SCAN_BLOCK),
        ],
        out_shape=[tile(inner, f32), tile(inner, f32), tile(state, bf16)],
        scratch_shapes=[pltpu.VMEM((prep["taps"] - 1, state, SCAN_BLOCK), f32)],
        compiler_params=params(),
        name="local",
    )(
        hidden, tail, prep["in_second"], conv_cols, prep["gain"], prep["head_cols"], inner_values, write, dec
    )
    enter = prefix_state(total)
    return enter, local, gate, read, dec, states


def finish_specs(group, model, inner, state):
    return [
        whole((state + 8, LANES)),
        blocks(group, model, SCAN_BLOCK),
        blocks(group, inner, SCAN_BLOCK),
        blocks(group, inner, SCAN_BLOCK),
        blocks(group, state, SCAN_BLOCK),
        blocks(group, 16, SCAN_BLOCK),
        blocks(group, state + 8, LANES),
        whole((inner, 1)),
        whole((model, inner)),
    ]


def prepare(norm_gain, in_proj, dt_proj, dt_bias, decay_rate, conv_weight, conv_bias, skip_gain, out_gain, out_proj):
    inner = out_proj.shape[1]
    heads = decay_rate.shape[0]
    state = (in_proj.shape[0] - 2 * inner) // 2
    tap_count = conv_weight.shape[1]
    cols = jnp.concatenate([conv_weight, conv_bias[:, None]], axis=1)
    cols = jnp.pad(cols, ((0, 0), (0, 8 - cols.shape[1])))
    head_cols = jnp.stack([dt_bias, -decay_rate, skip_gain], axis=1)
    return dict(
        heads=heads,
        inner=inner,
        state=state,
        taps=tap_count,
        cols=cols,
        gain=norm_gain[:, None],
        in_first=in_proj[inner : 2 * inner + state],
        in_second=jnp.concatenate([in_proj[:inner], in_proj[2 * inner + state :]], axis=0),
        dt_proj=jnp.pad(dt_proj, ((0, 8 - heads), (0, 0))),
        head_cols=jnp.pad(head_cols, ((0, 8 - heads), (0, 8 - head_cols.shape[1]))),
        out_gain=out_gain[:, None],
        out_proj=out_proj,
        tri=(
            lax.broadcasted_iota(jnp.int32, (SCAN_BLOCK, SCAN_BLOCK), 0)
            <= lax.broadcasted_iota(jnp.int32, (SCAN_BLOCK, SCAN_BLOCK), 1)
        ).astype(bf16),
    )


def per_device(
    volume, norm_gain, in_proj, dt_proj, dt_bias, decay_rate, conv_weight, conv_bias, skip_gain, out_gain,
    out_proj, head_weight, head_bias, labels, distance,
):
    arrays = (
        norm_gain, in_proj, dt_proj, dt_bias, decay_rate, conv_weight, conv_bias, skip_gain, out_gain, out_proj
    )
    size = lax.axis_size(axes)
    me = lax.axis_index(axes)
    model, _, cells_y, cells_x = volume.shape
    classes = head_weight.shape[0]
    prep = [prepare(*(entry[b] for entry in arrays)) for b in range(2)]
    heads, inner, state = (prep[0][k] for k in ("heads", "inner", "state"))
    forward = [(i, i + 1) for i in range(size - 1)]
    count = cells_y * cells_x // SCAN_BLOCK
    group = min(16, count)

    hidden = volume.reshape(model, count, SCAN_BLOCK).transpose(1, 0, 2)
    tail = lax.ppermute(hidden[-1], axes, forward)
    parts = layer_start(hidden, tail, prep[0], group)
    enter, local, gate, read, dec, states = parts
    after = pl.pallas_call(
        functools.partial(finish_kernel, heads),
        grid=(count // group,),
        in_specs=finish_specs(group, model, inner, state),
        out_specs=blocks(group, model, SCAN_BLOCK),
        out_shape=jax.ShapeDtypeStruct(hidden.shape, bf16),
        compiler_params=params(),
        name="finish",
    )(enter, hidden, local, gate, read, dec, states, prep[0]["out_gain"], prep[0]["out_proj"])

    planes = after.transpose(1, 0, 2).reshape(model, cells_y, cells_x).transpose(2, 0, 1)
    hidden = lax.all_to_all(planes, axes, split_axis=0, concat_axis=0, tiled=True)
    count = hidden.shape[0]
    group = min(16, count)
    tail = lax.ppermute(hidden[-1], axes, forward)
    parts = layer_start(hidden, tail, prep[1], group)
    enter, local, gate, read, dec, states = parts
    pad_classes = 16
    head_pad = jnp.pad(head_weight, ((0, pad_classes - classes), (0, 0)))
    bias_pad = jnp.pad(head_bias, (0, pad_classes - classes))[:, None]
    plane = lambda rows: pl.BlockSpec((rows, group, SCAN_BLOCK), lambda g: (0, g, 0))
    features, grad, loss = pl.pallas_call(
        functools.partial(head_kernel, heads),
        grid=(count // group,),
        in_specs=finish_specs(group, model, inner, state)
        + [
            whole((pad_classes, model)),
            whole((pad_classes, 1)),
            pl.BlockSpec((group, SCAN_BLOCK), lambda g: (g, 0)),
            plane(classes),
        ],
        out_specs=[plane(model), plane(classes), whole((8, SCAN_BLOCK))],
        out_shape=[
            jax.ShapeDtypeStruct((model, count, SCAN_BLOCK), bf16),
            jax.ShapeDtypeStruct((classes, count, SCAN_BLOCK), f32),
            jax.ShapeDtypeStruct((8, SCAN_BLOCK), f32),
        ],
        scratch_shapes=[
            pltpu.VMEM((model * group, SCAN_BLOCK), f32),
            pltpu.VMEM((pad_classes * group, SCAN_BLOCK), f32),
        ],
        compiler_params=params(),
        name="heads",
    )(
        enter, hidden, local, gate, read, dec, states, prep[1]["out_gain"], prep[1]["out_proj"],
        head_pad, bias_pad, labels.reshape(count, SCAN_BLOCK), distance.reshape(classes, count, SCAN_BLOCK),
    )
    voxel_weight = 1.0 + 3.0 * me.astype(f32) / (size - 1.0)
    voxel_count = count * SCAN_BLOCK * size
    own = voxel_weight * jnp.sum(loss, axis=0, keepdims=True)
    shared = lax.all_to_all(jnp.broadcast_to(own, (size, SCAN_BLOCK)), axes, 0, 0, tiled=True)
    total_loss = jnp.sum(shared) / (2.5 * voxel_count)
    return (
        features.reshape(model, 1, count, SCAN_BLOCK),
        grad.reshape(classes, 1, count, SCAN_BLOCK),
        total_loss,
    )


def solution(mesh):
    plane = P(None, axes, None, None)
    return jax.shard_map(
        per_device,
        mesh=mesh,
        in_specs=(plane,) + (P(),) * 12 + (P(axes, None, None), plane),
        out_specs=(plane, plane, P()),
        check_vma=False,
    )
```

profile of v0, /device:TPU:0, one launch (start us, length us, event | category | flops | bytes accessed | tf_op | source)
XLA Modules:
  0.0 139.6 jit_solution(453844168831693965)
XLA Ops:
  0.6 1.8 %copy.132 = bf16[48,1,128,32]{3,2,0,1:T(8,128)(2,1)S(1)} copy(bf16[48,1,128,32]{2,3,1,0:T(8,128)(2,1)} %param.15) | data formatting | bytes 786432 | tf_op args[0]
  2.5 0.8 reshape.62
  3.5 2.4 %collective-permute-start = (bf16[48,128]{1,0:T(8,128)(2,1)S(1)}, bf16[48,128]{1,0:T(8,128)(2,1)S(1)}, u32[]{:S(2)}, u32[]{:S(2)}) collective-permute-start(bf16[48,128]{1,0:T(8,128)(2,1)S(1)} %slice_bitcast_fusion.1), channel_id=1, source_target_pairs={{0,1},{1,2},{2,3},{3,4},{4,5},{5,6},{6,7},{7,8},{8,9},{9,10},{10,1... | collective-permute-start | bytes 36872 | tf_op jit(solution)/shard_map/ppermute | solution.py:393
  9.9 6.7 %states.2 = (bf16[32,96,128]{2,1,0:T(8,128)(2,1)S(1)}, bf16[32,64,128]{2,1,0:T(8,128)(2,1)S(1)}, f32[32,16,128]{2,1,0:T(8,128)S(1)}, f32[32,72,128]{2,1,0:T(8,128)S(1)}, f32[72,128]{1,0:T(8,128)S(1)}) custom-call(bf16[32,48,128]{2,1,0:T(8,128)(2,1)S(1)} %bitcast.101, bf16[48,128]{1,0:T(8,128)(2,1)S(1)} %collective-permute-done.tail_ref, ...), custom_call_target="tpu_custom_call" | custom-call | tf_op jit(solution)/shard_map/states/pallas_call | solution.py:267
  16.6 2.7 %collective-permute-start.1 = (f32[72,128]{1,0:T(8,128)S(1)}, f32[72,128]{1,0:T(8,128)}, u32[]{:S(2)}, u32[]{:S(2)}) collective-permute-start(f32[72,128]{1,0:T(8,128)S(1)} %get-tuple-element.22), channel_id=1, source_target_pairs={{0,1},{1,0},{2,3},{3,2},{4,5},{5,4},{6,7},{7,6},{8,9},{9,8},{10,11... | collective-permute-start | bytes 110600 | tf_op jit(solution)/shard_map/ppermute | solution.py:251
  19.4 13.2 %local.2 = (f32[32,96,128]{2,1,0:T(8,128)S(1)}, f32[32,96,128]{2,1,0:T(8,128)S(1)}, bf16[32,64,128]{2,1,0:T(8,128)(2,1)S(1)}) custom-call(bf16[32,48,128]{2,1,0:T(8,128)(2,1)S(1)} %bitcast.102, bf16[48,128]{1,0:T(8,128)(2,1)S(1)} %collective-permute-done.tail_ref, bf16[160,48]{1,0:T(8,128)(2,1)S(1)} %pad_maximum_fusion.weight_ref, ...), custom_call_target="tpu_custom_call" | custom-call | tf_op jit(solution)/shard_map/local/pallas_call | solution.py:303
  33.4 1.6 %collective-permute-start.2 = (f32[72,128]{1,0:T(8,128)S(1)}, f32[72,128]{1,0:T(8,128)S(1)}, u32[]{:S(2)}, u32[]{:S(2)}) collective-permute-start(f32[72,128]{1,0:T(8,128)S(1)} %pad_maximum_fusion.2), channel_id=1, source_target_pairs={{0,2},{1,3},{2,0},{3,1},{4,6},{5,7},{6,4},{7,5},{8,10},{9,11},{10,... | collective-permute-start | bytes 110600 | tf_op jit(solution)/shard_map/ppermute | solution.py:251
  34.9 2.5 %collective-permute-done.2 = f32[72,128]{1,0:T(8,128)S(1)} collective-permute-done((f32[72,128]{1,0:T(8,128)S(1)}, f32[72,128]{1,0:T(8,128)S(1)}, u32[]{:S(2)}, u32[]{:S(2)}) %collective-permute-start.2) | collective-permute-done | bytes 36896 | tf_op jit(solution)/shard_map/ppermute | solution.py:251
  37.5 1.6 %collective-permute-start.3 = (f32[72,128]{1,0:T(8,128)S(1)}, f32[72,128]{1,0:T(8,128)S(1)}, u32[]{:S(2)}, u32[]{:S(2)}) collective-permute-start(f32[72,128]{1,0:T(8,128)S(1)} %pad_maximum_fusion.3), channel_id=1, source_target_pairs={{0,4},{1,5},{2,6},{3,7},{4,0},{5,1},{6,2},{7,3},{8,12},{9,13},{10,... | collective-permute-start | bytes 110600 | tf_op jit(solution)/shard_map/ppermute | solution.py:251
  39.1 2.4 %collective-permute-done.3 = f32[72,128]{1,0:T(8,128)S(1)} collective-permute-done((f32[72,128]{1,0:T(8,128)S(1)}, f32[72,128]{1,0:T(8,128)S(1)}, u32[]{:S(2)}, u32[]{:S(2)}) %collective-permute-start.3) | collective-permute-done | bytes 36896 | tf_op jit(solution)/shard_map/ppermute | solution.py:251
  41.6 1.6 %collective-permute-start.4 = (f32[72,128]{1,0:T(8,128)S(1)}, f32[72,128]{1,0:T(8,128)S(1)}, u32[]{:S(2)}, u32[]{:S(2)}) collective-permute-start(f32[72,128]{1,0:T(8,128)S(1)} %pad_maximum_fusion.4), channel_id=1, source_target_pairs={{0,8},{1,9},{2,10},{3,11},{4,12},{5,13},{6,14},{7,15},{8,0},{9,1},... | collective-permute-start | bytes 110600 | tf_op jit(solution)/shard_map/ppermute | solution.py:251
  43.2 2.3 %collective-permute-done.4 = f32[72,128]{1,0:T(8,128)S(1)} collective-permute-done((f32[72,128]{1,0:T(8,128)S(1)}, f32[72,128]{1,0:T(8,128)S(1)}, u32[]{:S(2)}, u32[]{:S(2)}) %collective-permute-start.4) | collective-permute-done | bytes 36896 | tf_op jit(solution)/shard_map/ppermute | solution.py:251
  45.6 2.7 %collective-permute-start.5 = (f32[72,128]{1,0:T(8,128)S(1)}, f32[72,128]{1,0:T(8,128)S(1)}, u32[]{:S(2)}, u32[]{:S(2)}) collective-permute-start(f32[72,128]{1,0:T(8,128)S(1)} %pad_maximum_fusion.5), channel_id=1, source_target_pairs={{0,16},{1,17},{2,18},{3,19},{4,20},{5,21},{6,22},{7,23},{8,24},{9,... | collective-permute-start | bytes 110600 | tf_op jit(solution)/shard_map/ppermute | solution.py:251
  48.3 2.2 %collective-permute-done.5 = f32[72,128]{1,0:T(8,128)S(1)} collective-permute-done((f32[72,128]{1,0:T(8,128)S(1)}, f32[72,128]{1,0:T(8,128)S(1)}, u32[]{:S(2)}, u32[]{:S(2)}) %collective-permute-start.5) | collective-permute-done | bytes 36896 | tf_op jit(solution)/shard_map/ppermute | solution.py:251
  50.6 5.7 %finish.1 = bf16[32,48,128]{2,1,0:T(8,128)(2,1)S(1)} custom-call(f32[72,128]{1,0:T(8,128)S(1)} %maximum_select_fusion.3.enter_ref, bf16[32,48,128]{2,1,0:T(8,128)(2,1)S(1)} %bitcast.103, f32[32,96,128]{2,1,0:T(8,128)S(1)} %get-tuple-element.26.local_ref, f32[32,96,128]{2,1,0:T(8,128)S(1)} %get-tuple-element.27.gate_ref, ...), custom_call_target="tpu_custom_call" | custom-call | tf_op jit(solution)/shard_map/finish/pallas_call | solution.py:396
  57.1 1.4 copy.146
  58.5 5.2 %all-to-all-start = ((bf16[32,48,128]{2,1,0:T(8,128)(2,1)}), bf16[32,48,128]{2,1,0:T(8,128)(2,1)S(1)}, u32[]{:S(2)}, u32[]{:S(2)}) async-start(bf16[32,48,128]{2,1,0:T(8,128)(2,1)} %bitcast.23), calls=%async_computation | async-start | bytes 786432 | tf_op jit(solution)/shard_map/all_to_all | solution.py:407
  64.2 12.7 %all-to-all-done.hid_ref = bf16[32,48,128]{2,1,0:T(8,128)(2,1)S(1)} async-done(((bf16[32,48,128]{2,1,0:T(8,128)(2,1)}), bf16[32,48,128]{2,1,0:T(8,128)(2,1)S(1)}, u32[]{:S(2)}, u32[]{:S(2)}) %all-to-all-start) | async-done | bytes 393248 | tf_op jit(solution)/shard_map/all_to_all | solution.py:407
  76.9 1.6 %collective-permute-start.6 = (bf16[48,128]{1,0:T(8,128)(2,1)S(1)}, bf16[48,128]{1,0:T(8,128)(2,1)S(1)}, u32[]{:S(2)}, u32[]{:S(2)}) collective-permute-start(bf16[48,128]{1,0:T(8,128)(2,1)S(1)} %slice_bitcast_fusion), channel_id=1, source_target_pairs={{0,1},{1,2},{2,3},{3,4},{4,5},{5,6},{6,7},{7,8},{8,9},{9,10},{10,1... | collective-permute-start | bytes 36872 | tf_op jit(solution)/shard_map/ppermute | solution.py:410
  79.1 6.6 %states.3 = (bf16[32,96,128]{2,1,0:T(8,128)(2,1)S(1)}, bf16[32,64,128]{2,1,0:T(8,128)(2,1)S(1)}, f32[32,16,128]{2,1,0:T(8,128)S(1)}, f32[32,72,128]{2,1,0:T(8,128)S(1)}, f32[72,128]{1,0:T(8,128)S(1)}) custom-call(bf16[32,48,128]{2,1,0:T(8,128)(2,1)S(1)} %all-to-all-done.hid_ref, bf16[48,128]{1,0:T(8,128)(2,1)S(1)} %collective-permute-done.6.tail_ref, ...), custom_call_target="tpu_custom_call" | custom-call | tf_op jit(solution)/shard_map/states/pallas_call | solution.py:267
  85.7 1.2 collective-permute-start.7
  87.1 13.2 %local.3 = (f32[32,96,128]{2,1,0:T(8,128)S(1)}, f32[32,96,128]{2,1,0:T(8,128)S(1)}, bf16[32,64,128]{2,1,0:T(8,128)(2,1)S(1)}) custom-call(bf16[32,48,128]{2,1,0:T(8,128)(2,1)S(1)} %all-to-all-done.hid_ref, bf16[48,128]{1,0:T(8,128)(2,1)S(1)} %collective-permute-done.6.tail_ref, bf16[160,48]{1,0:T(8,128)(2,1)S(1)} %pad_maximum_fusion.1.weight_ref, ...), custom_call_target="tpu_custom_call" | custom-call | tf_op jit(solution)/shard_map/local/pallas_call | solution.py:303
  100.5 2.3 %collective-permute-start.8 = (f32[72,128]{1,0:T(8,128)S(1)}, f32[72,128]{1,0:T(8,128)S(1)}, u32[]{:S(2)}, u32[]{:S(2)}) collective-permute-start(f32[72,128]{1,0:T(8,128)S(1)} %pad_maximum_fusion.6), channel_id=1, source_target_pairs={{0,2},{1,3},{2,0},{3,1},{4,6},{5,7},{6,4},{7,5},{8,10},{9,11},{10,... | collective-permute-start | bytes 110600 | tf_op jit(solution)/shard_map/ppermute | solution.py:251
  102.7 2.1 %collective-permute-done.8 = f32[72,128]{1,0:T(8,128)S(1)} collective-permute-done((f32[72,128]{1,0:T(8,128)S(1)}, f32[72,128]{1,0:T(8,128)S(1)}, u32[]{:S(2)}, u32[]{:S(2)}) %collective-permute-start.8) | collective-permute-done | bytes 36896 | tf_op jit(solution)/shard_map/ppermute | solution.py:251
  104.9 3.3 %collective-permute-start.9 = (f32[72,128]{1,0:T(8,128)S(1)}, f32[72,128]{1,0:T(8,128)S(1)}, u32[]{:S(2)}, u32[]{:S(2)}) collective-permute-start(f32[72,128]{1,0:T(8,128)S(1)} %pad_maximum_fusion.7), channel_id=1, source_target_pairs={{0,4},{1,5},{2,6},{3,7},{4,0},{5,1},{6,2},{7,3},{8,12},{9,13},{10,... | collective-permute-start | bytes 110600 | tf_op jit(solution)/shard_map/ppermute | solution.py:251
  108.3 1.9 %collective-permute-done.9 = f32[72,128]{1,0:T(8,128)S(1)} collective-permute-done((f32[72,128]{1,0:T(8,128)S(1)}, f32[72,128]{1,0:T(8,128)S(1)}, u32[]{:S(2)}, u32[]{:S(2)}) %collective-permute-start.9) | collective-permute-done | bytes 36896 | tf_op jit(solution)/shard_map/ppermute | solution.py:251
  110.2 3.0 %collective-permute-start.10 = (f32[72,128]{1,0:T(8,128)S(1)}, f32[72,128]{1,0:T(8,128)S(1)}, u32[]{:S(2)}, u32[]{:S(2)}) collective-permute-start(f32[72,128]{1,0:T(8,128)S(1)} %pad_maximum_fusion.8), channel_id=1, source_target_pairs={{0,8},{1,9},{2,10},{3,11},{4,12},{5,13},{6,14},{7,15},{8,0},{9,1},... | collective-permute-start | bytes 110600 | tf_op jit(solution)/shard_map/ppermute | solution.py:251
  113.3 1.9 %collective-permute-done.10 = f32[72,128]{1,0:T(8,128)S(1)} collective-permute-done((f32[72,128]{1,0:T(8,128)S(1)}, f32[72,128]{1,0:T(8,128)S(1)}, u32[]{:S(2)}, u32[]{:S(2)}) %collective-permute-start.10) | collective-permute-done | bytes 36896 | tf_op jit(solution)/shard_map/ppermute | solution.py:251
  115.2 1.1 collective-permute-start.11
  116.4 3.7 %collective-permute-done.11 = f32[72,128]{1,0:T(8,128)S(1)} collective-permute-done((f32[72,128]{1,0:T(8,128)S(1)}, f32[72,128]{1,0:T(8,128)S(1)}, u32[]{:S(2)}, u32[]{:S(2)}) %collective-permute-start.11) | collective-permute-done | bytes 36896 | tf_op jit(solution)/shard_map/ppermute | solution.py:251
  120.2 7.3 %heads.1 = (bf16[48,32,128]{2,1,0:T(8,128)(2,1)}, f32[14,32,128]{2,1,0:T(8,128)}, f32[8,128]{1,0:T(8,128)S(1)}) custom-call(f32[72,128]{1,0:T(8,128)S(1)} %maximum_select_fusion.7.enter_ref, bf16[32,48,128]{2,1,0:T(8,128)(2,1)S(1)} %all-to-all-done.hid_ref, f32[32,96,128]{2,1,0:T(8,128)S(1)} %get-tuple-element.34.local_ref, ...), custom_call_target="tpu_custom_call" | custom-call | tf_op jit(solution)/shard_map/heads/pallas_call | solution.py:417
  127.5 9.7 %all_to_all.11 = f32[32,1,128]{2,1,0:T(1,128)S(1)} all-to-all(f32[32,1,128]{2,1,0:T(1,128)S(1)} %broadcast_in_dim.10), channel_id=1, replica_groups=mesh['row'=8,'col'=4] {'row','col'}, dimensions={0} | all-to-all | bytes 32768 | tf_op jit(solution)/shard_map/all_to_all | solution.py:446
  (168 shorter events, 8.2 us)
Async XLA Ops:
  2.4 3.5 %copy-start.2 = (bf16[2,320,48]{1,2,0:T(8,128)(2,1)S(1)}, bf16[2,320,48]{1,2,0:T(8,128)(2,1)}, u32[]{:S(2)}) copy-start(bf16[2,320,48]{1,2,0:T(8,128)(2,1)} %param.17) | copy-start | bytes 184324
  2.4 4.8 %copy-start.7 = (f32[2,224,4]{1,2,0:T(4,128)S(1)}, f32[2,224,4]{1,2,0:T(4,128)}, u32[]{:S(2)}) copy-start(f32[2,224,4]{1,2,0:T(4,128)} %param.21) | copy-start | bytes 21508
  2.4 4.8 %copy-start.11 = (f32[2,224]{1,0:T(2,128)S(1)}, f32[2,224]{1,0:T(2,128)}, u32[]{:S(2)}) copy-start(f32[2,224]{1,0:T(2,128)} %param.22) | copy-start | bytes 5380
  2.4 4.8 %copy-start.13 = (f32[2,3]{1,0:T(2,128)S(1)}, f32[2,3]{1,0:T(2,128)}, u32[]{:S(2)}) copy-start(f32[2,3]{1,0:T(2,128)} %param.19) | copy-start | bytes 76
  2.4 4.9 %copy-start.14 = (f32[2,3]{1,0:T(2,128)S(1)}, f32[2,3]{1,0:T(2,128)}, u32[]{:S(2)}) copy-start(f32[2,3]{1,0:T(2,128)} %param.20) | copy-start | bytes 76
  2.5 5.0 %copy-start.15 = (f32[2,3]{1,0:T(2,128)S(1)}, f32[2,3]{1,0:T(2,128)}, u32[]{:S(2)}) copy-start(f32[2,3]{1,0:T(2,128)} %param.23) | copy-start | bytes 76
  2.5 5.6 %copy-start.16 = (f32[2,48]{1,0:T(2,128)S(1)}, f32[2,48]{1,0:T(2,128)}, u32[]{:S(2)}) copy-start(f32[2,48]{1,0:T(2,128)} %param.16) | copy-start | bytes 1156
  2.5 5.6 %copy-start.8 = (bf16[2,3,48]{2,0,1:T(2,128)(2,1)S(1)}, bf16[2,3,48]{2,0,1:T(2,128)(2,1)}, u32[]{:S(2)}) copy-start(bf16[2,3,48]{2,0,1:T(2,128)(2,1)} %param.18) | copy-start | bytes 1732
  2.5 5.6 %copy-start.17 = (f32[2,96]{1,0:T(2,128)S(1)}, f32[2,96]{1,0:T(2,128)}, u32[]{:S(2)}) copy-start(f32[2,96]{1,0:T(2,128)} %param.24) | copy-start | bytes 2308
  2.5 6.1 %copy-start.6 = (bf16[2,48,96]{2,1,0:T(8,128)(2,1)S(1)}, bf16[2,48,96]{2,1,0:T(8,128)(2,1)}, u32[]{:S(2)}) copy-start(bf16[2,48,96]{2,1,0:T(8,128)(2,1)} %param.25) | copy-start | bytes 55300
  3.5 6.4 %collective-permute-start = (bf16[48,128]{1,0:T(8,128)(2,1)S(1)}, bf16[48,128]{1,0:T(8,128)(2,1)S(1)}, u32[]{:S(2)}, u32[]{:S(2)}) collective-permute-start(bf16[48,128]{1,0:T(8,128)(2,1)S(1)} %slice_bitcast_fusion.1), channel_id=1, source_target_pairs={{0,1},{1,2},{2,3},{3,4},{4,5},{5,6},{6,7},{7,8},{8,9},{9,10},{10,1... | collective-permute-start | bytes 36872 | tf_op jit(solution)/shard_map/ppermute | solution.py:393
  16.6 16.0 %collective-permute-start.1 = (f32[72,128]{1,0:T(8,128)S(1)}, f32[72,128]{1,0:T(8,128)}, u32[]{:S(2)}, u32[]{:S(2)}) collective-permute-start(f32[72,128]{1,0:T(8,128)S(1)} %get-tuple-element.22), channel_id=1, source_target_pairs={{0,1},{1,0},{2,3},{3,2},{4,5},{5,4},{6,7},{7,6},{8,9},{9,8},{10,11... | collective-permute-start | bytes 110600 | tf_op jit(solution)/shard_map/ppermute | solution.py:251
  33.4 4.0 %collective-permute-start.2 = (f32[72,128]{1,0:T(8,128)S(1)}, f32[72,128]{1,0:T(8,128)S(1)}, u32[]{:S(2)}, u32[]{:S(2)}) collective-permute-start(f32[72,128]{1,0:T(8,128)S(1)} %pad_maximum_fusion.2), channel_id=1, source_target_pairs={{0,2},{1,3},{2,0},{3,1},{4,6},{5,7},{6,4},{7,5},{8,10},{9,11},{10,... | collective-permute-start | bytes 110600 | tf_op jit(solution)/shard_map/ppermute | solution.py:251
  37.5 4.0 %collective-permute-start.3 = (f32[72,128]{1,0:T(8,128)S(1)}, f32[72,128]{1,0:T(8,128)S(1)}, u32[]{:S(2)}, u32[]{:S(2)}) collective-permute-start(f32[72,128]{1,0:T(8,128)S(1)} %pad_maximum_fusion.3), channel_id=1, source_target_pairs={{0,4},{1,5},{2,6},{3,7},{4,0},{5,1},{6,2},{7,3},{8,12},{9,13},{10,... | collective-permute-start | bytes 110600 | tf_op jit(solution)/shard_map/ppermute | solution.py:251
  41.6 4.0 %collective-permute-start.4 = (f32[72,128]{1,0:T(8,128)S(1)}, f32[72,128]{1,0:T(8,128)S(1)}, u32[]{:S(2)}, u32[]{:S(2)}) collective-permute-start(f32[72,128]{1,0:T(8,128)S(1)} %pad_maximum_fusion.4), channel_id=1, source_target_pairs={{0,8},{1,9},{2,10},{3,11},{4,12},{5,13},{6,14},{7,15},{8,0},{9,1},... | collective-permute-start | bytes 110600 | tf_op jit(solution)/shard_map/ppermute | solution.py:251
  45.6 4.9 %collective-permute-start.5 = (f32[72,128]{1,0:T(8,128)S(1)}, f32[72,128]{1,0:T(8,128)S(1)}, u32[]{:S(2)}, u32[]{:S(2)}) collective-permute-start(f32[72,128]{1,0:T(8,128)S(1)} %pad_maximum_fusion.5), channel_id=1, source_target_pairs={{0,16},{1,17},{2,18},{3,19},{4,20},{5,21},{6,22},{7,23},{8,24},{9,... | collective-permute-start | bytes 110600 | tf_op jit(solution)/shard_map/ppermute | solution.py:251
  57.1 6.8 %copy-start.12 = (f32[3,1]{0,1:T(1,128)S(1)}, f32[3,1]{0,1:T(1,128)}, u32[]{:S(2)}) copy-start(f32[3,1]{0,1:T(1,128)} %get-tuple-element.94) | copy-start | bytes 40
  57.1 6.9 %copy-start.4 = (bf16[1,96,48]{1,2,0:T(8,128)(2,1)S(1)}, bf16[1,96,48]{1,2,0:T(8,128)(2,1)}, u32[]{:S(2)}) copy-start(bf16[1,96,48]{1,2,0:T(8,128)(2,1)} %get-tuple-element.56) | copy-start | bytes 27652
  57.1 7.0 %copy-start.3 = (bf16[1,64,48]{1,2,0:T(8,128)(2,1)S(1)}, bf16[1,64,48]{1,2,0:T(8,128)(2,1)}, u32[]{:S(2)}) copy-start(bf16[1,64,48]{1,2,0:T(8,128)(2,1)} %get-tuple-element.58) | copy-start | bytes 18436
  57.1 21.4 %copy-start.5 = (f32[224,5]{0,1:T(8,128)S(1)}, f32[224,5]{0,1:T(8,128)}, u32[]{:S(2)}) copy-start(f32[224,5]{0,1:T(8,128)} %get-tuple-element.99) | copy-start | bytes 13444
  57.1 29.8 %copy-start.18 = (f32[14]{0:T(128)S(1)}, f32[14]{0:T(128)}, u32[]{:S(2)}) copy-start(f32[14]{0:T(128)} %param.27) | copy-start | bytes 172
  57.1 29.8 %copy-start.10 = (f32[96,1]{0,1:T(1,128)S(1)}, f32[96,1]{0,1:T(1,128)}, u32[]{:S(2)}) copy-start(f32[96,1]{0,1:T(1,128)} %get-tuple-element.88) | copy-start | bytes 1156
  57.1 30.0 %copy-start.9 = (bf16[14,48]{1,0:T(8,128)(2,1)S(1)}, bf16[14,48]{1,0:T(8,128)(2,1)}, u32[]{:S(2)}) copy-start(bf16[14,48]{1,0:T(8,128)(2,1)} %param.26) | copy-start | bytes 4036
  58.5 18.4 %all-to-all-start = ((bf16[32,48,128]{2,1,0:T(8,128)(2,1)}), bf16[32,48,128]{2,1,0:T(8,128)(2,1)S(1)}, u32[]{:S(2)}, u32[]{:S(2)}) async-start(bf16[32,48,128]{2,1,0:T(8,128)(2,1)} %bitcast.23), calls=%async_computation | async-start | bytes 786432 | tf_op jit(solution)/shard_map/all_to_all | solution.py:407
  76.9 2.2 %collective-permute-start.6 = (bf16[48,128]{1,0:T(8,128)(2,1)S(1)}, bf16[48,128]{1,0:T(8,128)(2,1)S(1)}, u32[]{:S(2)}, u32[]{:S(2)}) collective-permute-start(bf16[48,128]{1,0:T(8,128)(2,1)S(1)} %slice_bitcast_fusion), channel_id=1, source_target_pairs={{0,1},{1,2},{2,3},{3,4},{4,5},{5,6},{6,7},{7,8},{8,9},{9,10},{10,1... | collective-permute-start | bytes 36872 | tf_op jit(solution)/shard_map/ppermute | solution.py:410
  85.7 14.7 %collective-permute-start.7 = (f32[72,128]{1,0:T(8,128)S(1)}, f32[72,128]{1,0:T(8,128)S(1)}, u32[]{:S(2)}, u32[]{:S(2)}) collective-permute-start(f32[72,128]{1,0:T(8,128)S(1)} %get-tuple-element.30), channel_id=1, source_target_pairs={{0,1},{1,0},{2,3},{3,2},{4,5},{5,4},{6,7},{7,6},{8,9},{9,8},{10,11... | collective-permute-start | bytes 110600 | tf_op jit(solution)/shard_map/ppermute | solution.py:251
  100.3 19.8 %copy-start = (s32[14,1,32,128]{3,2,1,0:T(8,128)S(1)}, s32[14,1,32,128]{3,2,1,0:T(8,128)}, u32[]{:S(2)}) copy-start(s32[14,1,32,128]{3,2,1,0:T(8,128)} %param.29) | copy-start | bytes 688132
  100.4 19.8 %copy-start.1 = (s32[1,32,128]{2,1,0:T(8,128)S(1)}, s32[1,32,128]{2,1,0:T(8,128)}, u32[]{:S(2)}) copy-start(s32[1,32,128]{2,1,0:T(8,128)} %param.28) | copy-start | bytes 49156
  100.5 4.4 %collective-permute-start.8 = (f32[72,128]{1,0:T(8,128)S(1)}, f32[72,128]{1,0:T(8,128)S(1)}, u32[]{:S(2)}, u32[]{:S(2)}) collective-permute-start(f32[72,128]{1,0:T(8,128)S(1)} %pad_maximum_fusion.6), channel_id=1, source_target_pairs={{0,2},{1,3},{2,0},{3,1},{4,6},{5,7},{6,4},{7,5},{8,10},{9,11},{10,... | collective-permute-start | bytes 110600 | tf_op jit(solution)/shard_map/ppermute | solution.py:251
  104.9 5.2 %collective-permute-start.9 = (f32[72,128]{1,0:T(8,128)S(1)}, f32[72,128]{1,0:T(8,128)S(1)}, u32[]{:S(2)}, u32[]{:S(2)}) collective-permute-start(f32[72,128]{1,0:T(8,128)S(1)} %pad_maximum_fusion.7), channel_id=1, source_target_pairs={{0,4},{1,5},{2,6},{3,7},{4,0},{5,1},{6,2},{7,3},{8,12},{9,13},{10,... | collective-permute-start | bytes 110600 | tf_op jit(solution)/shard_map/ppermute | solution.py:251
  110.2 5.0 %collective-permute-start.10 = (f32[72,128]{1,0:T(8,128)S(1)}, f32[72,128]{1,0:T(8,128)S(1)}, u32[]{:S(2)}, u32[]{:S(2)}) collective-permute-start(f32[72,128]{1,0:T(8,128)S(1)} %pad_maximum_fusion.8), channel_id=1, source_target_pairs={{0,8},{1,9},{2,10},{3,11},{4,12},{5,13},{6,14},{7,15},{8,0},{9,1},... | collective-permute-start | bytes 110600 | tf_op jit(solution)/shard_map/ppermute | solution.py:251
  115.2 4.9 %collective-permute-start.11 = (f32[72,128]{1,0:T(8,128)S(1)}, f32[72,128]{1,0:T(8,128)S(1)}, u32[]{:S(2)}, u32[]{:S(2)}) collective-permute-start(f32[72,128]{1,0:T(8,128)S(1)} %pad_maximum_fusion.9), channel_id=1, source_target_pairs={{0,16},{1,17},{2,18},{3,19},{4,20},{5,21},{6,22},{7,23},{8,24},{9,... | collective-permute-start | bytes 110600 | tf_op jit(solution)/shard_map/ppermute | solution.py:251
where the time goes:
time: 140 us
  Pallas kernels  52.6 us (38%)
  waiting for transfers between devices  31.9 us (23%)
  starting transfers between devices  30.1 us (22%)
  blocking collectives  9.69 us (7%)
  local copies, waits for them, and re-layouts  9.36 us (7%)
  between operations  3.28 us (2%)
  other arithmetic  2.59 us (2%)
    pallas_call x2, Pallas kernels, layer_start(): pl.pallas_call(functools.partial(local_kernel, heads), grid=(steps,), in_...  26.4 us
    ppermute x10, starting transfers between devices, prefix_state(): other = lax.ppermute(total, axes, [(i, i ^ reach) for i in range(size)])  21 us
    ppermute x10, waiting for transfers between devices, prefix_state(): other = lax.ppermute(total, axes, [(i, i ^ reach) for i in range(size)])  19.1 us
    pallas_call x2, Pallas kernels, layer_start(): pl.pallas_call(functools.partial(state_kernel, heads), grid=(steps,), in_...  13.3 us
    all_to_all x1, waiting for transfers between devices, per_device(): lax.all_to_all(planes, axes, split_axis=0, concat_axis=0, tiled=True)  12.7 us
    all_to_all x1, blocking collectives, per_device(): lax.all_to_all(jnp.broadcast_to(own, (size, SCAN_BLOCK)), axes, 0, 0, til...  9.69 us
    pallas_call x1, Pallas kernels, per_device(): pl.pallas_call(functools.partial(head_kernel, heads), grid=(count // grou...  7.29 us
    pallas_call x1, Pallas kernels, per_device(): pl.pallas_call(functools.partial(finish_kernel, heads), grid=(count // gr...  5.7 us
  transfers between devices with their start and end apart: 13, of which 10 were waited for; matrix products, arithmetic and copies ran while one was open for 4% of the time, Pallas kernels for 19%

commit v1 on v0

v1 whole, which is shorter than its diff:
```python
import functools

import jax
import jax.numpy as jnp
from jax import lax
from jax.experimental import pallas as pl
from jax.experimental.pallas import tpu as pltpu
from jax.sharding import PartitionSpec as P

SCAN_BLOCK = 128
LANES = 128

eps = 1e-05
dist_unit = 4096.0
axes = ("row", "col")
f32, bf16 = jnp.float32, jnp.bfloat16
vmem_bytes = 24 * 1024 * 1024
wide = 4


def half_silu(v):
    return v + v * jnp.tanh(v)


def rounded(v):
    return v.astype(bf16).astype(f32)


def normalise(hidden, gain_col):
    values = hidden.astype(f32)
    mean_sq = jnp.mean(values * values, axis=0, keepdims=True)
    return (values * lax.rsqrt(mean_sq + eps) * gain_col).astype(bf16)


def project(weight, normed):
    return jnp.dot(weight, normed, preferred_element_type=f32)


def contract(a, b, dim):
    return lax.dot_general(a, b, (((dim,), (dim,)), ((), ())), preferred_element_type=f32)


def spread(rows, first, count, height):
    return jnp.concatenate(
        [jnp.broadcast_to(rows[first + h : first + h + 1], (height, rows.shape[1])) for h in range(count)], axis=0
    )


def side_by_side(ref, first, count, rows=None):
    rows = ref.shape[1] if rows is None else rows
    return jnp.concatenate([ref[u][:rows] for u in range(first, first + count)], axis=1)


def span(u, count=1):
    return slice(u * SCAN_BLOCK, (u + count) * SCAN_BLOCK)


def padded(values, rows, lanes):
    if values.shape[1] < lanes:
        values = jnp.concatenate([values, jnp.zeros((values.shape[0], lanes - values.shape[1]), f32)], axis=1)
    if values.shape[0] < rows:
        values = jnp.concatenate([values, jnp.zeros((rows - values.shape[0], lanes), f32)], axis=0)
    return values


def turned(values):
    lanes = -(-values.shape[1] // LANES) * LANES
    return jnp.transpose(padded(values, -(-values.shape[0] // 8) * 8, lanes), (1, 0))


def columns(*rows):
    return turned(jnp.concatenate(rows, axis=0))


def columns_of(layer, rows_ref):
    return jnp.transpose(rows_ref[layer], (1, 0))


def tail_tile(tail_ref, model):
    if tail_ref.ndim == 2:
        return tail_ref[...]
    block = tail_ref[0].astype(f32)
    rows = block[model:]
    kept = lax.broadcasted_iota(jnp.int32, rows.shape, 0) >= rows.shape[0] - 3
    rows = jnp.where(kept, rows, 0.0)
    tile = jnp.concatenate([jnp.zeros((SCAN_BLOCK - rows.shape[0], LANES), f32), rows], axis=0)
    return jnp.transpose(tile, (1, 0))[:model].astype(bf16)


def swap_lanes(parts):
    count = len(parts)
    if count == 1:
        return parts
    width = LANES // count
    place = lax.broadcasted_iota(jnp.int32, parts[0].shape, 1) // width
    result = []
    for b in range(count):
        total = None
        for a, part in enumerate(parts):
            shift = (a - b) * width % LANES
            moved = pltpu.roll(part, shift, 1) if shift else part
            total = moved if total is None else jnp.where(place == a, moved, total)
        result.append(total)
    return result


def to_sequence(volume_ref, hid_ref, turn_ref, tile_ref):
    model, cells_x, cells_y = volume_ref.shape
    count = hid_ref.shape[0]
    per = LANES // cells_x
    for c in range(0, model, per):
        turn_ref[c // per] = jnp.transpose(volume_ref[c : c + per].astype(f32).reshape(LANES, cells_y), (1, 0))
    for c in range(0, model, per):
        parts = [turn_ref[c // per, pl.ds(a, count, stride=per), :] for a in range(per)]
        for j, part in enumerate(swap_lanes(parts)):
            tile_ref[pl.ds(c + j, count, stride=model), :] = part
    for u in range(count):
        hid_ref[u] = tile_ref[u * model : (u + 1) * model, :].astype(bf16)


def to_planes(tile_ref, out_ref, turn_ref, plane_ref, model, cells_x):
    rows = out_ref.shape[1]
    cells_y = out_ref.shape[2]
    per = LANES // cells_x
    count = cells_y // per
    for c in range(0, model, per):
        parts = [tile_ref[pl.ds(c + j, count, stride=model), :] for j in range(per)]
        for a, part in enumerate(swap_lanes(parts)):
            turn_ref[c // per, pl.ds(a, count, stride=per), :] = part
    for c in range(0, model, per):
        turn = jnp.transpose(turn_ref[c // per], (1, 0))
        for j in range(per):
            plane_ref[pl.ds(c + j, cells_x, stride=rows), :] = turn[j * cells_x : (j + 1) * cells_x]
    for x in range(cells_x + 1):
        plane_ref[x * rows + model : (x + 1) * rows, :] = jnp.zeros((rows - model, LANES), f32)
    for y in range(cells_y - 3, cells_y):
        block, a = divmod(y, per)
        turn = jnp.transpose(padded(tile_ref[block * model : (block + 1) * model, :], LANES, LANES), (1, 0))
        at = 2 * rows - cells_y + y
        plane_ref[pl.ds(at, cells_x, stride=rows), :] = turn[a * cells_x : (a + 1) * cells_x]
    for x in range(cells_x):
        out_ref[x] = plane_ref[x * rows : (x + 1) * rows, :].astype(bf16)


def convolve(proj_ref, rows, cols, first, outs):
    group = proj_ref.shape[1] // SCAN_BLOCK - 1
    tap_count = 4
    for r in range(0, rows, 16):
        conv_in = proj_ref[r : r + 16, :]
        half = 0.5 * cols[first + r : first + r + 16, :]
        total = None
        for offset in range(tap_count):
            lag = tap_count - 1 - offset
            shifted = pltpu.roll(conv_in, lag, 1) if lag else conv_in
            term = half[:, offset : offset + 1] * shifted[:, SCAN_BLOCK:]
            total = half[:, tap_count : tap_count + 1] + term if total is None else total + term
        conv_out = half_silu(total).astype(bf16)
        ref, at = next((ref, r - low) for ref, low, high in outs if low <= r < high)
        for u in range(group):
            ref[u, at : at + 16, :] = conv_out[:, span(u)]
    proj_ref[:, span(0)] = proj_ref[:, span(group)]


def state_kernel(
    layer, heads, from_volume, hid_ref, tail_ref, matrix_ref, rows_ref, inner_ref, write_ref, dec_ref, state_ref, total_ref, *rest
):
    if from_volume:
        volume_ref, hid_ref, proj_ref, carry_ref, turn_ref, tile_ref = (hid_ref,) + rest

        @pl.when(pl.program_id(0) == 0)
        def _():
            to_sequence(volume_ref, hid_ref, turn_ref, tile_ref)

        hid_ref = hid_ref.at[pl.ds(pl.program_id(0) * inner_ref.shape[0], inner_ref.shape[0])]
    else:
        proj_ref, carry_ref = rest
    model = matrix_ref.shape[1]
    group = inner_ref.shape[0]
    inner = inner_ref.shape[1]
    width = inner // heads
    state = write_ref.shape[1]
    rows = inner + state
    weight = jnp.transpose(matrix_ref[layer].astype(f32), (1, 0))
    dt_first = 2 * (inner + state)
    weight = jnp.concatenate([weight[inner : inner + rows], weight[dt_first : dt_first + 8]], axis=0).astype(bf16)
    cols = columns_of(layer, rows_ref)
    gain_col = cols[:model, 5:6]
    head_cols = cols[:8, 6:8]

    @pl.when(pl.program_id(0) == 0)
    def _():
        carry_ref[...] = jnp.zeros_like(carry_ref)
        proj_ref[:, span(0)] = rounded(project(weight, normalise(tail_tile(tail_ref, model), gain_col))[:rows])

    lane = lax.broadcasted_iota(jnp.int32, (1, LANES), 1)
    dt_raw = []
    for q in range(0, group, wide):
        projected = project(weight, normalise(side_by_side(hid_ref, q, wide, model), gain_col))
        proj_ref[:, span(q + 1, wide)] = rounded(projected[:rows])
        dt_raw.append(projected[rows:])
    step = jnp.concatenate(dt_raw, axis=1) + head_cols[:, 0:1]
    step = jnp.maximum(step, 0.0) + jnp.log1p(jnp.exp(-jnp.abs(step)))
    log_decay = head_cols[:, 1:2] * step
    step = jnp.concatenate([step[:, span(u)] for u in range(group)], axis=0)
    log_decay = jnp.concatenate([log_decay[:, span(u)] for u in range(group)], axis=0)
    high = log_decay.astype(bf16)
    rest = log_decay - high.astype(f32)
    middle = rest.astype(bf16)
    low = (rest - middle.astype(f32)).astype(bf16)
    square = (SCAN_BLOCK, SCAN_BLOCK)
    earlier = lax.broadcasted_iota(jnp.int32, square, 0) <= lax.broadcasted_iota(jnp.int32, square, 1)
    tri = jnp.where(earlier, 1.0, 0.0).astype(bf16)
    cum = project(low, tri) + project(middle, tri) + project(high, tri)
    last = jnp.broadcast_to(cum[:, SCAN_BLOCK - 1 :], cum.shape)
    carry_weight = jnp.exp(last - cum) * step
    for u in range(group):
        dec_ref[u, 0:8, :] = cum[8 * u : 8 * u + 8]
        dec_ref[u, 8:16, :] = step[8 * u : 8 * u + 8]
    convolve(proj_ref, rows, cols, 0, [(inner_ref, 0, inner), (write_ref, inner, rows)])
    decay_rows, block_states = [], []
    for u in range(group):
        row = last[8 * u + heads - 1 : 8 * u + heads]
        for h in range(heads - 2, -1, -1):
            row = jnp.where(lane < (h + 1) * width, last[8 * u + h : 8 * u + h + 1], row)
        decay_rows.append(row)
        scaled = inner_ref[u].astype(f32) * spread(carry_weight, 8 * u, heads, width)
        scaled = jnp.concatenate([scaled.astype(bf16), jnp.zeros((LANES - inner, SCAN_BLOCK), bf16)], axis=0)
        block_states.append(contract(write_ref[u], scaled, 1))
    running = carry_ref[0:state, :]
    running_log = carry_ref[state:, :]
    for u in range(group):
        state_ref[u, 0:state, :] = running
        state_ref[u, state:, :] = running_log
        running = jnp.exp(decay_rows[u]) * running + block_states[u]
        running_log = running_log + decay_rows[u]
    carry_ref[0:state, :] = running
    carry_ref[state:, :] = running_log
    total_ref[0:state, :] = running
    total_ref[state:, :] = running_log


def local_kernel(
    layer, heads, hid_ref, tail_ref, matrix_ref, rows_ref, inner_ref, write_ref, dec_ref,
    local_ref, gate_ref, read_ref, proj_ref, score_ref, weights_ref,
):
    group = hid_ref.shape[0]
    model = matrix_ref.shape[1]
    inner = inner_ref.shape[1]
    width = inner // heads
    state = read_ref.shape[1]
    weight = jnp.transpose(matrix_ref[layer].astype(f32), (1, 0))
    weight = jnp.concatenate([weight[:inner], weight[2 * inner + state : 2 * (inner + state)]], axis=0).astype(bf16)
    cols = columns_of(layer, rows_ref)
    gain_col = cols[:model, 5:6]
    skip_cols = cols[:8, 8:9]

    @pl.when(pl.program_id(0) == 0)
    def _():
        proj_ref[:, span(0)] = rounded(project(weight[inner:], normalise(tail_tile(tail_ref, model), gain_col)))

    for q in range(0, group, wide):
        projected = rounded(project(weight, normalise(side_by_side(hid_ref, q, wide, model), gain_col)))
        proj_ref[:, span(q + 1, wide)] = projected[inner:]
        gate = half_silu(0.5 * projected[:inner])
        for u in range(wide):
            gate_ref[q + u] = gate[:, span(u)]
    convolve(proj_ref, state, cols, inner + state, [(read_ref, 0, state)])
    source = lax.broadcasted_iota(jnp.int32, (SCAN_BLOCK, SCAN_BLOCK), 0)
    target = lax.broadcasted_iota(jnp.int32, (SCAN_BLOCK, SCAN_BLOCK), 1)
    causal = source <= target
    log2e = 1.4426950408889634
    cum = jnp.concatenate([dec_ref[u, 0:8, :] for u in range(group)], axis=0)
    step = jnp.concatenate([dec_ref[u, 8:16, :] for u in range(group)], axis=0)
    source_cols = (cum - jnp.log(step)) * log2e
    if 8 * group < SCAN_BLOCK:
        unused = jnp.zeros((SCAN_BLOCK - 8 * group, SCAN_BLOCK), f32)
        source_cols = jnp.concatenate([source_cols, unused], axis=0)
    source_cols = jnp.transpose(source_cols, (1, 0))
    cum = cum * log2e
    for u in range(group):
        score_ref[u] = contract(write_ref[u], read_ref[u], 0)
    for u in range(group):
        scores = score_ref[u]
        for h in range(heads):
            at = 8 * u + h
            gap = jnp.where(causal, cum[at : at + 1] - source_cols[:, at : at + 1], -jnp.inf)
            weights_ref[u, h] = (scores * jnp.exp2(gap)).astype(bf16)
    for u in range(group):
        for h in range(heads):
            values = inner_ref[u, h * width : (h + 1) * width, :]
            local_ref[u, h * width : (h + 1) * width, :] = (
                project(values, weights_ref[u, h]) + skip_cols[h : h + 1, 0:1] * values.astype(f32)
            )


def finished(q, layer, heads, enter, refs, out_gain, out_proj):
    hid_ref, local_ref, gate_ref, read_ref, dec_ref, state_ref = refs
    inner = local_ref.shape[1]
    width = inner // heads
    state = read_ref.shape[1]
    inter = []
    for u in range(q, q + wide):
        entering = jnp.exp(state_ref[u, state : state + 1, :]) * enter + state_ref[u, 0:state, :]
        inter.append(contract(entering.astype(bf16), read_ref[u], 0)[:inner])
    decay = jnp.exp(jnp.concatenate([dec_ref[u, 0:8, :] for u in range(q, q + wide)], axis=1))
    scan_out = side_by_side(local_ref, q, wide) + spread(decay, 0, heads, width) * jnp.concatenate(inter, axis=1)
    gated = scan_out * side_by_side(gate_ref, q, wide)
    mean_sq = jnp.mean(gated * gated, axis=0, keepdims=True)
    gated = (gated * lax.rsqrt(mean_sq + eps) * out_gain).astype(bf16)
    hidden = side_by_side(hid_ref, q, wide, out_proj.shape[0]).astype(f32)
    return (hidden + project(out_proj, gated)).astype(bf16)


def entered(odd_ref, half_ref, other_half_ref, other_ref, state):
    odd = odd_ref[0] != 0
    mine, other = half_ref[...], other_half_ref[...]
    chip = jnp.concatenate([jnp.where(odd, other, mine), jnp.where(odd, mine, other)], axis=0)
    joined = jnp.exp(other_ref[state : state + 1, :]) * chip + other_ref[0:state, :]
    return jnp.where(odd, joined, chip)


def finish_kernel(
    layer, heads, cells_x, odd_ref, half_ref, other_half_ref, other_ref, hid_ref, local_ref, gate_ref, read_ref, dec_ref,
    state_ref, matrix_ref, rows_ref, out_ref, tile_ref, turn_ref, plane_ref,
):
    group = hid_ref.shape[0]
    model = matrix_ref.shape[1]
    inner = local_ref.shape[1]
    refs = (hid_ref, local_ref, gate_ref, read_ref, dec_ref, state_ref)
    enter = entered(odd_ref, half_ref, other_half_ref, other_ref, read_ref.shape[1])
    out_gain = columns_of(layer, rows_ref)[:inner, 9:10]
    out_proj = matrix_ref[layer][:, -LANES:][:, :inner]
    for q in range(0, group, wide):
        result = finished(q, layer, heads, enter, refs, out_gain, out_proj).astype(f32)
        for u in range(wide):
            at = pl.multiple_of((pl.program_id(0) * group + q + u) * model, 8)
            tile_ref[pl.ds(at, model), :] = result[:, span(u)]

    @pl.when(pl.program_id(0) == pl.num_programs(0) - 1)
    def _():
        to_planes(tile_ref, out_ref, turn_ref, plane_ref, model, cells_x)


def head_kernel(
    layer, heads, odd_ref, half_ref, other_half_ref, other_ref, hid_ref, local_ref, gate_ref, read_ref, dec_ref,
    state_ref, matrix_ref, rows_ref, head_ref, bias_ref, labels_ref, distance_ref, features_ref, grad_ref, loss_ref,
    feature_scr, logit_scr, sum_scr,
):
    group = hid_ref.shape[0]
    classes = distance_ref.shape[0]
    inner = local_ref.shape[1]
    refs = (hid_ref, local_ref, gate_ref, read_ref, dec_ref, state_ref)
    enter = entered(odd_ref, half_ref, other_half_ref, other_ref, read_ref.shape[1])
    out_gain = columns_of(layer, rows_ref)[:inner, 9:10]
    out_proj = matrix_ref[layer][:, -LANES:][:, :inner]
    bias = columns(bias_ref[...])[:classes, 0:1]

    @pl.when(pl.program_id(0) == 0)
    def _():
        sum_scr[...] = jnp.zeros_like(sum_scr)

    for q in range(0, group, wide):
        result = finished(q, layer, heads, enter, refs, out_gain, out_proj)
        logits = project(head_ref[...], result) + bias
        result = result.astype(f32)
        for u in range(wide):
            feature_scr[pl.ds(q + u, result.shape[0], stride=group), :] = result[:, span(u)]
            logit_scr[pl.ds(q + u, classes, stride=group), :] = logits[:, span(u)]
    features = feature_scr[...].reshape(-1, group, SCAN_BLOCK)
    features_ref[...] = features.astype(bf16)
    logits = logit_scr[...].reshape(-1, group, SCAN_BLOCK)
    labels = labels_ref[...]
    peak = jnp.max(logits, axis=0)
    shifted = jnp.exp(logits - peak[None])
    partition = jnp.sum(shifted, axis=0)
    probability = shifted / partition[None]
    distance_map = distance_ref[...].astype(f32) * (1.0 / dist_unit)
    weighted = probability * distance_map
    expect = jnp.sum(weighted, axis=0)
    hot = labels[None] == lax.broadcasted_iota(jnp.int32, logits.shape, 0)
    chosen = jnp.sum(jnp.where(hot, logits, 0.0), axis=0)
    loss = peak + jnp.log(partition) - chosen + expect
    grad_ref[...] = probability - jnp.where(hot, 1.0, 0.0) + weighted - probability * expect[None]
    sum_scr[...] += jnp.sum(loss, axis=0, keepdims=True)
    loss_ref[...] = jnp.broadcast_to(sum_scr[...], loss_ref.shape)


def whole(shape):
    return pl.BlockSpec(shape, lambda g: (0,) * len(shape))


def blocks(group, *rest):
    return pl.BlockSpec((group,) + rest, lambda g: (g,) + (0,) * len(rest))


def params(size=vmem_bytes):
    return pltpu.CompilerParams(vmem_limit_bytes=size)


def cost(us):
    return pl.CostEstimate(flops=0, bytes_accessed=int(us * 3.5e6), transcendentals=0)


def from_before(value):
    size = lax.axis_size(axes)
    value = jnp.where(lax.axis_index(axes) == size - 1, jnp.zeros_like(value), value)
    return lax.ppermute(value, axes, [(i, (i + 1) % size) for i in range(size)])


def prefix_state(total, state, beside):
    size = lax.axis_size(axes)
    me = lax.axis_index(axes)
    odd = (me & 1).astype(jnp.int32).reshape(1)
    swap = [(i, i ^ 1) for i in range(size)]
    other = lax.ppermute(total, axes, swap)
    chips = size // 2
    groups = [list(range(core, size, 2)) for core in range(2)]
    rows = state // 2 + 8
    smem, vmem = pl.BlockSpec(memory_space=pltpu.SMEM), pl.BlockSpec(memory_space=pltpu.VMEM)
    offer = pl.pallas_call(
        offer_kernel,
        in_specs=[smem, vmem, vmem],
        out_specs=vmem,
        out_shape=jax.ShapeDtypeStruct((chips, rows, LANES), f32),
        compiler_params=params(4 * 1024 * 1024),
        name="offer",
    )(odd, total, other)
    got = lax.all_to_all(offer, axes, 0, 0, tiled=True, axis_index_groups=groups)
    got, beside = lax.optimization_barrier((got, beside))
    ahead = pl.pallas_call(
        join_kernel,
        in_specs=[smem, vmem],
        out_specs=vmem,
        out_shape=jax.ShapeDtypeStruct((state // 2, LANES), f32),
        compiler_params=params(4 * 1024 * 1024),
        name="join",
    )((me // 2).astype(jnp.int32).reshape(1), got)
    return (odd, ahead, lax.ppermute(ahead, axes, swap), other), beside


def offer_kernel(odd_ref, mine_ref, other_ref, out_ref):
    odd = odd_ref[0] != 0
    half = out_ref.shape[1] - 8
    state = 2 * half
    first = jnp.where(odd, other_ref[...], mine_ref[...])
    second = jnp.where(odd, mine_ref[...], other_ref[...])
    pair = jnp.exp(second[state : state + 1]) * first[:state] + second[:state]
    part = jnp.where(odd, pair[half:], pair[:half])
    log = first[state:] + second[state:]
    for chip in range(out_ref.shape[0]):
        out_ref[chip, 0:half, :] = part
        out_ref[chip, half:, :] = log


def join_kernel(count_ref, parts_ref, out_ref):
    half = out_ref.shape[0]

    def step(j, running):
        return jnp.exp(parts_ref[j, half : half + 1, :]) * running + parts_ref[j, 0:half, :]

    out_ref[...] = lax.fori_loop(0, count_ref[0], step, jnp.zeros_like(out_ref))


def tile(count, rows, kind):
    return jax.ShapeDtypeStruct((count, rows, SCAN_BLOCK), kind)


def far_tile(count, rows, kind):
    return pltpu.HBM((count, rows, SCAN_BLOCK), kind)


def tail_spec(tail):
    if tail.ndim == 2:
        return whole(tail.shape)
    last = tail.shape[0] - 1
    return pl.BlockSpec((1,) + tail.shape[1:], lambda g: (last, 0, 0))


def call_states(layer, hidden, tail, weights, group):
    from_volume = tail.ndim == 2
    inner, heads, state = weights["inner"], weights["heads"], weights["state"]
    model = weights["model"]
    count = hidden.shape[1] * hidden.shape[2] // SCAN_BLOCK if from_volume else hidden.shape[0]
    first_rows = inner + state
    names = ("matrices", "rows")
    out_specs = [
        blocks(group, inner, SCAN_BLOCK),
        blocks(group, state, SCAN_BLOCK),
        blocks(group, 16, SCAN_BLOCK),
        blocks(group, state + 8, LANES),
        whole((state + 8, LANES)),
    ]
    out_shape = [
        tile(count, inner, bf16),
        far_tile(count, state, bf16),
        tile(count, 16, f32),
        far_tile(count, state + 8, f32),
        jax.ShapeDtypeStruct((state + 8, LANES), f32),
    ]
    scratch = [pltpu.VMEM((first_rows, (group + 1) * SCAN_BLOCK), f32), pltpu.VMEM((state + 8, LANES), f32)]
    if from_volume:
        out_specs.append(whole((count, model, SCAN_BLOCK)))
        out_shape.append(tile(count, model, bf16))
        per = LANES // hidden.shape[1]
        scratch.append(pltpu.VMEM((model // per, hidden.shape[2], LANES), f32))
        scratch.append(pltpu.VMEM((count * model, LANES), f32))
    return pl.pallas_call(
        functools.partial(state_kernel, layer, heads, from_volume),
        grid=(count // group,),
        in_specs=[whole(hidden.shape) if from_volume else blocks(group, *hidden.shape[1:]), tail_spec(tail)]
        + [whole(weights[name].shape) for name in names],
        out_specs=out_specs,
        out_shape=out_shape,
        scratch_shapes=scratch,
        compiler_params=params(),
        name="states",
    )(hidden, tail, *(weights[name] for name in names))


def call_local(layer, hidden, tail, inner_values, write, dec, weights, group):
    count = hidden.shape[0]
    inner, heads, state = weights["inner"], weights["heads"], weights["state"]
    names = ("matrices", "rows")
    return pl.pallas_call(
        functools.partial(local_kernel, layer, heads),
        grid=(count // group,),
        in_specs=[blocks(group, *hidden.shape[1:]), tail_spec(tail)]
        + [whole(weights[name].shape) for name in names]
        + [blocks(group, inner, SCAN_BLOCK), blocks(group, state, SCAN_BLOCK), blocks(group, 16, SCAN_BLOCK)],
        out_specs=[
            blocks(group, inner, SCAN_BLOCK),
            blocks(group, inner, SCAN_BLOCK),
            blocks(group, state, SCAN_BLOCK),
        ],
        out_shape=[far_tile(count, inner, f32), far_tile(count, inner, f32), far_tile(count, state, bf16)],
        scratch_shapes=[
            pltpu.VMEM((state, (group + 1) * SCAN_BLOCK), f32),
            pltpu.VMEM((group, SCAN_BLOCK, SCAN_BLOCK), f32),
            pltpu.VMEM((group, heads, SCAN_BLOCK, SCAN_BLOCK), bf16),
        ],
        compiler_params=params(),
        name="local",
    )(hidden, tail, *(weights[name] for name in names), inner_values, write, dec)


def finish_specs(group, hidden, weights):
    inner, state = weights["inner"], weights["state"]
    return [
        pl.BlockSpec(memory_space=pltpu.SMEM),
        whole((state // 2, LANES)),
        whole((state // 2, LANES)),
        whole((state + 8, LANES)),
        blocks(group, *hidden.shape[1:]),
        blocks(group, inner, SCAN_BLOCK),
        blocks(group, inner, SCAN_BLOCK),
        blocks(group, state, SCAN_BLOCK),
        blocks(group, 16, SCAN_BLOCK),
        blocks(group, state + 8, LANES),
        whole(weights["matrices"].shape),
        whole(weights["rows"].shape),
    ]


def call_finish(layer, cells, enter, hidden, local, gate, read, dec, states, weights, group):
    count, model, _ = hidden.shape
    cells_x, cells_y = cells
    rows = model + 8
    per = LANES // cells_x
    return pl.pallas_call(
        functools.partial(finish_kernel, layer, weights["heads"], cells_x),
        grid=(count // group,),
        in_specs=finish_specs(group, hidden, weights),
        out_specs=whole((cells_x, rows, cells_y)),
        out_shape=jax.ShapeDtypeStruct((cells_x, rows, cells_y), bf16),
        scratch_shapes=[
            pltpu.VMEM((count * model, LANES), f32),
            pltpu.VMEM((model // per, cells_y, LANES), f32),
            pltpu.VMEM(((cells_x + 1) * rows, LANES), f32),
        ],
        compiler_params=params(63 * 1024 * 1024),
        name="finish",
    )(*enter, hidden, local, gate, read, dec, states, weights["matrices"], weights["rows"])


def call_heads(
    layer, size, enter, hidden, local, gate, read, dec, states, weights, group, head_weight, head_bias, labels, distance
):
    classes, model = head_weight.shape
    count = hidden.shape[0]
    plane = lambda rows: pl.BlockSpec((rows, group, SCAN_BLOCK), lambda g: (0, g, 0))
    return pl.pallas_call(
        functools.partial(head_kernel, layer, weights["heads"]),
        grid=(count // group,),
        in_specs=finish_specs(group, hidden, weights)
        + [
            whole(head_weight.shape),
            whole(head_bias.shape),
            pl.BlockSpec((group, SCAN_BLOCK), lambda g: (g, 0)),
            plane(classes),
        ],
        out_specs=[plane(model), plane(classes), whole((size, SCAN_BLOCK))],
        out_shape=[
            jax.ShapeDtypeStruct((model, count, SCAN_BLOCK), bf16),
            jax.ShapeDtypeStruct((classes, count, SCAN_BLOCK), f32),
            jax.ShapeDtypeStruct((size, SCAN_BLOCK), f32),
        ],
        scratch_shapes=[
            pltpu.VMEM((model * group, SCAN_BLOCK), f32),
            pltpu.VMEM((classes * group, SCAN_BLOCK), f32),
            pltpu.VMEM((1, SCAN_BLOCK), f32),
        ],
        compiler_params=params(63 * 1024 * 1024),
        name="heads",
    )(
        *enter, hidden, local, gate, read, dec, states, weights["matrices"], weights["rows"],
        head_weight, head_bias, labels, distance,
    )


def packed(norm_gain, in_proj, dt_proj, dt_bias, decay_rate, conv_weight, conv_bias, skip_gain, out_gain, out_proj):
    lanes = lambda value, width: jnp.pad(value, ((0, 0),) * (value.ndim - 1) + ((0, width - value.shape[-1]),))
    first = jnp.concatenate([in_proj, dt_proj], axis=1)
    width = -(-(first.shape[1] + 8) // LANES) * LANES
    second = out_proj.shape[2]
    matrices = jnp.concatenate(
        [lanes(jnp.swapaxes(first, 1, 2), width), lanes(out_proj, -(-second // LANES) * LANES)], axis=2
    )
    width = -(-conv_bias.shape[1] // LANES) * LANES
    vectors = [conv_bias, norm_gain, dt_bias, -decay_rate, skip_gain, out_gain]
    rows = [lanes(jnp.swapaxes(conv_weight, 1, 2), width)] + [lanes(v, width)[:, None] for v in vectors]
    count = sum(r.shape[1] for r in rows)
    rows.append(jnp.zeros((rows[0].shape[0], -(-count // 8) * 8 - count, width), f32))
    return matrices, jnp.concatenate(rows, axis=1)


def per_device(
    volume, norm_gain, in_proj, dt_proj, dt_bias, decay_rate, conv_weight, conv_bias, skip_gain, out_gain,
    out_proj, head_weight, head_bias, labels, distance,
):
    size = lax.axis_size(axes)
    model, _, cells_y, cells_x = volume.shape
    classes = head_weight.shape[0]
    inner = out_proj.shape[2]
    heads = decay_rate.shape[1]
    weights = dict(heads=heads, inner=inner, state=(in_proj.shape[1] - 2 * inner) // 2, model=model)
    weights["matrices"], weights["rows"] = packed(
        norm_gain, in_proj, dt_proj, dt_bias, decay_rate, conv_weight, conv_bias, skip_gain, out_gain, out_proj
    )
    state = weights["state"]
    count = cells_y * cells_x // SCAN_BLOCK
    group = min(16, count)

    tail = from_before(jnp.pad(volume[:, 0, cells_y - 1, :], ((0, 0), (SCAN_BLOCK - cells_x, 0))))
    plane = jnp.swapaxes(volume[:, 0], 1, 2)
    inner_values, write, dec, states, total, hidden = call_states(0, plane, tail, weights, group)
    local, gate, read = call_local(0, hidden, tail, inner_values, write, dec, weights, group)
    enter, (local, gate, read) = prefix_state(total, state, (local, gate, read))
    planes = call_finish(0, (cells_x, cells_y), enter, hidden, local, gate, read, dec, states, weights, group)

    hidden = lax.all_to_all(planes, axes, split_axis=0, concat_axis=0, tiled=True)
    count = hidden.shape[0]
    group = min(16, count)
    inner_values, write, dec, states, total = call_states(1, hidden, hidden, weights, group)
    local, gate, read = call_local(1, hidden, hidden, inner_values, write, dec, weights, group)
    enter, (local, gate, read) = prefix_state(total, state, (local, gate, read))
    features, grad, loss = call_heads(
        1, size, enter, hidden, local, gate, read, dec, states, weights, group, head_weight, head_bias[None, :],
        labels.reshape(count, SCAN_BLOCK), distance.reshape(classes, count, SCAN_BLOCK),
    )
    shared = lax.all_to_all(loss, axes, 0, 0, tiled=True)
    voxel_weight = 1.0 + 3.0 * jnp.arange(size, dtype=f32) / (size - 1.0)
    total_loss = jnp.sum(voxel_weight[:, None] * shared) / (2.5 * count * SCAN_BLOCK * size)
    return (
        features.reshape(model, 1, count, SCAN_BLOCK),
        grad.reshape(classes, 1, count, SCAN_BLOCK),
        total_loss,
    )


def solution(mesh):
    plane = P(None, axes, None, None)
    return jax.shard_map(
        per_device,
        mesh=mesh,
        in_specs=(plane,) + (P(),) * 12 + (P(axes, None, None), plane),
        out_specs=(plane, plane, P()),
        check_vma=False,
    )
```

time: 140 us -> 101 us (0.72)
  starting transfers between devices: 30.1 us -> 10.9 us
  Pallas kernels: 52.6 us -> 36.4 us
  blocking collectives: 9.69 us -> 17.1 us
  waiting for transfers between devices: 31.9 us -> 25.3 us
  local copies, waits for them, and re-layouts: 9.36 us -> 5.86 us
    ppermute x12 -> x5, starting transfers between devices: 24.9 us -> 0.48 us  [the longest x1 0.47 us: from_before(): return lax.ppermute(value, axes, [(i, (i + 1) % size) for i in range(size)])]
    pallas_call x6 -> x10, Pallas kernels: 52.6 us -> 36.4 us  [the longest x2 12.4 us: call_local(): pl.pallas_call(functools.partial(local_kernel, layer, heads), grid=(count...]
    ppermute x12 -> x5, waiting for transfers between devices: 19.2 us -> 9.23 us  [the longest x1 4.46 us: from_before(): return lax.ppermute(value, axes, [(i, (i + 1) % size) for i in range(size)])]
    all_to_all x1, blocking collectives: 9.69 us -> 17.1 us  [per_device(): lax.all_to_all(planes, axes, split_axis=0, concat_axis=0, tiled=True)]
    all_to_all x1 -> x3, starting transfers between devices: 5.2 us -> 10.4 us  [the longest x2 7.66 us: prefix_state(): lax.all_to_all(offer, axes, 0, 0, tiled=True, axis_index_groups=groups)]
    all_to_all x1 -> x3, waiting for transfers between devices: 12.7 us -> 16 us  [the longest x2 8.9 us: prefix_state(): lax.all_to_all(offer, axes, 0, 0, tiled=True, axis_index_groups=groups)]
    reshape x4 -> x0, local copies, waits for them, and re-layouts: 2.95 us -> none  [the longest x2 1.99 us: per_device(): after.transpose(1, 0, 2).reshape(model, cells_y, cells_x).transpose(2, 0, 1)]
    unnamed x47 -> x50, local copies, waits for them, and re-layouts: 2.5 us -> 4.49 us
  transfers between devices with their start and end apart: 13 -> 8, of which waited for: 10 -> 8; matrix products, arithmetic and copies ran while one was open for 4% -> 3% of each run, Pallas kernels for 19% -> 12%
where the time goes in v1:
time: 101 us
  Pallas kernels  36.4 us (36%)
  waiting for transfers between devices  25.3 us (25%)
  blocking collectives  17.1 us (17%)
  starting transfers between devices  10.9 us (11%)
  local copies, waits for them, and re-layouts  5.86 us (6%)
  between operations  2.81 us (3%)
  other arithmetic  2.48 us (2%)
    all_to_all x1, blocking collectives, per_device(): lax.all_to_all(planes, axes, split_axis=0, concat_axis=0, tiled=True)  17.1 us
    pallas_call x2, Pallas kernels, call_local(): pl.pallas_call(functools.partial(local_kernel, layer, heads), grid=(count...  12.4 us
    pallas_call x2, Pallas kernels, call_states(): pl.pallas_call(functools.partial(state_kernel, layer, heads, from_volume)...  9.96 us
    all_to_all x2, waiting for transfers between devices, prefix_state(): lax.all_to_all(offer, axes, 0, 0, tiled=True, axis_index_groups=groups)  8.9 us
    all_to_all x2, starting transfers between devices, prefix_state(): lax.all_to_all(offer, axes, 0, 0, tiled=True, axis_index_groups=groups)  7.66 us
    all_to_all x1, waiting for transfers between devices, per_device(): shared = lax.all_to_all(loss, axes, 0, 0, tiled=True)  7.14 us
    pallas_call x1, Pallas kernels, call_finish(): pl.pallas_call(functools.partial(finish_kernel, layer, weights['heads'],...  6.41 us
    pallas_call x1, Pallas kernels, call_heads(): pl.pallas_call(functools.partial(head_kernel, layer, weights['heads']), g...  6.02 us
  transfers between devices with their start and end apart: 8, of which 8 were waited for; matrix products, arithmetic and copies ran while one was open for 3% of the time, Pallas kernels for 12%

profile of v1, /device:TPU:0, one launch (start us, length us, event | category | flops | bytes accessed | tf_op | source)
XLA Modules:
  0.0 100.7 jit_solution(10814396216586962900)
XLA Ops:
  0.7 1.3 %slice.3 = bf16[48,1,1,32]{2,3,1,0:T(8,128)(2,1)S(1)} slice(bf16[48,1,128,32]{2,3,1,0:T(8,128)(2,1)} %param.15), slice={[0:48], [0:1], [127:128], [0:32]} | slice | bytes 6144 | tf_op jit(solution)/shard_map/slice | solution.py:653
  2.0 0.4 copy.27
  2.3 0.1 pad_select_fusion
  2.4 0.5 collective-permute-start
  2.9 0.8 copy.23
  3.7 1.0 maximum_bitcast_fusion
  4.6 0.8 fusion.2.matrix_ref
  5.7 4.5 %collective-permute-done.tail_ref = bf16[48,128]{1,0:T(8,128)(2,1)S(1)} collective-permute-done((bf16[48,128]{1,0:T(8,128)(2,1)S(1)}, bf16[48,128]{1,0:T(8,128)(2,1)S(1)}, u32[]{:S(2)}, u32[]{:S(2)}) %collective-permute-start) | collective-permute-done | bytes 12320 | tf_op jit(solution)/shard_map/ppermute | solution.py:407
  10.2 5.3 %states.2 = (bf16[32,96,128]{2,1,0:T(8,128)(2,1)S(1)}, bf16[32,64,128]{2,1,0:T(8,128)(2,1)}, f32[32,16,128]{2,1,0:T(8,128)S(1)}, f32[32,72,128]{2,1,0:T(8,128)},...) custom-call(bf16[48,32,128]{2,1,0:T(8,128)(2,1)S(1)} %bitcast.22, ...), custom_call_target="tpu_custom_call" | custom-call | tf_op jit(solution)/shard_map/states/pallas_call | solution.py:507
  15.5 1.2 %collective-permute-done.1.other_ref = f32[72,128]{1,0:T(8,128)S(1)} collective-permute-done((f32[72,128]{1,0:T(8,128)S(1)}, f32[72,128]{1,0:T(8,128)S(1)}, u32[]{:S(2)}, u32[]{:S(2)}) %collective-permute-start.1) | collective-permute-done | bytes 36896 | tf_op jit(solution)/shard_map/ppermute | solution.py:415
  16.7 0.8 offer.2
  17.5 3.8 %all-to-all-start = ((f32[16,40,128]{2,1,0:T(8,128)}), f32[16,40,128]{2,1,0:T(8,128)S(1)}, u32[]{:S(2)}, u32[]{:S(2)}) async-start(f32[16,40,128]{2,1,0:T(8,128)} %offer.2), calls=%async_computation | async-start | bytes 655360 | tf_op jit(solution)/shard_map/all_to_all | solution.py:428
  21.3 1.0 %copy-done.10 = bf16[32,64,128]{2,1,0:T(8,128)(2,1)S(1)} copy-done((bf16[32,64,128]{2,1,0:T(8,128)(2,1)S(1)}, bf16[32,64,128]{2,1,0:T(8,128)(2,1)}, u32[]{:S(2)}) %copy-start.10) | copy-done | bytes 524312
  22.3 6.2 %local.2 = (f32[32,96,128]{2,1,0:T(8,128)}, f32[32,96,128]{2,1,0:T(8,128)}, bf16[32,64,128]{2,1,0:T(8,128)(2,1)}) custom-call(bf16[32,48,128]{2,1,0:T(8,128)(2,1)S(1)} %get-tuple-element.32.hid_ref, bf16[48,128]{1,0:T(8,128)(2,1)S(1)} %collective-permute-done.tail_ref, bf16[2,48,512]{2,1,0:T(8,128)(2,1)S(1)} %fusion.2.matrix_ref, ...), custom_call_target="tpu_custom_call" | custom-call | tf_op jit(solution)/shard_map/local/pallas_call | solution.py:524
  28.6 4.5 %all-to-all-done.parts_ref = f32[16,40,128]{2,1,0:T(8,128)S(1)} async-done(((f32[16,40,128]{2,1,0:T(8,128)}), f32[16,40,128]{2,1,0:T(8,128)S(1)}, u32[]{:S(2)}, u32[]{:S(2)}) %all-to-all-start) | async-done | bytes 327712 | tf_op jit(solution)/shard_map/all_to_all | solution.py:428
  33.1 1.2 %collective-permute-done.2.other_half_ref = f32[32,128]{1,0:T(8,128)S(1)} collective-permute-done((f32[32,128]{1,0:T(8,128)S(1)}, f32[32,128]{1,0:T(8,128)S(1)}, u32[]{:S(2)}, u32[]{:S(2)}) %collective-permute-start.2) | collective-permute-done | bytes 16416 | tf_op jit(solution)/shard_map/ppermute | solution.py:438
  34.3 0.6 copy-done.16
  34.9 6.4 %finish.1 = bf16[32,56,128]{2,1,0:T(8,128)(2,1)} custom-call(s32[1]{0:T(128)} %bitcast.odd_ref, f32[32,128]{1,0:T(8,128)} %copy-done.14, f32[32,128]{1,0:T(8,128)} %copy-done.16, f32[72,128]{1,0:T(8,128)} %copy-done.12, bf16[32,48,128]{2,1,0:T(8,128)(2,1)} %copy-done.5, f32[32,96,128]{2,1,0:T(8,128)} %get-tuple-element.40.local_ref, ...), custom_call_target="tpu_custom_call" | custom-call | tf_op jit(solution)/shard_map/finish/pallas_call | solution.py:569
  41.3 17.1 %all_to_all.27.hid_ref.tail_ref = bf16[32,56,128]{2,1,0:T(8,128)(2,1)S(1)} all-to-all(bf16[32,56,128]{2,1,0:T(8,128)(2,1)} %finish.1), channel_id=1, replica_groups=mesh['row'=8,'col'=4] {'row','col'}, dimensions={0} | all-to-all | bytes 917504 | tf_op jit(solution)/shard_map/all_to_all | solution.py:660
  58.4 4.7 %states.3 = (bf16[32,96,128]{2,1,0:T(8,128)(2,1)S(1)}, bf16[32,64,128]{2,1,0:T(8,128)(2,1)}, f32[32,16,128]{2,1,0:T(8,128)S(1)}, f32[32,72,128]{2,1,0:T(8,128)}, f32[72,128]{1,0:T(8,128)S(1)}) custom-call(bf16[32,56,128]{2,1,0:T(8,128)(2,1)S(1)} %all_to_all.27.hid_ref.tail_ref, bf16[32,56,128]{2,1,0:T(8,128)(2,1)S(1)} %all_to_all.27.hid_ref.tail_ref, ...), custom_call_target="tpu_custom_call" | custom-call | tf_op jit(solution)/shard_map/states/pallas_call | solution.py:507
  63.1 1.2 %collective-permute-done.3.other_ref = f32[72,128]{1,0:T(8,128)S(1)} collective-permute-done((f32[72,128]{1,0:T(8,128)S(1)}, f32[72,128]{1,0:T(8,128)S(1)}, u32[]{:S(2)}, u32[]{:S(2)}) %collective-permute-start.3) | collective-permute-done | bytes 36896 | tf_op jit(solution)/shard_map/ppermute | solution.py:415
  64.3 0.8 offer.3
  65.0 3.9 %all-to-all-start.2 = ((f32[16,40,128]{2,1,0:T(8,128)}), f32[16,40,128]{2,1,0:T(8,128)S(1)}, u32[]{:S(2)}, u32[]{:S(2)}) async-start(f32[16,40,128]{2,1,0:T(8,128)} %offer.3), calls=%async_computation.2 | async-start | bytes 655360 | tf_op jit(solution)/shard_map/all_to_all | solution.py:428
  68.9 1.0 %copy-done.9 = bf16[32,64,128]{2,1,0:T(8,128)(2,1)S(1)} copy-done((bf16[32,64,128]{2,1,0:T(8,128)(2,1)S(1)}, bf16[32,64,128]{2,1,0:T(8,128)(2,1)}, u32[]{:S(2)}) %copy-start.9) | copy-done | bytes 524312
  70.0 6.2 %local.3 = (f32[32,96,128]{2,1,0:T(8,128)}, f32[32,96,128]{2,1,0:T(8,128)}, bf16[32,64,128]{2,1,0:T(8,128)(2,1)}) custom-call(bf16[32,56,128]{2,1,0:T(8,128)(2,1)S(1)} %all_to_all.27.hid_ref.tail_ref, bf16[32,56,128]{2,1,0:T(8,128)(2,1)S(1)} %all_to_all.27.hid_ref.tail_ref, bf16[2,48,512]{2,1,0:T(8,128)(2,1)S(1)} %copy-done.2, f32[2,16,256]{2,1,0:T(8,128)S(1)} %copy-done.4, ...), custom_call_target="tpu_custom_call" | custom-call | tf_op jit(solution)/shard_map/local/pallas_call | solution.py:524
  76.2 4.4 %all-to-all-done.2.parts_ref = f32[16,40,128]{2,1,0:T(8,128)S(1)} async-done(((f32[16,40,128]{2,1,0:T(8,128)}), f32[16,40,128]{2,1,0:T(8,128)S(1)}, u32[]{:S(2)}, u32[]{:S(2)}) %all-to-all-start.2) | async-done | bytes 327712 | tf_op jit(solution)/shard_map/all_to_all | solution.py:428
  80.6 1.2 %collective-permute-done.4.other_half_ref = f32[32,128]{1,0:T(8,128)S(1)} collective-permute-done((f32[32,128]{1,0:T(8,128)S(1)}, f32[32,128]{1,0:T(8,128)S(1)}, u32[]{:S(2)}, u32[]{:S(2)}) %collective-permute-start.4) | collective-permute-done | bytes 16416 | tf_op jit(solution)/shard_map/ppermute | solution.py:438
  81.8 0.6 copy-done.15
  82.3 6.0 %heads.1 = (bf16[48,32,128]{2,1,0:T(8,128)(2,1)}, f32[14,32,128]{2,1,0:T(8,128)}, f32[32,128]{1,0:T(8,128)}) custom-call(s32[1]{0:T(128)} %bitcast.odd_ref, f32[32,128]{1,0:T(8,128)} %copy-done.13, f32[32,128]{1,0:T(8,128)} %copy-done.15, f32[72,128]{1,0:T(8,128)} %copy-done.11, bf16[32,56,128]{2,1,0:T(8,128)(2,1)} %copy-done, ...), custom_call_target="tpu_custom_call" | custom-call | tf_op jit(solution)/shard_map/heads/pallas_call | solution.py:591
  88.4 2.7 %all-to-all-start.3 = ((f32[32,1,128]{2,1,0:T(1,128)}), f32[32,1,128]{2,1,0:T(1,128)S(1)}, u32[]{:S(2)}, u32[]{:S(2)}) async-start(f32[32,1,128]{2,1,0:T(1,128)} %bitcast.27), calls=%async_computation.3 | async-start | bytes 32768 | tf_op jit(solution)/shard_map/all_to_all | solution.py:670
  91.1 7.1 %all-to-all-done.3 = f32[32,1,128]{2,1,0:T(1,128)S(1)} async-done(((f32[32,1,128]{2,1,0:T(1,128)}), f32[32,1,128]{2,1,0:T(1,128)S(1)}, u32[]{:S(2)}, u32[]{:S(2)}) %all-to-all-start.3) | async-done | bytes 16416 | tf_op jit(solution)/shard_map/all_to_all | solution.py:670
  98.3 0.7 multiply_reduce_fusion
  (67 shorter events, 0.2 us)
Async XLA Ops:
  0.6 9.5 %copy-start.6 = (bf16[48,1,128,32]{2,3,1,0:T(8,128)(2,1)S(1)}, bf16[48,1,128,32]{2,3,1,0:T(8,128)(2,1)}, u32[]{:S(2)}) copy-start(bf16[48,1,128,32]{2,3,1,0:T(8,128)(2,1)} %param.15) | copy-start | bytes 1179652
  0.6 4.8 %copy-start.23 = (f32[2,3]{1,0:T(2,128)S(1)}, f32[2,3]{1,0:T(2,128)}, u32[]{:S(2)}) copy-start(f32[2,3]{1,0:T(2,128)} %param.20) | copy-start | bytes 76
  0.7 4.8 %copy-start.17 = (f32[2,224,4]{1,2,0:T(4,128)S(1)}, f32[2,224,4]{1,2,0:T(4,128)}, u32[]{:S(2)}) copy-start(f32[2,224,4]{1,2,0:T(4,128)} %param.21) | copy-start | bytes 21508
  0.7 4.8 %copy-start.18 = (f32[2,224]{1,0:T(2,128)S(1)}, f32[2,224]{1,0:T(2,128)}, u32[]{:S(2)}) copy-start(f32[2,224]{1,0:T(2,128)} %param.22) | copy-start | bytes 5380
  0.7 4.8 %copy-start.19 = (f32[2,48]{1,0:T(2,128)S(1)}, f32[2,48]{1,0:T(2,128)}, u32[]{:S(2)}) copy-start(f32[2,48]{1,0:T(2,128)} %param.16) | copy-start | bytes 1156
  0.7 4.9 %copy-start.20 = (f32[2,3]{1,0:T(2,128)S(1)}, f32[2,3]{1,0:T(2,128)}, u32[]{:S(2)}) copy-start(f32[2,3]{1,0:T(2,128)} %param.19) | copy-start | bytes 76
  0.7 4.9 %copy-start.21 = (f32[2,3]{1,0:T(2,128)S(1)}, f32[2,3]{1,0:T(2,128)}, u32[]{:S(2)}) copy-start(f32[2,3]{1,0:T(2,128)} %param.23) | copy-start | bytes 76
  0.7 4.9 %copy-start.22 = (f32[2,96]{1,0:T(2,128)S(1)}, f32[2,96]{1,0:T(2,128)}, u32[]{:S(2)}) copy-start(f32[2,96]{1,0:T(2,128)} %param.24) | copy-start | bytes 2308
  2.4 7.8 %collective-permute-start = (bf16[48,128]{1,0:T(8,128)(2,1)S(1)}, bf16[48,128]{1,0:T(8,128)(2,1)S(1)}, u32[]{:S(2)}, u32[]{:S(2)}) collective-permute-start(bf16[48,128]{1,0:T(8,128)(2,1)S(1)} %pad_select_fusion), channel_id=1, source_target_pairs={{0,1},{1,2},{2,3},{3,4},{4,5},{5,6},{6,7},{7,8},{8,9},{9,10},{10,1... | collective-permute-start | bytes 36872 | tf_op jit(solution)/shard_map/ppermute | solution.py:407
  5.4 23.1 %copy-start.1 = (bf16[2,48,512]{2,1,0:T(8,128)(2,1)}, bf16[2,48,512]{2,1,0:T(8,128)(2,1)S(1)}, u32[]{:S(2)}) copy-start(bf16[2,48,512]{2,1,0:T(8,128)(2,1)S(1)} %fusion.2.matrix_ref) | copy-start | bytes 294916
  5.7 22.8 %copy-start.3 = (f32[2,16,256]{2,1,0:T(8,128)}, f32[2,16,256]{2,1,0:T(8,128)S(1)}, u32[]{:S(2)}) copy-start(f32[2,16,256]{2,1,0:T(8,128)S(1)} %concatenate.11.rows_ref) | copy-start | bytes 98308
  15.5 13.1 %copy-start.5 = (bf16[32,48,128]{2,1,0:T(8,128)(2,1)}, bf16[32,48,128]{2,1,0:T(8,128)(2,1)S(1)}, u32[]{:S(2)}) copy-start(bf16[32,48,128]{2,1,0:T(8,128)(2,1)S(1)} %get-tuple-element.32.hid_ref) | copy-start | bytes 1179652
  15.5 13.1 %copy-start.8 = (f32[32,16,128]{2,1,0:T(8,128)}, f32[32,16,128]{2,1,0:T(8,128)S(1)}, u32[]{:S(2)}) copy-start(f32[32,16,128]{2,1,0:T(8,128)S(1)} %get-tuple-element.35.dec_ref) | copy-start | bytes 786436
  15.5 1.2 %collective-permute-start.1 = (f32[72,128]{1,0:T(8,128)S(1)}, f32[72,128]{1,0:T(8,128)S(1)}, u32[]{:S(2)}, u32[]{:S(2)}) collective-permute-start(f32[72,128]{1,0:T(8,128)S(1)} %get-tuple-element.31.mine_ref), channel_id=1, source_target_pairs={{0,1},{1,0},{2,3},{3,2},{4,5},{5,4},{6,7},{7,6},{8,9},{9,8},{10,11... | collective-permute-start | bytes 110600 | tf_op jit(solution)/shard_map/ppermute | solution.py:415
  16.7 11.9 %copy-start.12 = (f32[72,128]{1,0:T(8,128)}, f32[72,128]{1,0:T(8,128)S(1)}, u32[]{:S(2)}) copy-start(f32[72,128]{1,0:T(8,128)S(1)} %collective-permute-done.1.other_ref) | copy-start | bytes 110596
  17.5 15.6 %all-to-all-start = ((f32[16,40,128]{2,1,0:T(8,128)}), f32[16,40,128]{2,1,0:T(8,128)S(1)}, u32[]{:S(2)}, u32[]{:S(2)}) async-start(f32[16,40,128]{2,1,0:T(8,128)} %offer.2), calls=%async_computation | async-start | bytes 655360 | tf_op jit(solution)/shard_map/all_to_all | solution.py:428
  21.3 1.0 %copy-start.10 = (bf16[32,64,128]{2,1,0:T(8,128)(2,1)S(1)}, bf16[32,64,128]{2,1,0:T(8,128)(2,1)}, u32[]{:S(2)}) copy-start(bf16[32,64,128]{2,1,0:T(8,128)(2,1)} %get-tuple-element.34.write_ref) | copy-start | bytes 1572868
  33.1 1.2 %copy-start.14 = (f32[32,128]{1,0:T(8,128)}, f32[32,128]{1,0:T(8,128)S(1)}, u32[]{:S(2)}) copy-start(f32[32,128]{1,0:T(8,128)S(1)} %join.2.half_ref) | copy-start | bytes 49156
  33.1 1.2 %collective-permute-start.2 = (f32[32,128]{1,0:T(8,128)S(1)}, f32[32,128]{1,0:T(8,128)S(1)}, u32[]{:S(2)}, u32[]{:S(2)}) collective-permute-start(f32[32,128]{1,0:T(8,128)S(1)} %join.2.half_ref), channel_id=1, source_target_pairs={{0,1},{1,0},{2,3},{3,2},{4,5},{5,4},{6,7},{7,6},{8,9},{9,8},{10,11... | collective-permute-start | bytes 49160 | tf_op jit(solution)/shard_map/ppermute | solution.py:438
  34.3 0.6 copy-start.16
  34.9 23.5 %copy-start.2 = (bf16[2,48,512]{2,1,0:T(8,128)(2,1)S(1)}, bf16[2,48,512]{2,1,0:T(8,128)(2,1)}, u32[]{:S(2)}) copy-start(bf16[2,48,512]{2,1,0:T(8,128)(2,1)} %copy-done.1) | copy-start | bytes 294916
  34.9 23.5 %copy-start.4 = (f32[2,16,256]{2,1,0:T(8,128)S(1)}, f32[2,16,256]{2,1,0:T(8,128)}, u32[]{:S(2)}) copy-start(f32[2,16,256]{2,1,0:T(8,128)} %copy-done.3) | copy-start | bytes 98308
  58.4 17.8 %copy-start = (bf16[32,56,128]{2,1,0:T(8,128)(2,1)}, bf16[32,56,128]{2,1,0:T(8,128)(2,1)S(1)}, u32[]{:S(2)}) copy-start(bf16[32,56,128]{2,1,0:T(8,128)(2,1)S(1)} %all_to_all.27.hid_ref.tail_ref) | copy-start | bytes 1376260
  63.1 13.1 %copy-start.7 = (f32[32,16,128]{2,1,0:T(8,128)}, f32[32,16,128]{2,1,0:T(8,128)S(1)}, u32[]{:S(2)}) copy-start(f32[32,16,128]{2,1,0:T(8,128)S(1)} %get-tuple-element.47.dec_ref) | copy-start | bytes 786436
  63.1 1.2 %collective-permute-start.3 = (f32[72,128]{1,0:T(8,128)S(1)}, f32[72,128]{1,0:T(8,128)S(1)}, u32[]{:S(2)}, u32[]{:S(2)}) collective-permute-start(f32[72,128]{1,0:T(8,128)S(1)} %get-tuple-element.44.mine_ref), channel_id=1, source_target_pairs={{0,1},{1,0},{2,3},{3,2},{4,5},{5,4},{6,7},{7,6},{8,9},{9,8},{10,11... | collective-permute-start | bytes 110600 | tf_op jit(solution)/shard_map/ppermute | solution.py:415
  64.3 11.9 %copy-start.11 = (f32[72,128]{1,0:T(8,128)}, f32[72,128]{1,0:T(8,128)S(1)}, u32[]{:S(2)}) copy-start(f32[72,128]{1,0:T(8,128)S(1)} %collective-permute-done.3.other_ref) | copy-start | bytes 110596
  65.0 15.5 %all-to-all-start.2 = ((f32[16,40,128]{2,1,0:T(8,128)}), f32[16,40,128]{2,1,0:T(8,128)S(1)}, u32[]{:S(2)}, u32[]{:S(2)}) async-start(f32[16,40,128]{2,1,0:T(8,128)} %offer.3), calls=%async_computation.2 | async-start | bytes 655360 | tf_op jit(solution)/shard_map/all_to_all | solution.py:428
  68.9 1.0 %copy-start.9 = (bf16[32,64,128]{2,1,0:T(8,128)(2,1)S(1)}, bf16[32,64,128]{2,1,0:T(8,128)(2,1)}, u32[]{:S(2)}) copy-start(bf16[32,64,128]{2,1,0:T(8,128)(2,1)} %get-tuple-element.46.write_ref) | copy-start | bytes 1572868
  80.6 1.2 %copy-start.13 = (f32[32,128]{1,0:T(8,128)}, f32[32,128]{1,0:T(8,128)S(1)}, u32[]{:S(2)}) copy-start(f32[32,128]{1,0:T(8,128)S(1)} %join.3.half_ref) | copy-start | bytes 49156
  80.6 1.2 %collective-permute-start.4 = (f32[32,128]{1,0:T(8,128)S(1)}, f32[32,128]{1,0:T(8,128)S(1)}, u32[]{:S(2)}, u32[]{:S(2)}) collective-permute-start(f32[32,128]{1,0:T(8,128)S(1)} %join.3.half_ref), channel_id=1, source_target_pairs={{0,1},{1,0},{2,3},{3,2},{4,5},{5,4},{6,7},{7,6},{8,9},{9,8},{10,11... | collective-permute-start | bytes 49160 | tf_op jit(solution)/shard_map/ppermute | solution.py:438
  81.7 0.6 copy-start.15
  88.4 9.9 %all-to-all-start.3 = ((f32[32,1,128]{2,1,0:T(1,128)}), f32[32,1,128]{2,1,0:T(1,128)S(1)}, u32[]{:S(2)}, u32[]{:S(2)}) async-start(f32[32,1,128]{2,1,0:T(1,128)} %bitcast.27), calls=%async_computation.3 | async-start | bytes 32768 | tf_op jit(solution)/shard_map/all_to_all | solution.py:670

commit v2 on v1

v2 whole, which is shorter than its diff:
```python
import functools

import jax
import jax.numpy as jnp
from jax import lax
from jax.experimental import pallas as pl
from jax.experimental.pallas import tpu as pltpu
from jax.sharding import PartitionSpec as P

SCAN_BLOCK = 128
LANES = 128

eps = 1e-05
dist_unit = 4096.0
axes = ("row", "col")
f32, bf16 = jnp.float32, jnp.bfloat16
vmem_bytes = 24 * 1024 * 1024
wide = 4


def half_silu(v):
    return v + v * jnp.tanh(v)


def rounded(v):
    return v.astype(bf16).astype(f32)


def normalise(hidden, gain_col):
    values = hidden.astype(f32)
    mean_sq = jnp.mean(values * values, axis=0, keepdims=True)
    return (values * lax.rsqrt(mean_sq + eps) * gain_col).astype(bf16)


def project(weight, normed):
    return jnp.dot(weight, normed, preferred_element_type=f32)


def contract(a, b, dim):
    return lax.dot_general(a, b, (((dim,), (dim,)), ((), ())), preferred_element_type=f32)


def spread(rows, first, count, height):
    return jnp.concatenate(
        [jnp.broadcast_to(rows[first + h : first + h + 1], (height, rows.shape[1])) for h in range(count)], axis=0
    )


def side_by_side(ref, first, count, rows=None):
    rows = ref.shape[1] if rows is None else rows
    return jnp.concatenate([ref[u][:rows] for u in range(first, first + count)], axis=1)


def span(u, count=1):
    return slice(u * SCAN_BLOCK, (u + count) * SCAN_BLOCK)


def padded(values, rows, lanes):
    if values.shape[1] < lanes:
        values = jnp.concatenate([values, jnp.zeros((values.shape[0], lanes - values.shape[1]), f32)], axis=1)
    if values.shape[0] < rows:
        values = jnp.concatenate([values, jnp.zeros((rows - values.shape[0], lanes), f32)], axis=0)
    return values


def turned(values):
    lanes = -(-values.shape[1] // LANES) * LANES
    return jnp.transpose(padded(values, -(-values.shape[0] // 8) * 8, lanes), (1, 0))


def columns(*rows):
    return turned(jnp.concatenate(rows, axis=0))


def columns_of(layer, rows_ref):
    return jnp.transpose(rows_ref[layer], (1, 0))


def tail_tile(tail_ref, model):
    if tail_ref.ndim == 2:
        return tail_ref[...]
    block = tail_ref[tail_ref.shape[0] - 1].astype(f32)
    rows = block[model:]
    kept = lax.broadcasted_iota(jnp.int32, rows.shape, 0) >= rows.shape[0] - 3
    rows = jnp.where(kept, rows, 0.0)
    tile = jnp.concatenate([jnp.zeros((SCAN_BLOCK - rows.shape[0], LANES), f32), rows], axis=0)
    return jnp.transpose(tile, (1, 0))[:model].astype(bf16)


def pack(running, running_log, heads):
    rows, lanes = running.shape
    width = lanes // (heads + 1)
    inner = heads * width
    kept = rows * heads // (heads + 1)
    high = rows - kept
    logs, blocks = [], []
    for h in range(heads):
        moved = pltpu.roll(running[kept:], inner - h * width, 1)
        log = pltpu.roll(running_log, inner - h * width, 1)
        lane = lax.broadcasted_iota(jnp.int32, moved.shape, 1)
        blocks.append(jnp.where(lane < inner, running[h * high : (h + 1) * high], moved))
        logs.append(jnp.where(lane[:1] < inner, running_log[:1], log[:1]))
    logs.append(jnp.zeros((8 - heads, lanes), f32))
    return jnp.concatenate(blocks + logs, axis=0)


def unpack(packed_state, heads):
    lanes = packed_state.shape[1]
    width = lanes // (heads + 1)
    inner = heads * width
    kept = packed_state.shape[0] - 8
    high = kept // heads
    lane = lax.broadcasted_iota(jnp.int32, (high, lanes), 1)
    last = jnp.zeros((high, lanes), f32)
    for h in range(heads):
        moved = pltpu.roll(packed_state[h * high : (h + 1) * high], (h * width - inner) % lanes, 1)
        last = jnp.where(lane // width == h, moved, last)
    return jnp.concatenate([packed_state[:kept], last], axis=0)


def swap_lanes(parts):
    count = len(parts)
    if count == 1:
        return parts
    width = LANES // count
    place = lax.broadcasted_iota(jnp.int32, parts[0].shape, 1) // width
    result = []
    for b in range(count):
        total = None
        for a, part in enumerate(parts):
            shift = (a - b) * width % LANES
            moved = pltpu.roll(part, shift, 1) if shift else part
            total = moved if total is None else jnp.where(place == a, moved, total)
        result.append(total)
    return result


def to_sequence(volume_ref, hid_ref, turn_ref, tile_ref):
    model, cells_x, cells_y = volume_ref.shape
    count = hid_ref.shape[0]
    per = LANES // cells_x
    for c in range(0, model, per):
        turn_ref[c // per] = jnp.transpose(volume_ref[c : c + per].astype(f32).reshape(LANES, cells_y), (1, 0))
    for c in range(0, model, per):
        parts = [turn_ref[c // per, pl.ds(a, count, stride=per), :] for a in range(per)]
        for j, part in enumerate(swap_lanes(parts)):
            tile_ref[pl.ds(c + j, count, stride=model), :] = part
    for u in range(count):
        hid_ref[u] = tile_ref[u * model : (u + 1) * model, :].astype(bf16)


def to_planes(tile_ref, out_ref, turn_ref, plane_ref, model, cells_x):
    rows = out_ref.shape[1]
    cells_y = out_ref.shape[2]
    per = LANES // cells_x
    count = cells_y // per
    for c in range(0, model, per):
        parts = [tile_ref[pl.ds(c + j, count, stride=model), :] for j in range(per)]
        for a, part in enumerate(swap_lanes(parts)):
            turn_ref[c // per, pl.ds(a, count, stride=per), :] = part
    for c in range(0, model, per):
        turn = jnp.transpose(turn_ref[c // per], (1, 0))
        for j in range(per):
            plane_ref[pl.ds(c + j, cells_x, stride=rows), :] = turn[j * cells_x : (j + 1) * cells_x]
    for x in range(cells_x + 1):
        plane_ref[x * rows + model : (x + 1) * rows, :] = jnp.zeros((rows - model, LANES), f32)
    for y in range(cells_y - 3, cells_y):
        block, a = divmod(y, per)
        turn = jnp.transpose(padded(tile_ref[block * model : (block + 1) * model, :], LANES, LANES), (1, 0))
        at = 2 * rows - cells_y + y
        plane_ref[pl.ds(at, cells_x, stride=rows), :] = turn[a * cells_x : (a + 1) * cells_x]
    for x in range(cells_x):
        out_ref[x] = plane_ref[x * rows : (x + 1) * rows, :].astype(bf16)


def convolve(proj_ref, rows, cols, first, outs):
    group = proj_ref.shape[1] // SCAN_BLOCK - 1
    tap_count = 4
    for r in range(0, rows, 16):
        conv_in = proj_ref[r : r + 16, :]
        half = 0.5 * cols[first + r : first + r + 16, :]
        total = None
        for offset in range(tap_count):
            lag = tap_count - 1 - offset
            shifted = pltpu.roll(conv_in, lag, 1) if lag else conv_in
            term = half[:, offset : offset + 1] * shifted[:, SCAN_BLOCK:]
            total = half[:, tap_count : tap_count + 1] + term if total is None else total + term
        conv_out = half_silu(total).astype(bf16)
        ref, at = next((ref, r - low) for ref, low, high in outs if low <= r < high)
        for u in range(group):
            ref[u, at : at + 16, :] = conv_out[:, span(u)]
    proj_ref[:, span(0)] = proj_ref[:, span(group)]


def state_kernel(
    layer, heads, from_volume, group, hid_ref, tail_ref, matrix_ref, rows_ref, inner_ref, write_ref, dec_ref,
    state_ref, total_ref, *rest
):
    if from_volume:
        volume_ref, hid_ref, proj_ref, carry_ref, turn_ref, tile_ref = (hid_ref,) + rest
        to_sequence(volume_ref, hid_ref, turn_ref, tile_ref)
    else:
        proj_ref, carry_ref = rest
    model = matrix_ref.shape[1]
    inner = inner_ref.shape[1]
    width = inner // heads
    state = write_ref.shape[1]
    rows = inner + state
    weight = jnp.transpose(matrix_ref[layer].astype(f32), (1, 0))
    dt_first = 2 * (inner + state)
    weight = jnp.concatenate([weight[inner : inner + rows], weight[dt_first : dt_first + 8]], axis=0).astype(bf16)
    cols = columns_of(layer, rows_ref)
    gain_col = cols[:model, 5:6]
    head_cols = cols[:8, 6:8]

    carry_ref[...] = jnp.zeros_like(carry_ref)
    proj_ref[:, span(0)] = rounded(project(weight, normalise(tail_tile(tail_ref, model), gain_col))[:rows])
    lane = lax.broadcasted_iota(jnp.int32, (1, LANES), 1)
    alls = (hid_ref, inner_ref, write_ref, dec_ref, state_ref)

    @pl.loop(0, inner_ref.shape[0] // group)
    def _(g):
        hid_ref, inner_ref, write_ref, dec_ref, state_ref = (r.at[pl.ds(g * group, group)] for r in alls)
        dt_raw = []
        for q in range(0, group, wide):
            projected = project(weight, normalise(side_by_side(hid_ref, q, wide, model), gain_col))
            proj_ref[:, span(q + 1, wide)] = rounded(projected[:rows])
            dt_raw.append(projected[rows:])
        step = jnp.concatenate(dt_raw, axis=1) + head_cols[:, 0:1]
        step = jnp.maximum(step, 0.0) + jnp.log1p(jnp.exp(-jnp.abs(step)))
        log_decay = head_cols[:, 1:2] * step
        step = jnp.concatenate([step[:, span(u)] for u in range(group)], axis=0)
        log_decay = jnp.concatenate([log_decay[:, span(u)] for u in range(group)], axis=0)
        high = log_decay.astype(bf16)
        rest = log_decay - high.astype(f32)
        middle = rest.astype(bf16)
        low = (rest - middle.astype(f32)).astype(bf16)
        square = (SCAN_BLOCK, SCAN_BLOCK)
        earlier = lax.broadcasted_iota(jnp.int32, square, 0) <= lax.broadcasted_iota(jnp.int32, square, 1)
        tri = jnp.where(earlier, 1.0, 0.0).astype(bf16)
        cum = project(low, tri) + project(middle, tri) + project(high, tri)
        last = jnp.broadcast_to(cum[:, SCAN_BLOCK - 1 :], cum.shape)
        carry_weight = jnp.exp(last - cum) * step
        for u in range(group):
            dec_ref[u, 0:8, :] = cum[8 * u : 8 * u + 8]
            dec_ref[u, 8:16, :] = step[8 * u : 8 * u + 8]
        convolve(proj_ref, rows, cols, 0, [(inner_ref, 0, inner), (write_ref, inner, rows)])
        decay_rows, block_states = [], []
        for u in range(group):
            row = last[8 * u + heads - 1 : 8 * u + heads]
            for h in range(heads - 2, -1, -1):
                row = jnp.where(lane < (h + 1) * width, last[8 * u + h : 8 * u + h + 1], row)
            decay_rows.append(row)
            scaled = inner_ref[u].astype(f32) * spread(carry_weight, 8 * u, heads, width)
            scaled = jnp.concatenate([scaled.astype(bf16), jnp.zeros((LANES - inner, SCAN_BLOCK), bf16)], axis=0)
            block_states.append(contract(write_ref[u], scaled, 1))
        running = carry_ref[0:state, :]
        running_log = carry_ref[state:, :]
        for u in range(group):
            state_ref[u, 0:state, :] = running
            state_ref[u, state:, :] = running_log
            running = jnp.exp(decay_rows[u]) * running + block_states[u]
            running_log = running_log + decay_rows[u]
        carry_ref[0:state, :] = running
        carry_ref[state:, :] = running_log

    total_ref[...] = pack(carry_ref[0:state, :], carry_ref[state:, :], heads)


def local_kernel(
    layer, heads, first, count, group, hid_ref, tail_ref, matrix_ref, rows_ref, inner_ref, write_ref, dec_ref, *rest
):
    local_ref, gate_ref, read_ref, proj_ref, score_ref, weights_ref = rest[-6:]
    model = matrix_ref.shape[1]
    inner = inner_ref.shape[1]
    width = inner // heads
    state = read_ref.shape[1]
    weight = jnp.transpose(matrix_ref[layer].astype(f32), (1, 0))
    weight = jnp.concatenate([weight[:inner], weight[2 * inner + state : 2 * (inner + state)]], axis=0).astype(bf16)
    cols = columns_of(layer, rows_ref)
    gain_col = cols[:model, 5:6]
    skip_cols = cols[:8, 8:9]

    before = hid_ref[first - 1][:model] if first else tail_tile(tail_ref, model)
    proj_ref[:, span(0)] = rounded(project(weight[inner:], normalise(before, gain_col)))
    source = lax.broadcasted_iota(jnp.int32, (SCAN_BLOCK, SCAN_BLOCK), 0)
    target = lax.broadcasted_iota(jnp.int32, (SCAN_BLOCK, SCAN_BLOCK), 1)
    causal = source <= target
    log2e = 1.4426950408889634
    alls = (hid_ref, inner_ref, write_ref, dec_ref, local_ref, gate_ref, read_ref)

    @pl.loop(0, count // group)
    def _(g):
        hid_ref, inner_ref, write_ref, dec_ref, local_ref, gate_ref, read_ref = (
            r.at[pl.ds(first + g * group, group)] for r in alls
        )
        for q in range(0, group, wide):
            projected = rounded(project(weight, normalise(side_by_side(hid_ref, q, wide, model), gain_col)))
            proj_ref[:, span(q + 1, wide)] = projected[inner:]
            gate = half_silu(0.5 * projected[:inner])
            for u in range(wide):
                gate_ref[q + u] = gate[:, span(u)]
        convolve(proj_ref, state, cols, inner + state, [(read_ref, 0, state)])
        cum = jnp.concatenate([dec_ref[u, 0:8, :] for u in range(group)], axis=0)
        step = jnp.concatenate([dec_ref[u, 8:16, :] for u in range(group)], axis=0)
        source_cols = (cum - jnp.log(step)) * log2e
        if 8 * group < SCAN_BLOCK:
            unused = jnp.zeros((SCAN_BLOCK - 8 * group, SCAN_BLOCK), f32)
            source_cols = jnp.concatenate([source_cols, unused], axis=0)
        source_cols = jnp.transpose(source_cols, (1, 0))
        cum = cum * log2e
        for u in range(group):
            score_ref[u] = contract(write_ref[u], read_ref[u], 0)
        for u in range(group):
            scores = score_ref[u]
            for h in range(heads):
                at = 8 * u + h
                gap = jnp.where(causal, cum[at : at + 1] - source_cols[:, at : at + 1], -jnp.inf)
                weights_ref[u, h] = (scores * jnp.exp2(gap)).astype(bf16)
        for u in range(group):
            for h in range(heads):
                values = inner_ref[u, h * width : (h + 1) * width, :]
                local_ref[u, h * width : (h + 1) * width, :] = (
                    project(values, weights_ref[u, h]) + skip_cols[h : h + 1, 0:1] * values.astype(f32)
                )


def finished(q, layer, heads, enter, refs, out_gain, out_proj):
    hid_ref, local_ref, gate_ref, read_ref, dec_ref, state_ref = refs
    inner = local_ref.shape[1]
    width = inner // heads
    state = read_ref.shape[1]
    inter = []
    for u in range(q, q + wide):
        entering = jnp.exp(state_ref[u, state : state + 1, :]) * enter + state_ref[u, 0:state, :]
        inter.append(contract(entering.astype(bf16), read_ref[u], 0)[:inner])
    decay = jnp.exp(jnp.concatenate([dec_ref[u, 0:8, :] for u in range(q, q + wide)], axis=1))
    scan_out = side_by_side(local_ref, q, wide) + spread(decay, 0, heads, width) * jnp.concatenate(inter, axis=1)
    gated = scan_out * side_by_side(gate_ref, q, wide)
    mean_sq = jnp.mean(gated * gated, axis=0, keepdims=True)
    gated = (gated * lax.rsqrt(mean_sq + eps) * out_gain).astype(bf16)
    hidden = side_by_side(hid_ref, q, wide, out_proj.shape[0]).astype(f32)
    return (hidden + project(out_proj, gated)).astype(bf16)


def finish_kernel(
    layer, heads, cells_x, group, enter_ref, hid_ref, local_ref, gate_ref, read_ref, dec_ref, state_ref, matrix_ref,
    rows_ref, out_ref, tile_ref, turn_ref, plane_ref,
):
    model = matrix_ref.shape[1]
    inner = local_ref.shape[1]
    alls = (hid_ref, local_ref, gate_ref, read_ref, dec_ref, state_ref)
    enter = unpack(enter_ref[...], heads)
    out_gain = columns_of(layer, rows_ref)[:inner, 9:10]
    out_proj = matrix_ref[layer][:, -LANES:][:, :inner]

    @pl.loop(0, hid_ref.shape[0] // group)
    def _(g):
        refs = tuple(r.at[pl.ds(g * group, group)] for r in alls)
        for q in range(0, group, wide):
            result = finished(q, layer, heads, enter, refs, out_gain, out_proj).astype(f32)
            for u in range(wide):
                at = pl.multiple_of((g * group + q + u) * model, 8)
                tile_ref[pl.ds(at, model), :] = result[:, span(u)]

    to_planes(tile_ref, out_ref, turn_ref, plane_ref, model, cells_x)


def head_kernel(
    layer, heads, group, enter_ref, hid_ref, local_ref, gate_ref, read_ref, dec_ref, state_ref, matrix_ref, rows_ref,
    head_ref, bias_ref, labels_ref, distance_ref, features_ref, grad_ref, loss_ref, feature_scr, logit_scr, sum_scr,
):
    classes = distance_ref.shape[0]
    inner = local_ref.shape[1]
    alls = (hid_ref, local_ref, gate_ref, read_ref, dec_ref, state_ref)
    enter = unpack(enter_ref[...], heads)
    out_gain = columns_of(layer, rows_ref)[:inner, 9:10]
    out_proj = matrix_ref[layer][:, -LANES:][:, :inner]
    bias = columns(bias_ref[...])[:classes, 0:1]
    sum_scr[...] = jnp.zeros_like(sum_scr)

    @pl.loop(0, hid_ref.shape[0] // group)
    def _(g):
        refs = tuple(r.at[pl.ds(g * group, group)] for r in alls)
        here = pl.ds(pl.multiple_of(g * group, group), group)
        for q in range(0, group, wide):
            result = finished(q, layer, heads, enter, refs, out_gain, out_proj)
            logits = project(head_ref[...], result) + bias
            result = result.astype(f32)
            for u in range(wide):
                feature_scr[pl.ds(q + u, result.shape[0], stride=group), :] = result[:, span(u)]
                logit_scr[pl.ds(q + u, classes, stride=group), :] = logits[:, span(u)]
        features = feature_scr[...].reshape(-1, group, SCAN_BLOCK)
        features_ref[:, here, :] = features.astype(bf16)
        logits = logit_scr[...].reshape(-1, group, SCAN_BLOCK)
        labels = labels_ref[here, :]
        peak = jnp.max(logits, axis=0)
        shifted = jnp.exp(logits - peak[None])
        partition = jnp.sum(shifted, axis=0)
        probability = shifted / partition[None]
        distance_map = distance_ref[:, here, :].astype(f32) * (1.0 / dist_unit)
        weighted = probability * distance_map
        expect = jnp.sum(weighted, axis=0)
        hot = labels[None] == lax.broadcasted_iota(jnp.int32, logits.shape, 0)
        chosen = jnp.sum(jnp.where(hot, logits, 0.0), axis=0)
        loss = peak + jnp.log(partition) - chosen + expect
        grad_ref[:, here, :] = probability - jnp.where(hot, 1.0, 0.0) + weighted - probability * expect[None]
        sum_scr[...] += jnp.sum(loss, axis=0, keepdims=True)

    loss_ref[...] = jnp.broadcast_to(sum_scr[...], loss_ref.shape)


def params(size=vmem_bytes):
    return pltpu.CompilerParams(vmem_limit_bytes=size)


vmem = pl.BlockSpec(memory_space=pltpu.VMEM)


def from_before(value):
    size = lax.axis_size(axes)
    value = jnp.where(lax.axis_index(axes) == size - 1, jnp.zeros_like(value), value)
    return lax.ppermute(value, axes, [(i, (i + 1) % size) for i in range(size)])


def join_kernel(heads, reach, me_ref, before_ref, *refs):
    members, before_out, total_out = refs[:-2], refs[-2], refs[-1]
    radix = len(members)
    digit = (me_ref[0] & (radix * reach - 1)) // reach
    rows = before_ref.shape[0] - 8
    third = rows // heads

    def combine(earlier, latter):
        log = latter[rows:]
        grow = jnp.exp(log)
        blocks = [
            grow[h : h + 1] * earlier[h * third : (h + 1) * third] + latter[h * third : (h + 1) * third]
            for h in range(heads)
        ]
        return jnp.concatenate(blocks + [earlier[rows:] + log], axis=0)

    values = [ref[...] for ref in members]
    before = before_ref[...]
    ahead, total = None, None
    for place in range(radix):
        value = values[0]
        for k in range(1, radix):
            value = jnp.where(digit ^ k == place, values[k], value)
        total = value if total is None else combine(total, value)
        if place < radix - 1:
            ahead = jnp.where(place < digit, total, jnp.zeros_like(total) if ahead is None else ahead)
    before_out[...] = combine(ahead, before)
    total_out[...] = total


def prefix_state(me, total, held, pieces, heads):
    size = lax.axis_size(axes)
    rounds = [(1, 2)]
    while rounds[-1][0] * rounds[-1][1] < size:
        reach = rounds[-1][0] * rounds[-1][1]
        rounds.append((reach, 4 if 4 * reach <= size else 2))
    before = jnp.zeros_like(total)
    done = None
    for i, (reach, radix) in enumerate(rounds):
        piece = i - (len(rounds) - len(pieces))
        if piece >= 0:
            total, held = lax.optimization_barrier((total, held))
            done = pieces[piece](held, done)
        others = [
            lax.ppermute(total, axes, [(k, k ^ (step * reach | 1)) for k in range(size)]) for step in range(1, radix)
        ]
        if piece >= 0:
            others, done = lax.optimization_barrier((others, done))
        before, total = pl.pallas_call(
            functools.partial(join_kernel, heads, reach),
            in_specs=[pl.BlockSpec(memory_space=pltpu.SMEM)] + [vmem] * (1 + radix),
            out_specs=[vmem] * 2,
            out_shape=[jax.ShapeDtypeStruct(total.shape, f32)] * 2,
            compiler_params=params(2 * 1024 * 1024),
            name="join",
        )(me, before, total, *others)
    return before, done


def tile(count, rows, kind):
    return jax.ShapeDtypeStruct((count, rows, SCAN_BLOCK), kind)


def call_states(layer, hidden, tail, weights):
    from_volume = tail.ndim == 2
    inner, heads, state, model = (weights[k] for k in ("inner", "heads", "state", "model"))
    count = hidden.shape[1] * hidden.shape[2] // SCAN_BLOCK if from_volume else hidden.shape[0]
    group = min(16, count)
    out_shape = [
        tile(count, inner, bf16),
        tile(count, state, bf16),
        tile(count, 16, f32),
        tile(count, state + 8, f32),
        jax.ShapeDtypeStruct((state * inner // LANES + 8, LANES), f32),
    ]
    scratch = [
        pltpu.VMEM((inner + state, (group + 1) * SCAN_BLOCK), f32),
        pltpu.VMEM((state + 8, LANES), f32),
    ]
    if from_volume:
        out_shape.append(tile(count, model, bf16))
        per = LANES // hidden.shape[1]
        scratch.append(pltpu.VMEM((model // per, hidden.shape[2], LANES), f32))
        scratch.append(pltpu.VMEM((count * model, LANES), f32))
    return pl.pallas_call(
        functools.partial(state_kernel, layer, heads, from_volume, group),
        in_specs=[vmem] * 4,
        out_specs=[vmem] * len(out_shape),
        out_shape=out_shape,
        scratch_shapes=scratch,
        compiler_params=params(),
        name="states",
    )(hidden, tail, weights["matrices"], weights["rows"])


def call_local(layer, first, count, held, done, weights):
    hidden, tail, inner_values, write, dec = held
    total = hidden.shape[0]
    inner, heads, state = weights["inner"], weights["heads"], weights["state"]
    group = min(8, count)
    taken = [] if done is None else list(done)
    return pl.pallas_call(
        functools.partial(local_kernel, layer, heads, first, count, group),
        in_specs=[vmem] * (7 + len(taken)),
        out_specs=[vmem] * 3,
        out_shape=[tile(total, inner, f32), tile(total, inner, f32), tile(total, state, bf16)],
        input_output_aliases={7 + i: i for i in range(len(taken))},
        scratch_shapes=[
            pltpu.VMEM((state, (group + 1) * SCAN_BLOCK), f32),
            pltpu.VMEM((group, SCAN_BLOCK, SCAN_BLOCK), f32),
            pltpu.VMEM((group, heads, SCAN_BLOCK, SCAN_BLOCK), bf16),
        ],
        compiler_params=params(),
        name="local",
    )(hidden, tail, weights["matrices"], weights["rows"], inner_values, write, dec, *taken)


def layer_start(layer, me, hidden, tail, weights):
    inner_values, write, dec, states, total, *sequence = call_states(layer, hidden, tail, weights)
    if sequence:
        (hidden,) = sequence
    else:
        tail = hidden
    cut = hidden.shape[0] // 2
    pieces = [
        lambda held, done, first=first: call_local(layer, first, cut, held, done, weights)
        for first in range(0, hidden.shape[0], cut)
    ]
    enter, done = prefix_state(me, total, (hidden, tail, inner_values, write, dec), pieces, weights["heads"])
    return (enter, hidden, *done, dec, states, weights["matrices"], weights["rows"])


def call_finish(cells, parts, weights):
    count, model, _ = parts[1].shape
    model = weights["model"]
    cells_x, cells_y = cells
    rows = model + 8
    per = LANES // cells_x
    return pl.pallas_call(
        functools.partial(finish_kernel, 0, weights["heads"], cells_x, min(16, count)),
        in_specs=[vmem] * len(parts),
        out_specs=vmem,
        out_shape=jax.ShapeDtypeStruct((cells_x, rows, cells_y), bf16),
        scratch_shapes=[
            pltpu.VMEM((count * model, LANES), f32),
            pltpu.VMEM((model // per, cells_y, LANES), f32),
            pltpu.VMEM(((cells_x + 1) * rows, LANES), f32),
        ],
        compiler_params=params(),
        name="finish",
    )(*parts)


def call_heads(size, parts, weights, head_weight, head_bias, labels, distance):
    classes, model = head_weight.shape
    count = parts[1].shape[0]
    group = min(16, count)
    return pl.pallas_call(
        functools.partial(head_kernel, 1, weights["heads"], group),
        in_specs=[vmem] * (len(parts) + 4),
        out_specs=[vmem] * 3,
        out_shape=[
            jax.ShapeDtypeStruct((model, count, SCAN_BLOCK), bf16),
            jax.ShapeDtypeStruct((classes, count, SCAN_BLOCK), f32),
            jax.ShapeDtypeStruct((size, SCAN_BLOCK), f32),
        ],
        scratch_shapes=[
            pltpu.VMEM((model * group, SCAN_BLOCK), f32),
            pltpu.VMEM((classes * group, SCAN_BLOCK), f32),
            pltpu.VMEM((1, SCAN_BLOCK), f32),
        ],
        compiler_params=params(),
        name="heads",
    )(*parts, head_weight, head_bias, labels, distance)


def packed(norm_gain, in_proj, dt_proj, dt_bias, decay_rate, conv_weight, conv_bias, skip_gain, out_gain, out_proj):
    lanes = lambda value, width: jnp.pad(value, ((0, 0),) * (value.ndim - 1) + ((0, width - value.shape[-1]),))
    first = jnp.concatenate([in_proj, dt_proj], axis=1)
    width = -(-(first.shape[1] + 8) // LANES) * LANES
    second = out_proj.shape[2]
    matrices = jnp.concatenate(
        [lanes(jnp.swapaxes(first, 1, 2), width), lanes(out_proj, -(-second // LANES) * LANES)], axis=2
    )
    width = -(-conv_bias.shape[1] // LANES) * LANES
    vectors = [conv_bias, norm_gain, dt_bias, -decay_rate, skip_gain, out_gain]
    rows = [lanes(jnp.swapaxes(conv_weight, 1, 2), width)] + [lanes(v, width)[:, None] for v in vectors]
    count = sum(r.shape[1] for r in rows)
    rows.append(jnp.zeros((rows[0].shape[0], -(-count // 8) * 8 - count, width), f32))
    return matrices, jnp.concatenate(rows, axis=1)


def per_device(
    volume, norm_gain, in_proj, dt_proj, dt_bias, decay_rate, conv_weight, conv_bias, skip_gain, out_gain,
    out_proj, head_weight, head_bias, labels, distance,
):
    size = lax.axis_size(axes)
    model, _, cells_y, cells_x = volume.shape
    classes = head_weight.shape[0]
    inner = out_proj.shape[2]
    heads = decay_rate.shape[1]
    weights = dict(heads=heads, inner=inner, state=(in_proj.shape[1] - 2 * inner) // 2, model=model)
    weights["matrices"], weights["rows"] = packed(
        norm_gain, in_proj, dt_proj, dt_bias, decay_rate, conv_weight, conv_bias, skip_gain, out_gain, out_proj
    )
    tail = from_before(jnp.pad(volume[:, 0, cells_y - 1, :], ((0, 0), (SCAN_BLOCK - cells_x, 0))))
    tail, me = lax.optimization_barrier((tail, lax.axis_index(axes).astype(jnp.int32).reshape(1)))
    plane = jnp.swapaxes(volume[:, 0], 1, 2)
    parts = layer_start(0, me, plane, tail, weights)
    planes = call_finish((cells_x, cells_y), parts, weights)
    hidden = lax.all_to_all(planes, axes, split_axis=0, concat_axis=0, tiled=True)
    count = hidden.shape[0]
    parts = layer_start(1, me, hidden, hidden, weights)
    features, grad, loss = call_heads(
        size, parts, weights, head_weight, head_bias[None, :], labels.reshape(count, SCAN_BLOCK),
        distance.reshape(classes, count, SCAN_BLOCK),
    )
    shared = lax.all_to_all(loss, axes, 0, 0, tiled=True)
    voxel_weight = 1.0 + 3.0 * jnp.arange(size, dtype=f32) / (size - 1.0)
    total_loss = jnp.sum(voxel_weight[:, None] * shared) / (2.5 * count * SCAN_BLOCK * size)
    return (
        features.reshape(model, 1, count, SCAN_BLOCK),
        grad.reshape(classes, 1, count, SCAN_BLOCK),
        total_loss,
    )


def solution(mesh):
    plane = P(None, axes, None, None)
    return jax.shard_map(
        per_device,
        mesh=mesh,
        in_specs=(plane,) + (P(),) * 12 + (P(axes, None, None), plane),
        out_specs=(plane, plane, P()),
        check_vma=False,
    )
```

time: 101 us -> 86.6 us (0.86)
  waiting for transfers between devices: 25.3 us -> 14.6 us
  Pallas kernels: 36.4 us -> 28.3 us
  starting transfers between devices: 10.9 us -> 18.5 us
  local copies, waits for them, and re-layouts: 5.86 us -> 2.58 us
    ppermute x4 -> x14, starting transfers between devices: 0.01 us -> 14.4 us  [prefix_state(): lax.ppermute(total, axes, [(k, k ^ (step * reach | 1)) for k in range(siz...]
    all_to_all x2 -> x0, waiting for transfers between devices: 8.9 us -> none  [prefix_state(): lax.all_to_all(offer, axes, 0, 0, tiled=True, axis_index_groups=groups)]
    pallas_call x10 -> x14, Pallas kernels: 36.4 us -> 28.3 us  [the longest x4 11.8 us: call_local(): pl.pallas_call(functools.partial(local_kernel, layer, heads, first, count...]
    all_to_all x2 -> x0, starting transfers between devices: 7.66 us -> none  [prefix_state(): lax.all_to_all(offer, axes, 0, 0, tiled=True, axis_index_groups=groups)]
    unnamed x50 -> x26, local copies, waits for them, and re-layouts: 4.49 us -> 1.21 us
    ppermute x4 -> x14, waiting for transfers between devices: 4.77 us -> 2.98 us  [prefix_state(): lax.ppermute(total, axes, [(k, k ^ (step * reach | 1)) for k in range(siz...]
  transfers between devices with their start and end apart: 8 -> 16, of which waited for: 8 -> 5; matrix products, arithmetic and copies ran while one was open for 3% -> 3% of each run, Pallas kernels for 12% -> 14%
where the time goes in v2:
time: 86.6 us; the launch traced here: 86.3 us
  Pallas kernels  28.3 us (33%)
  starting transfers between devices  18.5 us (21%)
  blocking collectives  17 us (20%)
  waiting for transfers between devices  14.6 us (17%)
  between operations  2.81 us (3%)
  local copies, waits for them, and re-layouts  2.58 us (3%)
  other arithmetic  2.48 us (3%)
    all_to_all x1, blocking collectives, per_device(): lax.all_to_all(planes, axes, split_axis=0, concat_axis=0, tiled=True)  17 us
    ppermute x14, starting transfers between devices, prefix_state(): lax.ppermute(total, axes, [(k, k ^ (step * reach | 1)) for k in range(siz...  14.4 us
    pallas_call x4, Pallas kernels, call_local(): pl.pallas_call(functools.partial(local_kernel, layer, heads, first, count...  11.8 us
    pallas_call x2, Pallas kernels, call_states(): pl.pallas_call(functools.partial(state_kernel, layer, heads, from_volume,...  7.79 us
    all_to_all x1, waiting for transfers between devices, per_device(): shared = lax.all_to_all(loss, axes, 0, 0, tiled=True)  7.14 us
    ppermute x1, waiting for transfers between devices, from_before(): return lax.ppermute(value, axes, [(i, (i + 1) % size) for i in range(size)])  4.48 us
    pallas_call x1, Pallas kernels, call_heads(): pl.pallas_call(functools.partial(head_kernel, 1, weights['heads'], group)...  4.16 us
    all_to_all x1, starting transfers between devices, per_device(): shared = lax.all_to_all(loss, axes, 0, 0, tiled=True)  3.6 us
  transfers between devices with their start and end apart: 16, of which 5 were waited for; matrix products, arithmetic and copies ran while one was open for 3% of the time, Pallas kernels for 14%

profile of v2, /device:TPU:0, one launch (start us, length us, event | category | flops | bytes accessed | tf_op | source)
XLA Modules:
  0.0 86.3 jit_solution(14603410315311142476)
XLA Ops:
  0.7 1.3 %slice.3 = bf16[48,1,1,32]{2,3,1,0:T(8,128)(2,1)S(1)} slice(bf16[48,1,128,32]{2,3,1,0:T(8,128)(2,1)} %param.15), slice={[0:48], [0:1], [127:128], [0:32]} | slice | bytes 6144 | tf_op jit(solution)/shard_map/slice | solution.py:631
  2.4 0.5 collective-permute-start
  2.9 0.8 copy.29
  3.7 1.0 %maximum_bitcast_fusion = bf16[2,48,323]{2,1,0:T(8,128)(2,1)S(1)} fusion(bf16[2,3,48]{1,2,0:T(8,128)(2,1)S(1)} %copy.29, bf16[2,320,48]{1,2,0:T(8,128)(2,1)} %param.17), kind=kLoop, calls=%fused_computation.5 | loop fusion | flops 124032 | bytes 124032 | tf_op jit(solution)/shard_map/transpose | solution.py:608
  4.6 0.8 fusion.2.matrix_ref
  5.7 4.5 %collective-permute-done.tail_ref = bf16[48,128]{1,0:T(8,128)(2,1)S(1)} collective-permute-done((bf16[48,128]{1,0:T(8,128)(2,1)S(1)}, bf16[48,128]{1,0:T(8,128)(2,1)S(1)}, u32[]{:S(2)}, u32[]{:S(2)}) %collective-permute-start) | collective-permute-done | bytes 12320 | tf_op jit(solution)/shard_map/ppermute | solution.py:423
  10.2 4.1 %states.2 = (bf16[32,96,128]{2,1,0:T(8,128)(2,1)S(1)}, bf16[32,64,128]{2,1,0:T(8,128)(2,1)S(1)}, f32[32,16,128]{2,1,0:T(8,128)S(1)}, f32[32,72,128]{2,1,0:T(8,12...) custom-call(bf16[48,32,128]{2,1,0:T(8,128)(2,1)S(1)} %bitcast.21, ...), custom_call_target="tpu_custom_call" | custom-call | tf_op jit(solution)/shard_map/states/pallas_call | solution.py:510
  14.3 1.2 %collective-permute-done.1.refs_1_ = f32[56,128]{1,0:T(8,128)S(1)} collective-permute-done((f32[56,128]{1,0:T(8,128)S(1)}, f32[56,128]{1,0:T(8,128)S(1)}, u32[]{:S(2)}, u32[]{:S(2)}) %collective-permute-start.1) | collective-permute-done | bytes 28704 | tf_op jit(solution)/shard_map/ppermute | solution.py:470
  15.6 0.5 collective-permute-start.3
  16.1 2.5 %collective-permute-start.4 = (f32[56,128]{1,0:T(8,128)S(1)}, f32[56,128]{1,0:T(8,128)S(1)}, u32[]{:S(2)}, u32[]{:S(2)}) collective-permute-start(f32[56,128]{1,0:T(8,128)S(1)} %get-tuple-element.98.refs_0_), channel_id=1, source_target_pairs={{0,7},{1,6},{2,5},{3,4},{4,3},{5,2},{6,1},{7,0},{8,15},{9,14},{10,... | collective-permute-start | bytes 86024 | tf_op jit(solution)/shard_map/ppermute | solution.py:470
  18.6 3.0 %local.4 = (f32[32,96,128]{2,1,0:T(8,128)S(1)}, f32[32,96,128]{2,1,0:T(8,128)S(1)}, bf16[32,64,128]{2,1,0:T(8,128)(2,1)S(1)}) custom-call(bf16[32,48,128]{2,1,0:T(8,128)(2,1)S(1)} %get-tuple-element.113.hid_ref, bf16[48,128]{1,0:T(8,128)(2,1)S(1)} %collective-permute-done.tail_ref, bf16[2,48,512]{2,1,0:T(8,128)(2,1)S(1)} %fusion.2.matrix_ref, ...), custom_call_target="tpu_custom_call" | custom-call | tf_op jit(solution)/shard_map/local/pallas_call | solution.py:527
  21.9 2.2 %collective-permute-start.6 = (f32[56,128]{1,0:T(8,128)S(1)}, f32[56,128]{1,0:T(8,128)S(1)}, u32[]{:S(2)}, u32[]{:S(2)}) collective-permute-start(f32[56,128]{1,0:T(8,128)S(1)} %get-tuple-element.112.refs_0_), channel_id=1, source_target_pairs={{0,17},{1,16},{2,19},{3,18},{4,21},{5,20},{6,23},{7,22},{8,25},{9,... | collective-permute-start | bytes 86024 | tf_op jit(solution)/shard_map/ppermute | solution.py:470
  24.2 1.6 %collective-permute-start.7 = (f32[56,128]{1,0:T(8,128)S(1)}, f32[56,128]{1,0:T(8,128)S(1)}, u32[]{:S(2)}, u32[]{:S(2)}) collective-permute-start(f32[56,128]{1,0:T(8,128)S(1)} %get-tuple-element.112.refs_0_), channel_id=1, source_target_pairs={{0,25},{1,24},{2,27},{3,26},{4,29},{5,28},{6,31},{7,30},{8,17},{9,... | collective-permute-start | bytes 86024 | tf_op jit(solution)/shard_map/ppermute | solution.py:470
  25.7 3.0 %local.5 = (f32[32,96,128]{2,1,0:T(8,128)S(1)}, f32[32,96,128]{2,1,0:T(8,128)S(1)}, bf16[32,64,128]{2,1,0:T(8,128)(2,1)S(1)}) custom-call(bf16[32,48,128]{2,1,0:T(8,128)(2,1)S(1)} %get-tuple-element.113.hid_ref, bf16[48,128]{1,0:T(8,128)(2,1)S(1)} %collective-permute-done.tail_ref, ...), custom_call_target="tpu_custom_call", output_to_operand_aliasing={{0}: (7, {}), {1}: (8, {}), {2}: (9, {})} | custom-call | tf_op jit(solution)/shard_map/local/pallas_call | solution.py:527
  28.7 0.6 collective-permute-done.7.refs_3_
  29.3 0.6 join.8
  29.9 3.1 %finish.1 = bf16[32,56,128]{2,1,0:T(8,128)(2,1)S(1)} custom-call(f32[56,128]{1,0:T(8,128)S(1)} %get-tuple-element.127.enter_ref, bf16[32,48,128]{2,1,0:T(8,128)(2,1)S(1)} %get-tuple-element.113.hid_ref, f32[32,96,128]{2,1,0:T(8,128)S(1)} %get-tuple-element.128.local_ref, f32[32,96,128]{2,1,0:T(8,128)S(1)} %get-tuple-element.129.gate_ref, ...), custom_call_target="tpu_custom_call" | custom-call | tf_op jit(solution)/shard_map/finish/pallas_call | solution.py:564
  33.0 17.0 %all_to_all.17.hid_ref.tail_ref = bf16[32,56,128]{2,1,0:T(8,128)(2,1)S(1)} all-to-all(bf16[32,56,128]{2,1,0:T(8,128)(2,1)S(1)} %finish.1), channel_id=1, replica_groups=mesh['row'=8,'col'=4] {'row','col'}, dimensions={0} | all-to-all | bytes 917504 | tf_op jit(solution)/shard_map/all_to_all | solution.py:636
  50.0 3.7 %states.3 = (bf16[32,96,128]{2,1,0:T(8,128)(2,1)S(1)}, bf16[32,64,128]{2,1,0:T(8,128)(2,1)S(1)}, f32[32,16,128]{2,1,0:T(8,128)S(1)}, f32[32,72,128]{2,1,0:T(8,128)S(1)}, f32[56,128]{1,0:T(8,128)S(1)}) custom-call(bf16[32,56,128]{2,1,0:T(8,128)(2,1)S(1)} %all_to_all.17.hid_ref.tail_ref, bf16[32,56,128]{2,1,0:T(8,128)(2,1)S(1)} %all_to_all.17.hid_ref.tail_ref, ...), custom_call_target="tpu_custom_call" | custom-call | tf_op jit(solution)/shard_map/states/pallas_call | solution.py:510
  53.8 1.2 %collective-permute-done.8.refs_1_ = f32[56,128]{1,0:T(8,128)S(1)} collective-permute-done((f32[56,128]{1,0:T(8,128)S(1)}, f32[56,128]{1,0:T(8,128)S(1)}, u32[]{:S(2)}, u32[]{:S(2)}) %collective-permute-start.8) | collective-permute-done | bytes 28704 | tf_op jit(solution)/shard_map/ppermute | solution.py:470
  55.0 1.0 %collective-permute-start.10 = (f32[56,128]{1,0:T(8,128)S(1)}, f32[56,128]{1,0:T(8,128)S(1)}, u32[]{:S(2)}, u32[]{:S(2)}) collective-permute-start(f32[56,128]{1,0:T(8,128)S(1)} %get-tuple-element.138.refs_0_), channel_id=1, source_target_pairs={{0,5},{1,4},{2,7},{3,6},{4,1},{5,0},{6,3},{7,2},{8,13},{9,12},{10,... | collective-permute-start | bytes 86024 | tf_op jit(solution)/shard_map/ppermute | solution.py:470
  56.0 1.1 %collective-permute-start.11 = (f32[56,128]{1,0:T(8,128)S(1)}, f32[56,128]{1,0:T(8,128)S(1)}, u32[]{:S(2)}, u32[]{:S(2)}) collective-permute-start(f32[56,128]{1,0:T(8,128)S(1)} %get-tuple-element.138.refs_0_), channel_id=1, source_target_pairs={{0,7},{1,6},{2,5},{3,4},{4,3},{5,2},{6,1},{7,0},{8,15},{9,14},{10,... | collective-permute-start | bytes 86024 | tf_op jit(solution)/shard_map/ppermute | solution.py:470
  57.1 1.0 %collective-permute-start.9 = (f32[56,128]{1,0:T(8,128)S(1)}, f32[56,128]{1,0:T(8,128)S(1)}, u32[]{:S(2)}, u32[]{:S(2)}) collective-permute-start(f32[56,128]{1,0:T(8,128)S(1)} %get-tuple-element.138.refs_0_), channel_id=1, source_target_pairs={{0,3},{1,2},{2,1},{3,0},{4,7},{5,6},{6,5},{7,4},{8,11},{9,10},{10,... | collective-permute-start | bytes 86024 | tf_op jit(solution)/shard_map/ppermute | solution.py:470
  58.1 3.0 %local.6 = (f32[32,96,128]{2,1,0:T(8,128)S(1)}, f32[32,96,128]{2,1,0:T(8,128)S(1)}, bf16[32,64,128]{2,1,0:T(8,128)(2,1)S(1)}) custom-call(bf16[32,56,128]{2,1,0:T(8,128)(2,1)S(1)} %all_to_all.17.hid_ref.tail_ref, bf16[32,56,128]{2,1,0:T(8,128)(2,1)S(1)} %all_to_all.17.hid_ref.tail_ref, bf16[2,48,512]{2,1,0:T(8,128)(2,1)S(1)} %fusion.2.matrix_ref, ...), custom_call_target="tpu_custom_call" | custom-call | tf_op jit(solution)/shard_map/local/pallas_call | solution.py:527
  61.1 1.2 %collective-permute-start.12 = (f32[56,128]{1,0:T(8,128)S(1)}, f32[56,128]{1,0:T(8,128)S(1)}, u32[]{:S(2)}, u32[]{:S(2)}) collective-permute-start(f32[56,128]{1,0:T(8,128)S(1)} %get-tuple-element.152.refs_0_), channel_id=1, source_target_pairs={{0,9},{1,8},{2,11},{3,10},{4,13},{5,12},{6,15},{7,14},{8,1},{9,0},... | collective-permute-start | bytes 86024 | tf_op jit(solution)/shard_map/ppermute | solution.py:470
  62.6 2.7 %collective-permute-start.14 = (f32[56,128]{1,0:T(8,128)S(1)}, f32[56,128]{1,0:T(8,128)S(1)}, u32[]{:S(2)}, u32[]{:S(2)}) collective-permute-start(f32[56,128]{1,0:T(8,128)S(1)} %get-tuple-element.152.refs_0_), channel_id=1, source_target_pairs={{0,25},{1,24},{2,27},{3,26},{4,29},{5,28},{6,31},{7,30},{8,17},{9,... | collective-permute-start | bytes 86024 | tf_op jit(solution)/shard_map/ppermute | solution.py:470
  65.3 2.9 %local.7 = (f32[32,96,128]{2,1,0:T(8,128)S(1)}, f32[32,96,128]{2,1,0:T(8,128)S(1)}, bf16[32,64,128]{2,1,0:T(8,128)(2,1)S(1)}) custom-call(bf16[32,56,128]{2,1,0:T(8,128)(2,1)S(1)} %all_to_all.17.hid_ref.tail_ref, bf16[32,56,128]{2,1,0:T(8,128)(2,1)S(1)} %all_to_all.17.hid_ref.tail_ref, ...), custom_call_target="tpu_custom_call", output_to_operand_aliasing={{0}: (7, {}), {1}: (8, {}), {2}: (9, {})} | custom-call | tf_op jit(solution)/shard_map/local/pallas_call | solution.py:527
  68.2 0.6 join.11
  68.9 4.2 %heads.1 = (bf16[48,32,128]{2,1,0:T(8,128)(2,1)}, f32[14,32,128]{2,1,0:T(8,128)}, f32[32,128]{1,0:T(8,128)}) custom-call(f32[56,128]{1,0:T(8,128)S(1)} %get-tuple-element.167.enter_ref, bf16[32,56,128]{2,1,0:T(8,128)(2,1)S(1)} %all_to_all.17.hid_ref.tail_ref, f32[32,96,128]{2,1,0:T(8,128)S(1)} %get-tuple-element.168.local_ref, ...), custom_call_target="tpu_custom_call" | custom-call | tf_op jit(solution)/shard_map/heads/pallas_call | solution.py:583
  73.0 3.6 %all-to-all-start.1 = ((f32[32,1,128]{2,1,0:T(1,128)}), f32[32,1,128]{2,1,0:T(1,128)S(1)}, u32[]{:S(2)}, u32[]{:S(2)}) async-start(f32[32,1,128]{2,1,0:T(1,128)} %bitcast.14), calls=%async_computation.1 | async-start | bytes 32768 | tf_op jit(solution)/shard_map/all_to_all | solution.py:643
  76.7 7.1 %all-to-all-done.1 = f32[32,1,128]{2,1,0:T(1,128)S(1)} async-done(((f32[32,1,128]{2,1,0:T(1,128)}), f32[32,1,128]{2,1,0:T(1,128)S(1)}, u32[]{:S(2)}, u32[]{:S(2)}) %all-to-all-start.1) | async-done | bytes 16416 | tf_op jit(solution)/shard_map/all_to_all | solution.py:643
  83.8 0.7 multiply_reduce_fusion
  (64 shorter events, 1.6 us)
Async XLA Ops:
  0.6 9.5 %copy-start = (bf16[48,1,128,32]{2,3,1,0:T(8,128)(2,1)S(1)}, bf16[48,1,128,32]{2,3,1,0:T(8,128)(2,1)}, u32[]{:S(2)}) copy-start(bf16[48,1,128,32]{2,3,1,0:T(8,128)(2,1)} %param.15) | copy-start | bytes 1179652
  0.6 4.7 %copy-start.11 = (f32[2,3]{1,0:T(2,128)S(1)}, f32[2,3]{1,0:T(2,128)}, u32[]{:S(2)}) copy-start(f32[2,3]{1,0:T(2,128)} %param.20) | copy-start | bytes 76
  0.7 4.8 %copy-start.5 = (f32[2,224,4]{1,2,0:T(4,128)S(1)}, f32[2,224,4]{1,2,0:T(4,128)}, u32[]{:S(2)}) copy-start(f32[2,224,4]{1,2,0:T(4,128)} %param.21) | copy-start | bytes 21508
  0.7 4.8 %copy-start.6 = (f32[2,224]{1,0:T(2,128)S(1)}, f32[2,224]{1,0:T(2,128)}, u32[]{:S(2)}) copy-start(f32[2,224]{1,0:T(2,128)} %param.22) | copy-start | bytes 5380
  0.7 4.8 %copy-start.7 = (f32[2,48]{1,0:T(2,128)S(1)}, f32[2,48]{1,0:T(2,128)}, u32[]{:S(2)}) copy-start(f32[2,48]{1,0:T(2,128)} %param.16) | copy-start | bytes 1156
  0.7 4.8 %copy-start.8 = (f32[2,3]{1,0:T(2,128)S(1)}, f32[2,3]{1,0:T(2,128)}, u32[]{:S(2)}) copy-start(f32[2,3]{1,0:T(2,128)} %param.19) | copy-start | bytes 76
  0.7 4.9 %copy-start.9 = (f32[2,3]{1,0:T(2,128)S(1)}, f32[2,3]{1,0:T(2,128)}, u32[]{:S(2)}) copy-start(f32[2,3]{1,0:T(2,128)} %param.23) | copy-start | bytes 76
  0.7 4.9 %copy-start.10 = (f32[2,96]{1,0:T(2,128)S(1)}, f32[2,96]{1,0:T(2,128)}, u32[]{:S(2)}) copy-start(f32[2,96]{1,0:T(2,128)} %param.24) | copy-start | bytes 2308
  2.4 7.8 %collective-permute-start = (bf16[48,128]{1,0:T(8,128)(2,1)S(1)}, bf16[48,128]{1,0:T(8,128)(2,1)S(1)}, u32[]{:S(2)}, u32[]{:S(2)}) collective-permute-start(bf16[48,128]{1,0:T(8,128)(2,1)S(1)} %pad_select_fusion), channel_id=1, source_target_pairs={{0,1},{1,2},{2,3},{3,4},{4,5},{5,6},{6,7},{7,8},{8,9},{9,10},{10,1... | collective-permute-start | bytes 36872 | tf_op jit(solution)/shard_map/ppermute | solution.py:423
  14.2 1.2 %collective-permute-start.1 = (f32[56,128]{1,0:T(8,128)S(1)}, f32[56,128]{1,0:T(8,128)S(1)}, u32[]{:S(2)}, u32[]{:S(2)}) collective-permute-start(f32[56,128]{1,0:T(8,128)S(1)} %get-tuple-element.91.refs_0_), channel_id=1, source_target_pairs={{0,1},{1,0},{2,3},{3,2},{4,5},{5,4},{6,7},{7,6},{8,9},{9,8},{10,11... | collective-permute-start | bytes 86024 | tf_op jit(solution)/shard_map/ppermute | solution.py:470
  15.5 6.0 %collective-permute-start.2 = (f32[56,128]{1,0:T(8,128)S(1)}, f32[56,128]{1,0:T(8,128)S(1)}, u32[]{:S(2)}, u32[]{:S(2)}) collective-permute-start(f32[56,128]{1,0:T(8,128)S(1)} %get-tuple-element.98.refs_0_), channel_id=1, source_target_pairs={{0,3},{1,2},{2,1},{3,0},{4,7},{5,6},{6,5},{7,4},{8,11},{9,10},{10,... | collective-permute-start | bytes 86024 | tf_op jit(solution)/shard_map/ppermute | solution.py:470
  15.6 5.9 %collective-permute-start.3 = (f32[56,128]{1,0:T(8,128)S(1)}, f32[56,128]{1,0:T(8,128)S(1)}, u32[]{:S(2)}, u32[]{:S(2)}) collective-permute-start(f32[56,128]{1,0:T(8,128)S(1)} %get-tuple-element.98.refs_0_), channel_id=1, source_target_pairs={{0,5},{1,4},{2,7},{3,6},{4,1},{5,0},{6,3},{7,2},{8,13},{9,12},{10,... | collective-permute-start | bytes 86024 | tf_op jit(solution)/shard_map/ppermute | solution.py:470
  16.1 5.4 %collective-permute-start.4 = (f32[56,128]{1,0:T(8,128)S(1)}, f32[56,128]{1,0:T(8,128)S(1)}, u32[]{:S(2)}, u32[]{:S(2)}) collective-permute-start(f32[56,128]{1,0:T(8,128)S(1)} %get-tuple-element.98.refs_0_), channel_id=1, source_target_pairs={{0,7},{1,6},{2,5},{3,4},{4,3},{5,2},{6,1},{7,0},{8,15},{9,14},{10,... | collective-permute-start | bytes 86024 | tf_op jit(solution)/shard_map/ppermute | solution.py:470
  21.6 7.1 %collective-permute-start.5 = (f32[56,128]{1,0:T(8,128)S(1)}, f32[56,128]{1,0:T(8,128)S(1)}, u32[]{:S(2)}, u32[]{:S(2)}) collective-permute-start(f32[56,128]{1,0:T(8,128)S(1)} %get-tuple-element.112.refs_0_), channel_id=1, source_target_pairs={{0,9},{1,8},{2,11},{3,10},{4,13},{5,12},{6,15},{7,14},{8,1},{9,0},... | collective-permute-start | bytes 86024 | tf_op jit(solution)/shard_map/ppermute | solution.py:470
  21.9 6.7 %collective-permute-start.6 = (f32[56,128]{1,0:T(8,128)S(1)}, f32[56,128]{1,0:T(8,128)S(1)}, u32[]{:S(2)}, u32[]{:S(2)}) collective-permute-start(f32[56,128]{1,0:T(8,128)S(1)} %get-tuple-element.112.refs_0_), channel_id=1, source_target_pairs={{0,17},{1,16},{2,19},{3,18},{4,21},{5,20},{6,23},{7,22},{8,25},{9,... | collective-permute-start | bytes 86024 | tf_op jit(solution)/shard_map/ppermute | solution.py:470
  24.2 5.1 %collective-permute-start.7 = (f32[56,128]{1,0:T(8,128)S(1)}, f32[56,128]{1,0:T(8,128)S(1)}, u32[]{:S(2)}, u32[]{:S(2)}) collective-permute-start(f32[56,128]{1,0:T(8,128)S(1)} %get-tuple-element.112.refs_0_), channel_id=1, source_target_pairs={{0,25},{1,24},{2,27},{3,26},{4,29},{5,28},{6,31},{7,30},{8,17},{9,... | collective-permute-start | bytes 86024 | tf_op jit(solution)/shard_map/ppermute | solution.py:470
  53.8 1.2 %collective-permute-start.8 = (f32[56,128]{1,0:T(8,128)S(1)}, f32[56,128]{1,0:T(8,128)S(1)}, u32[]{:S(2)}, u32[]{:S(2)}) collective-permute-start(f32[56,128]{1,0:T(8,128)S(1)} %get-tuple-element.132.refs_0_), channel_id=1, source_target_pairs={{0,1},{1,0},{2,3},{3,2},{4,5},{5,4},{6,7},{7,6},{8,9},{9,8},{10,11... | collective-permute-start | bytes 86024 | tf_op jit(solution)/shard_map/ppermute | solution.py:470
  55.0 6.0 %collective-permute-start.10 = (f32[56,128]{1,0:T(8,128)S(1)}, f32[56,128]{1,0:T(8,128)S(1)}, u32[]{:S(2)}, u32[]{:S(2)}) collective-permute-start(f32[56,128]{1,0:T(8,128)S(1)} %get-tuple-element.138.refs_0_), channel_id=1, source_target_pairs={{0,5},{1,4},{2,7},{3,6},{4,1},{5,0},{6,3},{7,2},{8,13},{9,12},{10,... | collective-permute-start | bytes 86024 | tf_op jit(solution)/shard_map/ppermute | solution.py:470
  56.0 5.0 %collective-permute-start.11 = (f32[56,128]{1,0:T(8,128)S(1)}, f32[56,128]{1,0:T(8,128)S(1)}, u32[]{:S(2)}, u32[]{:S(2)}) collective-permute-start(f32[56,128]{1,0:T(8,128)S(1)} %get-tuple-element.138.refs_0_), channel_id=1, source_target_pairs={{0,7},{1,6},{2,5},{3,4},{4,3},{5,2},{6,1},{7,0},{8,15},{9,14},{10,... | collective-permute-start | bytes 86024 | tf_op jit(solution)/shard_map/ppermute | solution.py:470
  57.1 4.0 %collective-permute-start.9 = (f32[56,128]{1,0:T(8,128)S(1)}, f32[56,128]{1,0:T(8,128)S(1)}, u32[]{:S(2)}, u32[]{:S(2)}) collective-permute-start(f32[56,128]{1,0:T(8,128)S(1)} %get-tuple-element.138.refs_0_), channel_id=1, source_target_pairs={{0,3},{1,2},{2,1},{3,0},{4,7},{5,6},{6,5},{7,4},{8,11},{9,10},{10,... | collective-permute-start | bytes 86024 | tf_op jit(solution)/shard_map/ppermute | solution.py:470
  61.1 7.8 %copy-start.1 = (s32[14,1,32,128]{3,2,1,0:T(8,128)S(1)}, s32[14,1,32,128]{3,2,1,0:T(8,128)}, u32[]{:S(2)}) copy-start(s32[14,1,32,128]{3,2,1,0:T(8,128)} %param.29) | copy-start | bytes 688132
  61.1 7.8 %copy-start.2 = (s32[1,32,128]{2,1,0:T(8,128)S(1)}, s32[1,32,128]{2,1,0:T(8,128)}, u32[]{:S(2)}) copy-start(s32[1,32,128]{2,1,0:T(8,128)} %param.28) | copy-start | bytes 49156
  61.1 7.8 %copy-start.3 = (bf16[14,48]{1,0:T(8,128)(2,1)S(1)}, bf16[14,48]{1,0:T(8,128)(2,1)}, u32[]{:S(2)}) copy-start(bf16[14,48]{1,0:T(8,128)(2,1)} %head_ref.1) | copy-start | bytes 4036
  61.1 7.8 %copy-start.4 = (f32[14]{0:T(128)S(1)}, f32[14]{0:T(128)}, u32[]{:S(2)}) copy-start(f32[14]{0:T(128)} %param.27) | copy-start | bytes 172
  61.1 7.1 %collective-permute-start.12 = (f32[56,128]{1,0:T(8,128)S(1)}, f32[56,128]{1,0:T(8,128)S(1)}, u32[]{:S(2)}, u32[]{:S(2)}) collective-permute-start(f32[56,128]{1,0:T(8,128)S(1)} %get-tuple-element.152.refs_0_), channel_id=1, source_target_pairs={{0,9},{1,8},{2,11},{3,10},{4,13},{5,12},{6,15},{7,14},{8,1},{9,0},... | collective-permute-start | bytes 86024 | tf_op jit(solution)/shard_map/ppermute | solution.py:470
  62.3 5.9 %collective-permute-start.13 = (f32[56,128]{1,0:T(8,128)S(1)}, f32[56,128]{1,0:T(8,128)S(1)}, u32[]{:S(2)}, u32[]{:S(2)}) collective-permute-start(f32[56,128]{1,0:T(8,128)S(1)} %get-tuple-element.152.refs_0_), channel_id=1, source_target_pairs={{0,17},{1,16},{2,19},{3,18},{4,21},{5,20},{6,23},{7,22},{8,25},{9,... | collective-permute-start | bytes 86024 | tf_op jit(solution)/shard_map/ppermute | solution.py:470
  62.6 5.6 %collective-permute-start.14 = (f32[56,128]{1,0:T(8,128)S(1)}, f32[56,128]{1,0:T(8,128)S(1)}, u32[]{:S(2)}, u32[]{:S(2)}) collective-permute-start(f32[56,128]{1,0:T(8,128)S(1)} %get-tuple-element.152.refs_0_), channel_id=1, source_target_pairs={{0,25},{1,24},{2,27},{3,26},{4,29},{5,28},{6,31},{7,30},{8,17},{9,... | collective-permute-start | bytes 86024 | tf_op jit(solution)/shard_map/ppermute | solution.py:470
  73.0 10.8 %all-to-all-start.1 = ((f32[32,1,128]{2,1,0:T(1,128)}), f32[32,1,128]{2,1,0:T(1,128)S(1)}, u32[]{:S(2)}, u32[]{:S(2)}) async-start(f32[32,1,128]{2,1,0:T(1,128)} %bitcast.14), calls=%async_computation.1 | async-start | bytes 32768 | tf_op jit(solution)/shard_map/all_to_all | solution.py:643

commit v3 on v2

--- a/solution.py
+++ b/solution.py
@@ -16,6 +16,7 @@
 f32, bf16 = jnp.float32, jnp.bfloat16
 vmem_bytes = 24 * 1024 * 1024
 wide = 4
+tap_count = 4
 
 
 def half_silu(v):
@@ -72,8 +73,12 @@
     return turned(jnp.concatenate(rows, axis=0))
 
 
-def columns_of(layer, rows_ref):
-    return jnp.transpose(rows_ref[layer], (1, 0))
+def repeat(steps, body):
+    if steps <= 2:
+        for g in range(steps):
+            body(g)
+    else:
+        pl.loop(0, steps)(body)
 
 
 def tail_tile(tail_ref, model):
@@ -119,20 +124,19 @@
 
 
 def swap_lanes(parts):
-    count = len(parts)
-    if count == 1:
-        return parts
-    width = LANES // count
+    parts = list(parts)
+    width = LANES // len(parts)
     place = lax.broadcasted_iota(jnp.int32, parts[0].shape, 1) // width
-    result = []
-    for b in range(count):
-        total = None
-        for a, part in enumerate(parts):
-            shift = (a - b) * width % LANES
-            moved = pltpu.roll(part, shift, 1) if shift else part
-            total = moved if total is None else jnp.where(place == a, moved, total)
-        result.append(total)
-    return result
+    bit = 1
+    while bit < len(parts):
+        for a in range(len(parts)):
+            if not a & bit:
+                low, high = parts[a], parts[a | bit]
+                upper = (place & bit) != 0
+                parts[a] = jnp.where(upper, pltpu.roll(high, bit * width, 1), low)
+                parts[a | bit] = jnp.where(upper, high, pltpu.roll(low, LANES - bit * width, 1))
+        bit *= 2
+    return parts
 
 
 def to_sequence(volume_ref, hid_ref, turn_ref, tile_ref):
@@ -175,57 +179,79 @@
 
 def convolve(proj_ref, rows, cols, first, outs):
     group = proj_ref.shape[1] // SCAN_BLOCK - 1
-    tap_count = 4
+    lags = range(1, tap_count)
+    lane = lax.broadcasted_iota(jnp.int32, (16, SCAN_BLOCK), 1)
     for r in range(0, rows, 16):
-        conv_in = proj_ref[r : r + 16, :]
-        half = 0.5 * cols[first + r : first + r + 16, :]
-        total = None
-        for offset in range(tap_count):
-            lag = tap_count - 1 - offset
-            shifted = pltpu.roll(conv_in, lag, 1) if lag else conv_in
-            term = half[:, offset : offset + 1] * shifted[:, SCAN_BLOCK:]
-            total = half[:, tap_count : tap_count + 1] + term if total is None else total + term
-        conv_out = half_silu(total).astype(bf16)
+        half = [
+            jnp.broadcast_to(cols[first + r : first + r + 16, k : k + 1], (16, SCAN_BLOCK)) for k in range(tap_count + 1)
+        ]
         ref, at = next((ref, r - low) for ref, low, high in outs if low <= r < high)
+        before = proj_ref[r : r + 16, span(0)]
+        before = [pltpu.roll(before, lag, 1) for lag in lags]
         for u in range(group):
-            ref[u, at : at + 16, :] = conv_out[:, span(u)]
+            conv_in = proj_ref[r : r + 16, span(u + 1)]
+            now = [pltpu.roll(conv_in, lag, 1) for lag in lags]
+            total = half[tap_count]
+            for lag in reversed(lags):
+                shifted = jnp.where(lane < lag, before[lag - 1], now[lag - 1])
+                total = total + half[tap_count - 1 - lag] * shifted
+            total = total + half[tap_count - 1] * conv_in
+            ref[u, at : at + 16, :] = half_silu(total).astype(bf16)
+            before = now
     proj_ref[:, span(0)] = proj_ref[:, span(group)]
 
 
+def sequence_kernel(size, me_ref, volume_ref, hid_ref, tail_ref, turn_ref, tile_ref):
+    to_sequence(volume_ref, hid_ref, turn_ref, tile_ref)
+    last = hid_ref[hid_ref.shape[0] - 1]
+    tail_ref[...] = jnp.where(me_ref[0] == size - 1, jnp.zeros_like(last), last)
+
+
+def weights_kernel(
+    in_ref, dt_ref, taps_ref, conv_bias_ref, gain_ref, dt_bias_ref, rate_ref, skip_ref, out_gain_ref, weight_ref, cols_ref
+):
+    model = in_ref.shape[1]
+    lanes = cols_ref.shape[1]
+    for layer in range(in_ref.shape[0]):
+        here = slice(layer, layer + 1)
+        weight = turned(in_ref[layer].astype(f32))[: in_ref.shape[2]]
+        steps = [dt_ref[h, here, :].astype(f32) for h in range(dt_ref.shape[0])]
+        unused = jnp.zeros((weight_ref.shape[1] - weight.shape[0] - len(steps), model), f32)
+        weight_ref[layer] = jnp.concatenate([weight] + steps + [unused], axis=0).astype(bf16)
+        rows = [0.5 * taps_ref[layer], 0.5 * conv_bias_ref[here, :], gain_ref[here, :], dt_bias_ref[here, :]]
+        rows += [-rate_ref[here, :], skip_ref[here, :], out_gain_ref[here, :]]
+        rows = [padded(r, r.shape[0], lanes) for r in rows]
+        count = sum(r.shape[0] for r in rows)
+        rows.append(jnp.zeros((cols_ref.shape[2] - count, lanes), f32))
+        cols_ref[layer] = jnp.transpose(jnp.concatenate(rows, axis=0), (1, 0))
+
+
 def state_kernel(
-    layer, heads, from_volume, group, hid_ref, tail_ref, matrix_ref, rows_ref, inner_ref, write_ref, dec_ref,
-    state_ref, total_ref, *rest
+    layer, heads, group, hid_ref, tail_ref, weight_ref, cols_ref, inner_ref, write_ref, dec_ref, state_ref, total_ref,
+    proj_ref, carry_ref,
 ):
-    if from_volume:
-        volume_ref, hid_ref, proj_ref, carry_ref, turn_ref, tile_ref = (hid_ref,) + rest
-        to_sequence(volume_ref, hid_ref, turn_ref, tile_ref)
-    else:
-        proj_ref, carry_ref = rest
-    model = matrix_ref.shape[1]
+    model = weight_ref.shape[2]
     inner = inner_ref.shape[1]
     width = inner // heads
     state = write_ref.shape[1]
     rows = inner + state
-    weight = jnp.transpose(matrix_ref[layer].astype(f32), (1, 0))
-    dt_first = 2 * (inner + state)
-    weight = jnp.concatenate([weight[inner : inner + rows], weight[dt_first : dt_first + 8]], axis=0).astype(bf16)
-    cols = columns_of(layer, rows_ref)
+    dt_first = 2 * rows
+    weight = jnp.concatenate([weight_ref[layer, inner : inner + rows], weight_ref[layer, dt_first : dt_first + 16]], axis=0)
+    cols = cols_ref[layer]
     gain_col = cols[:model, 5:6]
     head_cols = cols[:8, 6:8]
-
     carry_ref[...] = jnp.zeros_like(carry_ref)
     proj_ref[:, span(0)] = rounded(project(weight, normalise(tail_tile(tail_ref, model), gain_col))[:rows])
     lane = lax.broadcasted_iota(jnp.int32, (1, LANES), 1)
     alls = (hid_ref, inner_ref, write_ref, dec_ref, state_ref)
 
-    @pl.loop(0, inner_ref.shape[0] // group)
-    def _(g):
+    def step_group(g):
         hid_ref, inner_ref, write_ref, dec_ref, state_ref = (r.at[pl.ds(g * group, group)] for r in alls)
         dt_raw = []
         for q in range(0, group, wide):
             projected = project(weight, normalise(side_by_side(hid_ref, q, wide, model), gain_col))
             proj_ref[:, span(q + 1, wide)] = rounded(projected[:rows])
-            dt_raw.append(projected[rows:])
+            dt_raw.append(projected[rows : rows + 8])
         step = jnp.concatenate(dt_raw, axis=1) + head_cols[:, 0:1]
         step = jnp.maximum(step, 0.0) + jnp.log1p(jnp.exp(-jnp.abs(step)))
         log_decay = head_cols[:, 1:2] * step
@@ -264,23 +290,23 @@
         carry_ref[0:state, :] = running
         carry_ref[state:, :] = running_log
 
+    repeat(inner_ref.shape[0] // group, step_group)
     total_ref[...] = pack(carry_ref[0:state, :], carry_ref[state:, :], heads)
 
 
 def local_kernel(
-    layer, heads, first, count, group, hid_ref, tail_ref, matrix_ref, rows_ref, inner_ref, write_ref, dec_ref, *rest
+    layer, heads, first, count, group, hid_ref, tail_ref, weight_ref, cols_ref, inner_ref, write_ref, dec_ref, *rest
 ):
     local_ref, gate_ref, read_ref, proj_ref, score_ref, weights_ref = rest[-6:]
-    model = matrix_ref.shape[1]
+    model = weight_ref.shape[2]
     inner = inner_ref.shape[1]
     width = inner // heads
     state = read_ref.shape[1]
-    weight = jnp.transpose(matrix_ref[layer].astype(f32), (1, 0))
-    weight = jnp.concatenate([weight[:inner], weight[2 * inner + state : 2 * (inner + state)]], axis=0).astype(bf16)
-    cols = columns_of(layer, rows_ref)
+    read_first = 2 * inner + state
+    weight = jnp.concatenate([weight_ref[layer, :inner], weight_ref[layer, read_first : read_first + state]], axis=0)
+    cols = cols_ref[layer]
     gain_col = cols[:model, 5:6]
     skip_cols = cols[:8, 8:9]
-
     before = hid_ref[first - 1][:model] if first else tail_tile(tail_ref, model)
     proj_ref[:, span(0)] = rounded(project(weight[inner:], normalise(before, gain_col)))
     source = lax.broadcasted_iota(jnp.int32, (SCAN_BLOCK, SCAN_BLOCK), 0)
@@ -289,8 +315,7 @@
     log2e = 1.4426950408889634
     alls = (hid_ref, inner_ref, write_ref, dec_ref, local_ref, gate_ref, read_ref)
 
-    @pl.loop(0, count // group)
-    def _(g):
+    def step_group(g):
         hid_ref, inner_ref, write_ref, dec_ref, local_ref, gate_ref, read_ref = (
             r.at[pl.ds(first + g * group, group)] for r in alls
         )
@@ -324,108 +349,138 @@
                     project(values, weights_ref[u, h]) + skip_cols[h : h + 1, 0:1] * values.astype(f32)
                 )
 
-
-def finished(q, layer, heads, enter, refs, out_gain, out_proj):
+    repeat(count // group, step_group)
+
+
+def finish_group(heads, enter, refs, out_gain, out_proj, gated_ref, square_ref, take):
     hid_ref, local_ref, gate_ref, read_ref, dec_ref, state_ref = refs
-    inner = local_ref.shape[1]
+    group, inner, _ = local_ref.shape
     width = inner // heads
     state = read_ref.shape[1]
-    inter = []
-    for u in range(q, q + wide):
+    for u in range(group):
         entering = jnp.exp(state_ref[u, state : state + 1, :]) * enter + state_ref[u, 0:state, :]
-        inter.append(contract(entering.astype(bf16), read_ref[u], 0)[:inner])
-    decay = jnp.exp(jnp.concatenate([dec_ref[u, 0:8, :] for u in range(q, q + wide)], axis=1))
-    scan_out = side_by_side(local_ref, q, wide) + spread(decay, 0, heads, width) * jnp.concatenate(inter, axis=1)
-    gated = scan_out * side_by_side(gate_ref, q, wide)
-    mean_sq = jnp.mean(gated * gated, axis=0, keepdims=True)
-    gated = (gated * lax.rsqrt(mean_sq + eps) * out_gain).astype(bf16)
-    hidden = side_by_side(hid_ref, q, wide, out_proj.shape[0]).astype(f32)
-    return (hidden + project(out_proj, gated)).astype(bf16)
+        inter = contract(entering.astype(bf16), read_ref[u], 0)[:inner]
+        decay = jnp.exp(dec_ref[u, 0:8, :])
+        gated = (local_ref[u] + spread(decay, 0, heads, width) * inter) * gate_ref[u]
+        gated_ref[u] = gated
+        square_ref[u] = jnp.sum((gated * gated).reshape(inner // 8, 8, SCAN_BLOCK), axis=0)
+    for u in range(group):
+        mean_sq = jnp.sum(square_ref[u], axis=0, keepdims=True) * (1.0 / inner)
+        square_ref[u, 0:1, :] = lax.rsqrt(mean_sq + eps)
+    for q in range(0, group, wide):
+        scale = jnp.concatenate([square_ref[u, 0:1, :] for u in range(q, q + wide)], axis=1)
+        gated = (side_by_side(gated_ref, q, wide) * scale * out_gain).astype(bf16)
+        hidden = side_by_side(hid_ref, q, wide, out_proj.shape[0]).astype(f32)
+        result = (hidden + project(out_proj, gated)).astype(bf16)
+        for u in range(wide):
+            take(q + u, result[:, span(u)])
 
 
 def finish_kernel(
-    layer, heads, cells_x, group, enter_ref, hid_ref, local_ref, gate_ref, read_ref, dec_ref, state_ref, matrix_ref,
-    rows_ref, out_ref, tile_ref, turn_ref, plane_ref,
+    layer, heads, cells_x, group, enter_ref, hid_ref, local_ref, gate_ref, read_ref, dec_ref, state_ref, cols_ref,
+    out_proj_ref, out_ref, tile_ref, turn_ref, plane_ref, gated_ref, square_ref,
 ):
-    model = matrix_ref.shape[1]
+    model = out_proj_ref.shape[1]
     inner = local_ref.shape[1]
     alls = (hid_ref, local_ref, gate_ref, read_ref, dec_ref, state_ref)
     enter = unpack(enter_ref[...], heads)
-    out_gain = columns_of(layer, rows_ref)[:inner, 9:10]
-    out_proj = matrix_ref[layer][:, -LANES:][:, :inner]
-
-    @pl.loop(0, hid_ref.shape[0] // group)
-    def _(g):
+    out_gain = cols_ref[layer, :inner, 9:10]
+
+    def step_group(g):
+        def take(u, result):
+            at = (g * group + u) * model
+            at = at if isinstance(at, int) else pl.multiple_of(at, 8)
+            tile_ref[pl.ds(at, model), :] = result.astype(f32)
+
         refs = tuple(r.at[pl.ds(g * group, group)] for r in alls)
-        for q in range(0, group, wide):
-            result = finished(q, layer, heads, enter, refs, out_gain, out_proj).astype(f32)
-            for u in range(wide):
-                at = pl.multiple_of((g * group + q + u) * model, 8)
-                tile_ref[pl.ds(at, model), :] = result[:, span(u)]
-
+        finish_group(heads, enter, refs, out_gain, out_proj_ref[layer], gated_ref, square_ref, take)
+
+    repeat(hid_ref.shape[0] // group, step_group)
     to_planes(tile_ref, out_ref, turn_ref, plane_ref, model, cells_x)
 
 
+def softmax_parts(logits_ref, labels_ref, distance_ref, here):
+    classes = logits_ref.shape[0]
+    logits = logits_ref[:, here, :]
+    peak = jnp.max(logits, axis=0)
+    shifted = jnp.exp(logits - peak[None])
+    partition = jnp.sum(shifted, axis=0)
+    probability = shifted / partition[None]
+    weighted = probability * (distance_ref[:, here, :].astype(f32) * (1.0 / dist_unit))
+    expect = jnp.sum(weighted, axis=0)
+    hot = labels_ref[here, :][None] == lax.broadcasted_iota(jnp.int32, logits.shape, 0)
+    return logits, peak, partition, probability, weighted, expect, hot
+
+
+def tiles_of(count, body):
+    if count <= 32:
+        for z in range(0, count, 8):
+            body(pl.ds(z, 8))
+    else:
+        pl.loop(0, count // 8)(lambda z: body(pl.ds(pl.multiple_of(z * 8, 8), 8)))
+
+
 def head_kernel(
-    layer, heads, group, enter_ref, hid_ref, local_ref, gate_ref, read_ref, dec_ref, state_ref, matrix_ref, rows_ref,
-    head_ref, bias_ref, labels_ref, distance_ref, features_ref, grad_ref, loss_ref, feature_scr, logit_scr, sum_scr,
+    layer, heads, group, enter_ref, hid_ref, local_ref, gate_ref, read_ref, dec_ref, state_ref, cols_ref, out_proj_ref,
+    head_ref, bias_ref, labels_ref, distance_ref, after_ref, logits_ref, loss_ref, gated_ref, square_ref, logit_scr,
+    sum_scr,
 ):
+    count = hid_ref.shape[0]
     classes = distance_ref.shape[0]
     inner = local_ref.shape[1]
     alls = (hid_ref, local_ref, gate_ref, read_ref, dec_ref, state_ref)
     enter = unpack(enter_ref[...], heads)
-    out_gain = columns_of(layer, rows_ref)[:inner, 9:10]
-    out_proj = matrix_ref[layer][:, -LANES:][:, :inner]
+    out_gain = cols_ref[layer, :inner, 9:10]
     bias = columns(bias_ref[...])[:classes, 0:1]
+
+    def step_group(g):
+        def take(u, result):
+            after_ref[g * group + u] = result
+            logit_scr[pl.ds(u, classes, stride=group), :] = project(head_ref[...], result) + bias
+
+        refs = tuple(r.at[pl.ds(g * group, group)] for r in alls)
+        finish_group(heads, enter, refs, out_gain, out_proj_ref[layer], gated_ref, square_ref, take)
+        at = g * group if isinstance(g, int) else pl.multiple_of(g * group, group)
+        logits_ref[:, pl.ds(at, group), :] = logit_scr[...].reshape(classes, group, SCAN_BLOCK)
+
+    repeat(count // group, step_group)
     sum_scr[...] = jnp.zeros_like(sum_scr)
 
-    @pl.loop(0, hid_ref.shape[0] // group)
-    def _(g):
-        refs = tuple(r.at[pl.ds(g * group, group)] for r in alls)
-        here = pl.ds(pl.multiple_of(g * group, group), group)
-        for q in range(0, group, wide):
-            result = finished(q, layer, heads, enter, refs, out_gain, out_proj)
-            logits = project(head_ref[...], result) + bias
-            result = result.astype(f32)
-            for u in range(wide):
-                feature_scr[pl.ds(q + u, result.shape[0], stride=group), :] = result[:, span(u)]
-                logit_scr[pl.ds(q + u, classes, stride=group), :] = logits[:, span(u)]
-        features = feature_scr[...].reshape(-1, group, SCAN_BLOCK)
-        features_ref[:, here, :] = features.astype(bf16)
-        logits = logit_scr[...].reshape(-1, group, SCAN_BLOCK)
-        labels = labels_ref[here, :]
-        peak = jnp.max(logits, axis=0)
-        shifted = jnp.exp(logits - peak[None])
-        partition = jnp.sum(shifted, axis=0)
-        probability = shifted / partition[None]
-        distance_map = distance_ref[:, here, :].astype(f32) * (1.0 / dist_unit)
-        weighted = probability * distance_map
-        expect = jnp.sum(weighted, axis=0)
-        hot = labels[None] == lax.broadcasted_iota(jnp.int32, logits.shape, 0)
+    def losses(here):
+        logits, peak, partition, _, _, expect, hot = softmax_parts(logits_ref, labels_ref, distance_ref, here)
         chosen = jnp.sum(jnp.where(hot, logits, 0.0), axis=0)
-        loss = peak + jnp.log(partition) - chosen + expect
+        sum_scr[...] += peak + jnp.log(partition) - chosen + expect
+
+    tiles_of(count, losses)
+    loss_ref[...] = jnp.broadcast_to(jnp.sum(sum_scr[...], axis=0, keepdims=True), loss_ref.shape)
+
+
+def gradient_kernel(after_ref, logits_ref, labels_ref, distance_ref, features_ref, grad_ref, feature_scr):
+    count, model, _ = after_ref.shape
+    for u in range(count):
+        feature_scr[pl.ds(u, model, stride=count), :] = after_ref[u].astype(f32)
+    features_ref[...] = feature_scr[...].reshape(model, count, SCAN_BLOCK).astype(bf16)
+
+    def gradients(here):
+        _, _, _, probability, weighted, expect, hot = softmax_parts(logits_ref, labels_ref, distance_ref, here)
         grad_ref[:, here, :] = probability - jnp.where(hot, 1.0, 0.0) + weighted - probability * expect[None]
-        sum_scr[...] += jnp.sum(loss, axis=0, keepdims=True)
-
-    loss_ref[...] = jnp.broadcast_to(sum_scr[...], loss_ref.shape)
+
+    tiles_of(count, gradients)
 
 
 def params(size=vmem_bytes):
     return pltpu.CompilerParams(vmem_limit_bytes=size)
 
 
+def cost(us):
+    return pl.CostEstimate(flops=int(us * 1e9), bytes_accessed=int(us * 3.5e6), transcendentals=0)
+
+
 vmem = pl.BlockSpec(memory_space=pltpu.VMEM)
 
 
-def from_before(value):
-    size = lax.axis_size(axes)
-    value = jnp.where(lax.axis_index(axes) == size - 1, jnp.zeros_like(value), value)
-    return lax.ppermute(value, axes, [(i, (i + 1) % size) for i in range(size)])
-
-
-def join_kernel(heads, reach, me_ref, before_ref, *refs):
-    members, before_out, total_out = refs[:-2], refs[-2], refs[-1]
-    radix = len(members)
+def join_kernel(heads, reach, radix, me_ref, before_ref, *refs):
+    members, outs = refs[:radix], refs[radix:]
     digit = (me_ref[0] & (radix * reach - 1)) // reach
     rows = before_ref.shape[0] - 8
     third = rows // heads
@@ -442,15 +497,16 @@
     values = [ref[...] for ref in members]
     before = before_ref[...]
     ahead, total = None, None
-    for place in range(radix):
+    for place in range(radix if len(outs) > 1 else radix - 1):
         value = values[0]
         for k in range(1, radix):
             value = jnp.where(digit ^ k == place, values[k], value)
         total = value if total is None else combine(total, value)
         if place < radix - 1:
             ahead = jnp.where(place < digit, total, jnp.zeros_like(total) if ahead is None else ahead)
-    before_out[...] = combine(ahead, before)
-    total_out[...] = total
+    outs[0][...] = combine(ahead, before)
+    if len(outs) > 1:
+        outs[1][...] = total
 
 
 def prefix_state(me, total, held, pieces, heads):
@@ -471,14 +527,16 @@
         ]
         if piece >= 0:
             others, done = lax.optimization_barrier((others, done))
-        before, total = pl.pallas_call(
-            functools.partial(join_kernel, heads, reach),
+        outs = 2 if reach * radix < size else 1
+        before, *total = pl.pallas_call(
+            functools.partial(join_kernel, heads, reach, radix),
             in_specs=[pl.BlockSpec(memory_space=pltpu.SMEM)] + [vmem] * (1 + radix),
-            out_specs=[vmem] * 2,
-            out_shape=[jax.ShapeDtypeStruct(total.shape, f32)] * 2,
+            out_specs=[vmem] * outs,
+            out_shape=[jax.ShapeDtypeStruct(before.shape, f32)] * outs,
             compiler_params=params(2 * 1024 * 1024),
             name="join",
         )(me, before, total, *others)
+        total = total[0] if total else None
     return before, done
 
 
@@ -486,43 +544,71 @@
     return jax.ShapeDtypeStruct((count, rows, SCAN_BLOCK), kind)
 
 
+def call_sequence(me, size, volume):
+    model, cells_x, cells_y = volume.shape
+    count = cells_x * cells_y // SCAN_BLOCK
+    return pl.pallas_call(
+        functools.partial(sequence_kernel, size),
+        in_specs=[pl.BlockSpec(memory_space=pltpu.SMEM), vmem],
+        out_specs=[vmem] * 2,
+        out_shape=[tile(count, model, bf16), jax.ShapeDtypeStruct((model, SCAN_BLOCK), bf16)],
+        scratch_shapes=[
+            pltpu.VMEM((model * cells_x // LANES, cells_y, LANES), f32),
+            pltpu.VMEM((count * model, LANES), f32),
+        ],
+        compiler_params=params(),
+        cost_estimate=cost(8),
+        name="sequence",
+    )(me, volume)
+
+
+def call_weights(norm_gain, in_proj, dt_proj, dt_bias, decay_rate, conv_weight, conv_bias, skip_gain, out_gain):
+    layers, projected, model = in_proj.shape
+    return pl.pallas_call(
+        weights_kernel,
+        in_specs=[vmem] * 9,
+        out_specs=[vmem] * 2,
+        out_shape=[
+            jax.ShapeDtypeStruct((layers, projected + 16, model), bf16),
+            jax.ShapeDtypeStruct((layers, -(-conv_bias.shape[1] // LANES) * LANES, 16), f32),
+        ],
+        compiler_params=params(4 * 1024 * 1024),
+        name="weights",
+    )(
+        jnp.swapaxes(in_proj, 1, 2), jnp.swapaxes(dt_proj, 0, 1), jnp.swapaxes(conv_weight, 1, 2), conv_bias, norm_gain,
+        dt_bias, decay_rate, skip_gain, out_gain,
+    )
+
+
 def call_states(layer, hidden, tail, weights):
-    from_volume = tail.ndim == 2
-    inner, heads, state, model = (weights[k] for k in ("inner", "heads", "state", "model"))
-    count = hidden.shape[1] * hidden.shape[2] // SCAN_BLOCK if from_volume else hidden.shape[0]
-    group = min(16, count)
-    out_shape = [
-        tile(count, inner, bf16),
-        tile(count, state, bf16),
-        tile(count, 16, f32),
-        tile(count, state + 8, f32),
-        jax.ShapeDtypeStruct((state * inner // LANES + 8, LANES), f32),
-    ]
-    scratch = [
-        pltpu.VMEM((inner + state, (group + 1) * SCAN_BLOCK), f32),
-        pltpu.VMEM((state + 8, LANES), f32),
-    ]
-    if from_volume:
-        out_shape.append(tile(count, model, bf16))
-        per = LANES // hidden.shape[1]
-        scratch.append(pltpu.VMEM((model // per, hidden.shape[2], LANES), f32))
-        scratch.append(pltpu.VMEM((count * model, LANES), f32))
+    inner, heads, state = (weights[k] for k in ("inner", "heads", "state"))
+    count = hidden.shape[0]
+    group = min(32, count)
     return pl.pallas_call(
-        functools.partial(state_kernel, layer, heads, from_volume, group),
+        functools.partial(state_kernel, layer, heads, group),
         in_specs=[vmem] * 4,
-        out_specs=[vmem] * len(out_shape),
-        out_shape=out_shape,
-        scratch_shapes=scratch,
+        out_specs=[vmem] * 5,
+        out_shape=[
+            tile(count, inner, bf16),
+            tile(count, state, bf16),
+            tile(count, 16, f32),
+            tile(count, state + 8, f32),
+            jax.ShapeDtypeStruct((state * inner // LANES + 8, LANES), f32),
+        ],
+        scratch_shapes=[
+            pltpu.VMEM((inner + state, (group + 1) * SCAN_BLOCK), f32),
+            pltpu.VMEM((state + 8, LANES), f32),
+        ],
         compiler_params=params(),
         name="states",
-    )(hidden, tail, weights["matrices"], weights["rows"])
+    )(hidden, tail, weights["rows"], weights["cols"])
 
 
 def call_local(layer, first, count, held, done, weights):
     hidden, tail, inner_values, write, dec = held
     total = hidden.shape[0]
     inner, heads, state = weights["inner"], weights["heads"], weights["state"]
-    group = min(8, count)
+    group = min(16, count)
     taken = [] if done is None else list(done)
     return pl.pallas_call(
         functools.partial(local_kernel, layer, heads, first, count, group),
@@ -537,22 +623,22 @@
         ],
         compiler_params=params(),
         name="local",
-    )(hidden, tail, weights["matrices"], weights["rows"], inner_values, write, dec, *taken)
+    )(hidden, tail, weights["rows"], weights["cols"], inner_values, write, dec, *taken)
 
 
 def layer_start(layer, me, hidden, tail, weights):
-    inner_values, write, dec, states, total, *sequence = call_states(layer, hidden, tail, weights)
-    if sequence:
-        (hidden,) = sequence
-    else:
-        tail = hidden
+    inner_values, write, dec, states, total = call_states(layer, hidden, tail, weights)
     cut = hidden.shape[0] // 2
     pieces = [
         lambda held, done, first=first: call_local(layer, first, cut, held, done, weights)
         for first in range(0, hidden.shape[0], cut)
     ]
     enter, done = prefix_state(me, total, (hidden, tail, inner_values, write, dec), pieces, weights["heads"])
-    return (enter, hidden, *done, dec, states, weights["matrices"], weights["rows"])
+    return (enter, hidden, *done, dec, states, weights["cols"], weights["out_proj"])
+
+
+def finish_scratch(group, weights):
+    return [pltpu.VMEM((group, weights["inner"], SCAN_BLOCK), f32), pltpu.VMEM((group, 8, SCAN_BLOCK), f32)]
 
 
 def call_finish(cells, parts, weights):
@@ -562,7 +648,7 @@
     rows = model + 8
     per = LANES // cells_x
     return pl.pallas_call(
-        functools.partial(finish_kernel, 0, weights["heads"], cells_x, min(16, count)),
+        functools.partial(finish_kernel, 0, weights["heads"], cells_x, min(32, count)),
         in_specs=[vmem] * len(parts),
         out_specs=vmem,
         out_shape=jax.ShapeDtypeStruct((cells_x, rows, cells_y), bf16),
@@ -570,7 +656,8 @@
             pltpu.VMEM((count * model, LANES), f32),
             pltpu.VMEM((model // per, cells_y, LANES), f32),
             pltpu.VMEM(((cells_x + 1) * rows, LANES), f32),
-        ],
+        ]
+        + finish_scratch(min(32, count), weights),
         compiler_params=params(),
         name="finish",
     )(*parts)
@@ -579,40 +666,38 @@
 def call_heads(size, parts, weights, head_weight, head_bias, labels, distance):
     classes, model = head_weight.shape
     count = parts[1].shape[0]
-    group = min(16, count)
+    group = min(32, count)
     return pl.pallas_call(
         functools.partial(head_kernel, 1, weights["heads"], group),
         in_specs=[vmem] * (len(parts) + 4),
         out_specs=[vmem] * 3,
         out_shape=[
-            jax.ShapeDtypeStruct((model, count, SCAN_BLOCK), bf16),
+            tile(count, model, bf16),
             jax.ShapeDtypeStruct((classes, count, SCAN_BLOCK), f32),
             jax.ShapeDtypeStruct((size, SCAN_BLOCK), f32),
         ],
-        scratch_shapes=[
-            pltpu.VMEM((model * group, SCAN_BLOCK), f32),
-            pltpu.VMEM((classes * group, SCAN_BLOCK), f32),
-            pltpu.VMEM((1, SCAN_BLOCK), f32),
-        ],
+        scratch_shapes=finish_scratch(group, weights)
+        + [pltpu.VMEM((classes * group, SCAN_BLOCK), f32), pltpu.VMEM((8, SCAN_BLOCK), f32)],
         compiler_params=params(),
         name="heads",
     )(*parts, head_weight, head_bias, labels, distance)
 
 
-def packed(norm_gain, in_proj, dt_proj, dt_bias, decay_rate, conv_weight, conv_bias, skip_gain, out_gain, out_proj):
-    lanes = lambda value, width: jnp.pad(value, ((0, 0),) * (value.ndim - 1) + ((0, width - value.shape[-1]),))
-    first = jnp.concatenate([in_proj, dt_proj], axis=1)
-    width = -(-(first.shape[1] + 8) // LANES) * LANES
-    second = out_proj.shape[2]
-    matrices = jnp.concatenate(
-        [lanes(jnp.swapaxes(first, 1, 2), width), lanes(out_proj, -(-second // LANES) * LANES)], axis=2
-    )
-    width = -(-conv_bias.shape[1] // LANES) * LANES
-    vectors = [conv_bias, norm_gain, dt_bias, -decay_rate, skip_gain, out_gain]
-    rows = [lanes(jnp.swapaxes(conv_weight, 1, 2), width)] + [lanes(v, width)[:, None] for v in vectors]
-    count = sum(r.shape[1] for r in rows)
-    rows.append(jnp.zeros((rows[0].shape[0], -(-count // 8) * 8 - count, width), f32))
-    return matrices, jnp.concatenate(rows, axis=1)
+def call_gradient(after, logits, labels, distance):
+    count, model, _ = after.shape
+    return pl.pallas_call(
+        gradient_kernel,
+        in_specs=[vmem] * 4,
+        out_specs=[vmem] * 2,
+        out_shape=[
+            jax.ShapeDtypeStruct((model, count, SCAN_BLOCK), bf16),
+            jax.ShapeDtypeStruct(logits.shape, f32),
+        ],
+        scratch_shapes=[pltpu.VMEM((model * count, SCAN_BLOCK), f32)],
+        compiler_params=params(),
+        cost_estimate=cost(4),
+        name="gradient",
+    )(after, logits, labels, distance)
 
 
 def per_device(
@@ -625,22 +710,23 @@
     inner = out_proj.shape[2]
     heads = decay_rate.shape[1]
     weights = dict(heads=heads, inner=inner, state=(in_proj.shape[1] - 2 * inner) // 2, model=model)
-    weights["matrices"], weights["rows"] = packed(
-        norm_gain, in_proj, dt_proj, dt_bias, decay_rate, conv_weight, conv_bias, skip_gain, out_gain, out_proj
+    me = lax.axis_index(axes).astype(jnp.int32).reshape(1)
+    hidden, tail = call_sequence(me, size, jnp.swapaxes(volume[:, 0], 1, 2))
+    weights["rows"], weights["cols"] = call_weights(
+        norm_gain, in_proj, dt_proj, dt_bias, decay_rate, conv_weight, conv_bias, skip_gain, out_gain
     )
-    tail = from_before(jnp.pad(volume[:, 0, cells_y - 1, :], ((0, 0), (SCAN_BLOCK - cells_x, 0))))
-    tail, me = lax.optimization_barrier((tail, lax.axis_index(axes).astype(jnp.int32).reshape(1)))
-    plane = jnp.swapaxes(volume[:, 0], 1, 2)
-    parts = layer_start(0, me, plane, tail, weights)
+    weights["out_proj"] = out_proj
+    tail = lax.ppermute(tail, axes, [(i, (i + 1) % size) for i in range(size)])
+    parts = layer_start(0, me, hidden, tail, weights)
     planes = call_finish((cells_x, cells_y), parts, weights)
     hidden = lax.all_to_all(planes, axes, split_axis=0, concat_axis=0, tiled=True)
     count = hidden.shape[0]
     parts = layer_start(1, me, hidden, hidden, weights)
-    features, grad, loss = call_heads(
-        size, parts, weights, head_weight, head_bias[None, :], labels.reshape(count, SCAN_BLOCK),
-        distance.reshape(classes, count, SCAN_BLOCK),
-    )
+    labels, distance = labels.reshape(count, SCAN_BLOCK), distance.reshape(classes, count, SCAN_BLOCK)
+    after, logits, loss = call_heads(size, parts, weights, head_weight, head_bias[None, :], labels, distance)
     shared = lax.all_to_all(loss, axes, 0, 0, tiled=True)
+    features, grad = call_gradient(after, logits, labels, distance)
+    shared, features, grad = lax.optimization_barrier((shared, features, grad))
     voxel_weight = 1.0 + 3.0 * jnp.arange(size, dtype=f32) / (size - 1.0)
     total_loss = jnp.sum(voxel_weight[:, None] * shared) / (2.5 * count * SCAN_BLOCK * size)
     return (

time: 86.6 us -> 80.4 us (0.928)
  Pallas kernels: 28.3 us -> 22.4 us
  waiting for transfers between devices: 14.6 us -> 16.8 us
  other arithmetic: 2.48 us -> 0.68 us
  local copies, waits for them, and re-layouts: 2.58 us -> 1.05 us
    pallas_call x4, Pallas kernels: 11.8 us -> 8.89 us  [call_local(): pl.pallas_call(functools.partial(local_kernel, layer, heads, first, count...]
    ppermute x1, waiting for transfers between devices: 4.48 us -> 7.04 us  [per_device(): tail = lax.ppermute(tail, axes, [(i, (i + 1) % size) for i in range(size)])]
    all_to_all x1, waiting for transfers between devices: 7.14 us -> 5.45 us  [per_device(): shared = lax.all_to_all(loss, axes, 0, 0, tiled=True)]
    pallas_call x1, Pallas kernels: 4.16 us -> 2.61 us  [call_heads(): pl.pallas_call(functools.partial(head_kernel, 1, weights['heads'], group)...]
    pallas_call x1, Pallas kernels: 3.12 us -> 1.76 us  [call_finish(): pl.pallas_call(functools.partial(finish_kernel, 0, weights['heads'], cell...]
    ppermute x14, waiting for transfers between devices: 2.98 us -> 4.26 us  [prefix_state(): lax.ppermute(total, axes, [(k, k ^ (step * reach | 1)) for k in range(siz...]
    slice x1 -> x0, local copies, waits for them, and re-layouts: 1.25 us -> none  [per_device(): volume[:, 0, cells_y - 1, :]]
    transpose x1 -> x0, other arithmetic: 0.97 us -> none  [packed(): jnp.swapaxes(first, 1, 2)]
  transfers between devices with their start and end apart: 16 -> 16, of which waited for: 5 -> 7; matrix products, arithmetic and copies ran while one was open for 3% -> 0% of each run, Pallas kernels for 14% -> 13%
where the time goes in v3:
time: 80.4 us; the launch traced here: 80.2 us
  Pallas kernels  22.4 us (28%)
  starting transfers between devices  18.8 us (23%)
  blocking collectives  17.8 us (22%)
  waiting for transfers between devices  16.8 us (21%)
  between operations  2.7 us (3%)
  local copies, waits for them, and re-layouts  1.05 us (1%)
    all_to_all x1, blocking collectives, per_device(): lax.all_to_all(planes, axes, split_axis=0, concat_axis=0, tiled=True)  17.8 us
    ppermute x14, starting transfers between devices, prefix_state(): lax.ppermute(total, axes, [(k, k ^ (step * reach | 1)) for k in range(siz...  14.3 us
    pallas_call x4, Pallas kernels, call_local(): pl.pallas_call(functools.partial(local_kernel, layer, heads, first, count...  8.89 us
    ppermute x1, waiting for transfers between devices, per_device(): tail = lax.ppermute(tail, axes, [(i, (i + 1) % size) for i in range(size)])  7.04 us
    pallas_call x2, Pallas kernels, call_states(): pl.pallas_call(functools.partial(state_kernel, layer, heads, group), in_s...  6.02 us
    all_to_all x1, waiting for transfers between devices, per_device(): shared = lax.all_to_all(loss, axes, 0, 0, tiled=True)  5.45 us
    ppermute x14, waiting for transfers between devices, prefix_state(): lax.ppermute(total, axes, [(k, k ^ (step * reach | 1)) for k in range(siz...  4.26 us
    all_to_all x1, starting transfers between devices, per_device(): shared = lax.all_to_all(loss, axes, 0, 0, tiled=True)  4.06 us
  transfers between devices with their start and end apart: 16, of which 7 were waited for; matrix products, arithmetic and copies ran while one was open for 0% of the time, Pallas kernels for 13%

profile of v3, /device:TPU:0, one launch (start us, length us, event | category | flops | bytes accessed | tf_op | source)
XLA Modules:
  0.0 80.2 jit_solution(16193893537097024363)
XLA Ops:
  0.7 1.0 %copy-done.14 = bf16[48,1,128,32]{2,3,1,0:T(8,128)(2,1)S(1)} copy-done((bf16[48,1,128,32]{2,3,1,0:T(8,128)(2,1)S(1)}, bf16[48,1,128,32]{2,3,1,0:T(8,128)(2,1)}, u32[]{:S(2)}) %copy-start.14) | copy-done | bytes 393240
  1.7 1.1 %sequence.1 = (bf16[32,48,128]{2,1,0:T(8,128)(2,1)S(1)}, bf16[48,128]{1,0:T(8,128)(2,1)S(1)}) custom-call(s32[1]{0:T(128)} %bitcast.me_ref, bf16[48,32,128]{2,1,0:T(8,128)(2,1)S(1)} %bitcast.28), custom_call_target="tpu_custom_call" | custom-call | flops 8000000000 | bytes 28000000 | tf_op jit(solution)/shard_map/sequence/pallas_call | solution.py:550
  2.8 0.5 collective-permute-start
  3.4 0.2 weights.1
  3.6 7.0 %collective-permute-done.tail_ref = bf16[48,128]{1,0:T(8,128)(2,1)S(1)} collective-permute-done((bf16[48,128]{1,0:T(8,128)(2,1)S(1)}, bf16[48,128]{1,0:T(8,128)(2,1)S(1)}, u32[]{:S(2)}, u32[]{:S(2)}) %collective-permute-start) | collective-permute-done | bytes 12320 | tf_op jit(solution)/shard_map/ppermute | solution.py:719
  10.6 3.0 %states.2 = (bf16[32,96,128]{2,1,0:T(8,128)(2,1)S(1)}, bf16[32,64,128]{2,1,0:T(8,128)(2,1)S(1)}, f32[32,16,128]{2,1,0:T(8,128)S(1)}, f32[32,72,128]{2,1,0:T(8,128)S(1)}, f32[56,128]{1,0:T(8,128)S(1)}) custom-call(bf16[32,48,128]{2,1,0:T(8,128)(2,1)S(1)} %get-tuple-element.118.hid_ref, bf16[48,128]{1,0:T(8,128)(2,1)S(1)} %collective-permute-done.tail_ref, ...), custom_call_target="tpu_custom_call" | custom-call | tf_op jit(solution)/shard_map/states/pallas_call | solution.py:587
  13.6 1.2 %collective-permute-done.1.refs_1_ = f32[56,128]{1,0:T(8,128)S(1)} collective-permute-done((f32[56,128]{1,0:T(8,128)S(1)}, f32[56,128]{1,0:T(8,128)S(1)}, u32[]{:S(2)}, u32[]{:S(2)}) %collective-permute-start.1) | collective-permute-done | bytes 28704 | tf_op jit(solution)/shard_map/ppermute | solution.py:526
  15.0 2.9 %collective-permute-start.4 = (f32[56,128]{1,0:T(8,128)S(1)}, f32[56,128]{1,0:T(8,128)S(1)}, u32[]{:S(2)}, u32[]{:S(2)}) collective-permute-start(f32[56,128]{1,0:T(8,128)S(1)} %get-tuple-element.103.refs_0_), channel_id=1, source_target_pairs={{0,7},{1,6},{2,5},{3,4},{4,3},{5,2},{6,1},{7,0},{8,15},{9,14},{10,... | collective-permute-start | bytes 86024 | tf_op jit(solution)/shard_map/ppermute | solution.py:526
  17.9 2.2 %local.4 = (f32[32,96,128]{2,1,0:T(8,128)S(1)}, f32[32,96,128]{2,1,0:T(8,128)S(1)}, bf16[32,64,128]{2,1,0:T(8,128)(2,1)S(1)}) custom-call(bf16[32,48,128]{2,1,0:T(8,128)(2,1)S(1)} %get-tuple-element.118.hid_ref, bf16[48,128]{1,0:T(8,128)(2,1)S(1)} %collective-permute-done.tail_ref, bf16[2,336,48]{2,1,0:T(8,128)(2,1)S(1)} %get-tuple-element.95.weight_ref, ...), custom_call_target="tpu_custom_call" | custom-call | tf_op jit(solution)/shard_map/local/pallas_call | solution.py:613
  20.2 0.2 collective-permute-start.5
  20.4 2.4 %collective-permute-start.6 = (f32[56,128]{1,0:T(8,128)S(1)}, f32[56,128]{1,0:T(8,128)S(1)}, u32[]{:S(2)}, u32[]{:S(2)}) collective-permute-start(f32[56,128]{1,0:T(8,128)S(1)} %get-tuple-element.117.refs_0_), channel_id=1, source_target_pairs={{0,17},{1,16},{2,19},{3,18},{4,21},{5,20},{6,23},{7,22},{8,25},{9,... | collective-permute-start | bytes 86024 | tf_op jit(solution)/shard_map/ppermute | solution.py:526
  22.8 1.6 %collective-permute-start.7 = (f32[56,128]{1,0:T(8,128)S(1)}, f32[56,128]{1,0:T(8,128)S(1)}, u32[]{:S(2)}, u32[]{:S(2)}) collective-permute-start(f32[56,128]{1,0:T(8,128)S(1)} %get-tuple-element.117.refs_0_), channel_id=1, source_target_pairs={{0,25},{1,24},{2,27},{3,26},{4,29},{5,28},{6,31},{7,30},{8,17},{9,... | collective-permute-start | bytes 86024 | tf_op jit(solution)/shard_map/ppermute | solution.py:526
  24.3 2.2 %local.5 = (f32[32,96,128]{2,1,0:T(8,128)S(1)}, f32[32,96,128]{2,1,0:T(8,128)S(1)}, bf16[32,64,128]{2,1,0:T(8,128)(2,1)S(1)}) custom-call(bf16[32,48,128]{2,1,0:T(8,128)(2,1)S(1)} %get-tuple-element.118.hid_ref, bf16[48,128]{1,0:T(8,128)(2,1)S(1)} %collective-permute-done.tail_ref, ...), custom_call_target="tpu_custom_call", output_to_operand_aliasing={{0}: (7, {}), {1}: (8, {}), {2}: (9, {})} | custom-call | tf_op jit(solution)/shard_map/local/pallas_call | solution.py:613
  26.6 1.3 %collective-permute-done.7.refs_3_ = f32[56,128]{1,0:T(8,128)S(1)} collective-permute-done((f32[56,128]{1,0:T(8,128)S(1)}, f32[56,128]{1,0:T(8,128)S(1)}, u32[]{:S(2)}, u32[]{:S(2)}) %collective-permute-start.7) | collective-permute-done | bytes 28704 | tf_op jit(solution)/shard_map/ppermute | solution.py:526
  27.9 1.8 %finish.1 = bf16[32,56,128]{2,1,0:T(8,128)(2,1)S(1)} custom-call(f32[56,128]{1,0:T(8,128)S(1)} %join.8.enter_ref, bf16[32,48,128]{2,1,0:T(8,128)(2,1)S(1)} %get-tuple-element.118.hid_ref, f32[32,96,128]{2,1,0:T(8,128)S(1)} %get-tuple-element.132.local_ref, f32[32,96,128]{2,1,0:T(8,128)S(1)} %get-tuple-element.133.gate_ref, ...), custom_call_target="tpu_custom_call" | custom-call | tf_op jit(solution)/shard_map/finish/pallas_call | solution.py:650
  29.7 17.8 %all_to_all.17.hid_ref.tail_ref = bf16[32,56,128]{2,1,0:T(8,128)(2,1)S(1)} all-to-all(bf16[32,56,128]{2,1,0:T(8,128)(2,1)S(1)} %finish.1), channel_id=1, replica_groups=mesh['row'=8,'col'=4] {'row','col'}, dimensions={0} | all-to-all | bytes 917504 | tf_op jit(solution)/shard_map/all_to_all | solution.py:722
  47.4 3.0 %states.3 = (bf16[32,96,128]{2,1,0:T(8,128)(2,1)S(1)}, bf16[32,64,128]{2,1,0:T(8,128)(2,1)S(1)}, f32[32,16,128]{2,1,0:T(8,128)S(1)}, f32[32,72,128]{2,1,0:T(8,128)S(1)}, f32[56,128]{1,0:T(8,128)S(1)}) custom-call(bf16[32,56,128]{2,1,0:T(8,128)(2,1)S(1)} %all_to_all.17.hid_ref.tail_ref, bf16[32,56,128]{2,1,0:T(8,128)(2,1)S(1)} %all_to_all.17.hid_ref.tail_ref, ...), custom_call_target="tpu_custom_call" | custom-call | tf_op jit(solution)/shard_map/states/pallas_call | solution.py:587
  50.5 1.2 %collective-permute-done.8.refs_1_ = f32[56,128]{1,0:T(8,128)S(1)} collective-permute-done((f32[56,128]{1,0:T(8,128)S(1)}, f32[56,128]{1,0:T(8,128)S(1)}, u32[]{:S(2)}, u32[]{:S(2)}) %collective-permute-start.8) | collective-permute-done | bytes 28704 | tf_op jit(solution)/shard_map/ppermute | solution.py:526
  51.7 1.0 %collective-permute-start.10 = (f32[56,128]{1,0:T(8,128)S(1)}, f32[56,128]{1,0:T(8,128)S(1)}, u32[]{:S(2)}, u32[]{:S(2)}) collective-permute-start(f32[56,128]{1,0:T(8,128)S(1)} %get-tuple-element.142.refs_0_), channel_id=1, source_target_pairs={{0,5},{1,4},{2,7},{3,6},{4,1},{5,0},{6,3},{7,2},{8,13},{9,12},{10,... | collective-permute-start | bytes 86024 | tf_op jit(solution)/shard_map/ppermute | solution.py:526
  52.6 1.1 %collective-permute-start.11 = (f32[56,128]{1,0:T(8,128)S(1)}, f32[56,128]{1,0:T(8,128)S(1)}, u32[]{:S(2)}, u32[]{:S(2)}) collective-permute-start(f32[56,128]{1,0:T(8,128)S(1)} %get-tuple-element.142.refs_0_), channel_id=1, source_target_pairs={{0,7},{1,6},{2,5},{3,4},{4,3},{5,2},{6,1},{7,0},{8,15},{9,14},{10,... | collective-permute-start | bytes 86024 | tf_op jit(solution)/shard_map/ppermute | solution.py:526
  53.7 1.0 %collective-permute-start.9 = (f32[56,128]{1,0:T(8,128)S(1)}, f32[56,128]{1,0:T(8,128)S(1)}, u32[]{:S(2)}, u32[]{:S(2)}) collective-permute-start(f32[56,128]{1,0:T(8,128)S(1)} %get-tuple-element.142.refs_0_), channel_id=1, source_target_pairs={{0,3},{1,2},{2,1},{3,0},{4,7},{5,6},{6,5},{7,4},{8,11},{9,10},{10,... | collective-permute-start | bytes 86024 | tf_op jit(solution)/shard_map/ppermute | solution.py:526
  54.7 2.2 %local.6 = (f32[32,96,128]{2,1,0:T(8,128)S(1)}, f32[32,96,128]{2,1,0:T(8,128)S(1)}, bf16[32,64,128]{2,1,0:T(8,128)(2,1)S(1)}) custom-call(bf16[32,56,128]{2,1,0:T(8,128)(2,1)S(1)} %all_to_all.17.hid_ref.tail_ref, bf16[32,56,128]{2,1,0:T(8,128)(2,1)S(1)} %all_to_all.17.hid_ref.tail_ref, bf16[2,336,48]{2,1,0:T(8,128)(2,1)S(1)} %get-tuple-element.95.weight_ref, ...), custom_call_target="tpu_custom_call" | custom-call | tf_op jit(solution)/shard_map/local/pallas_call | solution.py:613
  57.1 1.0 %collective-permute-start.12 = (f32[56,128]{1,0:T(8,128)S(1)}, f32[56,128]{1,0:T(8,128)S(1)}, u32[]{:S(2)}, u32[]{:S(2)}) collective-permute-start(f32[56,128]{1,0:T(8,128)S(1)} %get-tuple-element.156.refs_0_), channel_id=1, source_target_pairs={{0,9},{1,8},{2,11},{3,10},{4,13},{5,12},{6,15},{7,14},{8,1},{9,0},... | collective-permute-start | bytes 86024 | tf_op jit(solution)/shard_map/ppermute | solution.py:526
  58.2 0.6 collective-permute-start.13
  58.8 2.4 %collective-permute-start.14 = (f32[56,128]{1,0:T(8,128)S(1)}, f32[56,128]{1,0:T(8,128)S(1)}, u32[]{:S(2)}, u32[]{:S(2)}) collective-permute-start(f32[56,128]{1,0:T(8,128)S(1)} %get-tuple-element.156.refs_0_), channel_id=1, source_target_pairs={{0,25},{1,24},{2,27},{3,26},{4,29},{5,28},{6,31},{7,30},{8,17},{9,... | collective-permute-start | bytes 86024 | tf_op jit(solution)/shard_map/ppermute | solution.py:526
  61.2 2.2 %local.7 = (f32[32,96,128]{2,1,0:T(8,128)S(1)}, f32[32,96,128]{2,1,0:T(8,128)S(1)}, bf16[32,64,128]{2,1,0:T(8,128)(2,1)S(1)}) custom-call(bf16[32,56,128]{2,1,0:T(8,128)(2,1)S(1)} %all_to_all.17.hid_ref.tail_ref, bf16[32,56,128]{2,1,0:T(8,128)(2,1)S(1)} %all_to_all.17.hid_ref.tail_ref, ...), custom_call_target="tpu_custom_call", output_to_operand_aliasing={{0}: (7, {}), {1}: (8, {}), {2}: (9, {})} | custom-call | tf_op jit(solution)/shard_map/local/pallas_call | solution.py:613
  63.5 0.4 collective-permute-done.14.refs_3_
  63.9 2.6 %heads.1 = (bf16[32,48,128]{2,1,0:T(8,128)(2,1)S(1)}, f32[14,32,128]{2,1,0:T(8,128)S(1)}, f32[32,128]{1,0:T(8,128)}) custom-call(f32[56,128]{1,0:T(8,128)S(1)} %join.11.enter_ref, bf16[32,56,128]{2,1,0:T(8,128)(2,1)S(1)} %all_to_all.17.hid_ref.tail_ref, f32[32,96,128]{2,1,0:T(8,128)S(1)} %get-tuple-element.171.local_ref, ...), custom_call_target="tpu_custom_call" | custom-call | tf_op jit(solution)/shard_map/heads/pallas_call | solution.py:670
  66.6 4.1 %all-to-all-start.1 = ((f32[32,1,128]{2,1,0:T(1,128)}), f32[32,1,128]{2,1,0:T(1,128)S(1)}, u32[]{:S(2)}, u32[]{:S(2)}) async-start(f32[32,1,128]{2,1,0:T(1,128)} %bitcast.10), calls=%async_computation.1 | async-start | bytes 32768 | tf_op jit(solution)/shard_map/all_to_all | solution.py:727
  70.6 1.7 %gradient.1 = (bf16[48,32,128]{2,1,0:T(8,128)(2,1)}, f32[14,32,128]{2,1,0:T(8,128)}) custom-call(bf16[32,48,128]{2,1,0:T(8,128)(2,1)S(1)} %get-tuple-element.176.after_ref, f32[14,32,128]{2,1,0:T(8,128)S(1)} %get-tuple-element.177.logits_ref, s32[32,128]{1,0:T(8,128)S(1)} %bitcast.24, s32[14,32,128]{2,1,0:T(8,128)S(1)} %bitcast.21), custom_call_target="tpu_custom_call" | custom-call | flops 4000000000 | bytes 14000000 | tf_op jit(solution)/shard_map/gradient/pallas_call | solution.py:688
  72.3 5.5 %all-to-all-done.1 = f32[32,1,128]{2,1,0:T(1,128)S(1)} async-done(((f32[32,1,128]{2,1,0:T(1,128)}), f32[32,1,128]{2,1,0:T(1,128)S(1)}, u32[]{:S(2)}, u32[]{:S(2)}) %all-to-all-start.1) | async-done | bytes 16416 | tf_op jit(solution)/shard_map/all_to_all | solution.py:727
  77.8 0.7 multiply_reduce_fusion
  (51 shorter events, 0.6 us)
Async XLA Ops:
  0.6 1.0 %copy-start.14 = (bf16[48,1,128,32]{2,3,1,0:T(8,128)(2,1)S(1)}, bf16[48,1,128,32]{2,3,1,0:T(8,128)(2,1)}, u32[]{:S(2)}) copy-start(bf16[48,1,128,32]{2,3,1,0:T(8,128)(2,1)} %param.15) | copy-start | bytes 1179652
  1.6 1.7 %copy-start.2 = (bf16[2,320,48]{1,2,0:T(8,128)(2,1)S(1)}, bf16[2,320,48]{1,2,0:T(8,128)(2,1)}, u32[]{:S(2)}) copy-start(bf16[2,320,48]{1,2,0:T(8,128)(2,1)} %param.17) | copy-start | bytes 184324
  1.6 1.7 %copy-start.4 = (f32[2,224,4]{1,2,0:T(4,128)S(1)}, f32[2,224,4]{1,2,0:T(4,128)}, u32[]{:S(2)}) copy-start(f32[2,224,4]{1,2,0:T(4,128)} %param.21) | copy-start | bytes 21508
  1.6 1.7 %copy-start.6 = (f32[2,224]{1,0:T(2,128)S(1)}, f32[2,224]{1,0:T(2,128)}, u32[]{:S(2)}) copy-start(f32[2,224]{1,0:T(2,128)} %conv_bias_ref.1) | copy-start | bytes 5380
  1.6 1.7 %copy-start.7 = (bf16[2,3,48]{2,0,1:T(2,128)(2,1)S(1)}, bf16[2,3,48]{2,0,1:T(2,128)(2,1)}, u32[]{:S(2)}) copy-start(bf16[2,3,48]{2,0,1:T(2,128)(2,1)} %param.18) | copy-start | bytes 1732
  1.6 1.7 %copy-start.8 = (f32[2,48]{1,0:T(2,128)S(1)}, f32[2,48]{1,0:T(2,128)}, u32[]{:S(2)}) copy-start(f32[2,48]{1,0:T(2,128)} %gain_ref.1) | copy-start | bytes 1156
  1.7 1.7 %copy-start.9 = (f32[2,3]{1,0:T(2,128)S(1)}, f32[2,3]{1,0:T(2,128)}, u32[]{:S(2)}) copy-start(f32[2,3]{1,0:T(2,128)} %dt_bias_ref.1) | copy-start | bytes 76
  1.7 1.7 %copy-start.10 = (f32[2,3]{1,0:T(2,128)S(1)}, f32[2,3]{1,0:T(2,128)}, u32[]{:S(2)}) copy-start(f32[2,3]{1,0:T(2,128)} %rate_ref.1) | copy-start | bytes 76
  1.7 1.7 %copy-start.11 = (f32[2,3]{1,0:T(2,128)S(1)}, f32[2,3]{1,0:T(2,128)}, u32[]{:S(2)}) copy-start(f32[2,3]{1,0:T(2,128)} %skip_ref.1) | copy-start | bytes 76
  1.7 1.7 %copy-start.12 = (f32[2,96]{1,0:T(2,128)S(1)}, f32[2,96]{1,0:T(2,128)}, u32[]{:S(2)}) copy-start(f32[2,96]{1,0:T(2,128)} %out_gain_ref.1) | copy-start | bytes 2308
  2.8 7.8 %collective-permute-start = (bf16[48,128]{1,0:T(8,128)(2,1)S(1)}, bf16[48,128]{1,0:T(8,128)(2,1)S(1)}, u32[]{:S(2)}, u32[]{:S(2)}) collective-permute-start(bf16[48,128]{1,0:T(8,128)(2,1)S(1)} %get-tuple-element.94), channel_id=1, source_target_pairs={{0,1},{1,2},{2,3},{3,4},{4,5},{5,6},{6,7},{7,8},{8,9},{9,10},{10,1... | collective-permute-start | bytes 36872 | tf_op jit(solution)/shard_map/ppermute | solution.py:719
  13.6 1.2 %collective-permute-start.1 = (f32[56,128]{1,0:T(8,128)S(1)}, f32[56,128]{1,0:T(8,128)S(1)}, u32[]{:S(2)}, u32[]{:S(2)}) collective-permute-start(f32[56,128]{1,0:T(8,128)S(1)} %get-tuple-element.97.refs_0_), channel_id=1, source_target_pairs={{0,1},{1,0},{2,3},{3,2},{4,5},{5,4},{6,7},{7,6},{8,9},{9,8},{10,11... | collective-permute-start | bytes 86024 | tf_op jit(solution)/shard_map/ppermute | solution.py:526
  14.9 5.3 %collective-permute-start.2 = (f32[56,128]{1,0:T(8,128)S(1)}, f32[56,128]{1,0:T(8,128)S(1)}, u32[]{:S(2)}, u32[]{:S(2)}) collective-permute-start(f32[56,128]{1,0:T(8,128)S(1)} %get-tuple-element.103.refs_0_), channel_id=1, source_target_pairs={{0,3},{1,2},{2,1},{3,0},{4,7},{5,6},{6,5},{7,4},{8,11},{9,10},{10,... | collective-permute-start | bytes 86024 | tf_op jit(solution)/shard_map/ppermute | solution.py:526
  14.9 5.2 %collective-permute-start.3 = (f32[56,128]{1,0:T(8,128)S(1)}, f32[56,128]{1,0:T(8,128)S(1)}, u32[]{:S(2)}, u32[]{:S(2)}) collective-permute-start(f32[56,128]{1,0:T(8,128)S(1)} %get-tuple-element.103.refs_0_), channel_id=1, source_target_pairs={{0,5},{1,4},{2,7},{3,6},{4,1},{5,0},{6,3},{7,2},{8,13},{9,12},{10,... | collective-permute-start | bytes 86024 | tf_op jit(solution)/shard_map/ppermute | solution.py:526
  15.0 5.1 %collective-permute-start.4 = (f32[56,128]{1,0:T(8,128)S(1)}, f32[56,128]{1,0:T(8,128)S(1)}, u32[]{:S(2)}, u32[]{:S(2)}) collective-permute-start(f32[56,128]{1,0:T(8,128)S(1)} %get-tuple-element.103.refs_0_), channel_id=1, source_target_pairs={{0,7},{1,6},{2,5},{3,4},{4,3},{5,2},{6,1},{7,0},{8,15},{9,14},{10,... | collective-permute-start | bytes 86024 | tf_op jit(solution)/shard_map/ppermute | solution.py:526
  20.2 7.7 %copy-start.1 = (bf16[2,48,96]{2,1,0:T(8,128)(2,1)S(1)}, bf16[2,48,96]{2,1,0:T(8,128)(2,1)}, u32[]{:S(2)}) copy-start(bf16[2,48,96]{2,1,0:T(8,128)(2,1)} %out_proj_ref.3) | copy-start | bytes 55300
  20.2 6.3 %collective-permute-start.5 = (f32[56,128]{1,0:T(8,128)S(1)}, f32[56,128]{1,0:T(8,128)S(1)}, u32[]{:S(2)}, u32[]{:S(2)}) collective-permute-start(f32[56,128]{1,0:T(8,128)S(1)} %get-tuple-element.117.refs_0_), channel_id=1, source_target_pairs={{0,9},{1,8},{2,11},{3,10},{4,13},{5,12},{6,15},{7,14},{8,1},{9,0},... | collective-permute-start | bytes 86024 | tf_op jit(solution)/shard_map/ppermute | solution.py:526
  20.4 6.1 %collective-permute-start.6 = (f32[56,128]{1,0:T(8,128)S(1)}, f32[56,128]{1,0:T(8,128)S(1)}, u32[]{:S(2)}, u32[]{:S(2)}) collective-permute-start(f32[56,128]{1,0:T(8,128)S(1)} %get-tuple-element.117.refs_0_), channel_id=1, source_target_pairs={{0,17},{1,16},{2,19},{3,18},{4,21},{5,20},{6,23},{7,22},{8,25},{9,... | collective-permute-start | bytes 86024 | tf_op jit(solution)/shard_map/ppermute | solution.py:526
  22.8 5.1 %collective-permute-start.7 = (f32[56,128]{1,0:T(8,128)S(1)}, f32[56,128]{1,0:T(8,128)S(1)}, u32[]{:S(2)}, u32[]{:S(2)}) collective-permute-start(f32[56,128]{1,0:T(8,128)S(1)} %get-tuple-element.117.refs_0_), channel_id=1, source_target_pairs={{0,25},{1,24},{2,27},{3,26},{4,29},{5,28},{6,31},{7,30},{8,17},{9,... | collective-permute-start | bytes 86024 | tf_op jit(solution)/shard_map/ppermute | solution.py:526
  50.4 1.2 %collective-permute-start.8 = (f32[56,128]{1,0:T(8,128)S(1)}, f32[56,128]{1,0:T(8,128)S(1)}, u32[]{:S(2)}, u32[]{:S(2)}) collective-permute-start(f32[56,128]{1,0:T(8,128)S(1)} %get-tuple-element.136.refs_0_), channel_id=1, source_target_pairs={{0,1},{1,0},{2,3},{3,2},{4,5},{5,4},{6,7},{7,6},{8,9},{9,8},{10,11... | collective-permute-start | bytes 86024 | tf_op jit(solution)/shard_map/ppermute | solution.py:526
  51.7 5.3 %collective-permute-start.10 = (f32[56,128]{1,0:T(8,128)S(1)}, f32[56,128]{1,0:T(8,128)S(1)}, u32[]{:S(2)}, u32[]{:S(2)}) collective-permute-start(f32[56,128]{1,0:T(8,128)S(1)} %get-tuple-element.142.refs_0_), channel_id=1, source_target_pairs={{0,5},{1,4},{2,7},{3,6},{4,1},{5,0},{6,3},{7,2},{8,13},{9,12},{10,... | collective-permute-start | bytes 86024 | tf_op jit(solution)/shard_map/ppermute | solution.py:526
  52.6 4.3 %collective-permute-start.11 = (f32[56,128]{1,0:T(8,128)S(1)}, f32[56,128]{1,0:T(8,128)S(1)}, u32[]{:S(2)}, u32[]{:S(2)}) collective-permute-start(f32[56,128]{1,0:T(8,128)S(1)} %get-tuple-element.142.refs_0_), channel_id=1, source_target_pairs={{0,7},{1,6},{2,5},{3,4},{4,3},{5,2},{6,1},{7,0},{8,15},{9,14},{10,... | collective-permute-start | bytes 86024 | tf_op jit(solution)/shard_map/ppermute | solution.py:526
  53.7 3.4 %collective-permute-start.9 = (f32[56,128]{1,0:T(8,128)S(1)}, f32[56,128]{1,0:T(8,128)S(1)}, u32[]{:S(2)}, u32[]{:S(2)}) collective-permute-start(f32[56,128]{1,0:T(8,128)S(1)} %get-tuple-element.142.refs_0_), channel_id=1, source_target_pairs={{0,3},{1,2},{2,1},{3,0},{4,7},{5,6},{6,5},{7,4},{8,11},{9,10},{10,... | collective-permute-start | bytes 86024 | tf_op jit(solution)/shard_map/ppermute | solution.py:526
  57.1 6.3 %collective-permute-start.12 = (f32[56,128]{1,0:T(8,128)S(1)}, f32[56,128]{1,0:T(8,128)S(1)}, u32[]{:S(2)}, u32[]{:S(2)}) collective-permute-start(f32[56,128]{1,0:T(8,128)S(1)} %get-tuple-element.156.refs_0_), channel_id=1, source_target_pairs={{0,9},{1,8},{2,11},{3,10},{4,13},{5,12},{6,15},{7,14},{8,1},{9,0},... | collective-permute-start | bytes 86024 | tf_op jit(solution)/shard_map/ppermute | solution.py:526
  58.2 5.3 %collective-permute-start.13 = (f32[56,128]{1,0:T(8,128)S(1)}, f32[56,128]{1,0:T(8,128)S(1)}, u32[]{:S(2)}, u32[]{:S(2)}) collective-permute-start(f32[56,128]{1,0:T(8,128)S(1)} %get-tuple-element.156.refs_0_), channel_id=1, source_target_pairs={{0,17},{1,16},{2,19},{3,18},{4,21},{5,20},{6,23},{7,22},{8,25},{9,... | collective-permute-start | bytes 86024 | tf_op jit(solution)/shard_map/ppermute | solution.py:526
  58.8 5.1 %collective-permute-start.14 = (f32[56,128]{1,0:T(8,128)S(1)}, f32[56,128]{1,0:T(8,128)S(1)}, u32[]{:S(2)}, u32[]{:S(2)}) collective-permute-start(f32[56,128]{1,0:T(8,128)S(1)} %get-tuple-element.156.refs_0_), channel_id=1, source_target_pairs={{0,25},{1,24},{2,27},{3,26},{4,29},{5,28},{6,31},{7,30},{8,17},{9,... | collective-permute-start | bytes 86024 | tf_op jit(solution)/shard_map/ppermute | solution.py:526
  61.2 2.7 %copy-start = (s32[14,1,32,128]{3,2,1,0:T(8,128)S(1)}, s32[14,1,32,128]{3,2,1,0:T(8,128)}, u32[]{:S(2)}) copy-start(s32[14,1,32,128]{3,2,1,0:T(8,128)} %param.29) | copy-start | bytes 688132
  61.2 2.7 %copy-start.3 = (s32[1,32,128]{2,1,0:T(8,128)S(1)}, s32[1,32,128]{2,1,0:T(8,128)}, u32[]{:S(2)}) copy-start(s32[1,32,128]{2,1,0:T(8,128)} %param.28) | copy-start | bytes 49156
  61.2 2.7 %copy-start.5 = (bf16[14,48]{1,0:T(8,128)(2,1)S(1)}, bf16[14,48]{1,0:T(8,128)(2,1)}, u32[]{:S(2)}) copy-start(bf16[14,48]{1,0:T(8,128)(2,1)} %head_ref.1) | copy-start | bytes 4036
  61.2 2.7 %copy-start.13 = (f32[14]{0:T(128)S(1)}, f32[14]{0:T(128)}, u32[]{:S(2)}) copy-start(f32[14]{0:T(128)} %param.27) | copy-start | bytes 172
  66.6 11.2 %all-to-all-start.1 = ((f32[32,1,128]{2,1,0:T(1,128)}), f32[32,1,128]{2,1,0:T(1,128)S(1)}, u32[]{:S(2)}, u32[]{:S(2)}) async-start(f32[32,1,128]{2,1,0:T(1,128)} %bitcast.10), calls=%async_computation.1 | async-start | bytes 32768 | tf_op jit(solution)/shard_map/all_to_all | solution.py:727

commit v4 on v3

--- a/solution.py
+++ b/solution.py
@@ -177,40 +177,68 @@
         out_ref[x] = plane_ref[x * rows : (x + 1) * rows, :].astype(bf16)
 
 
-def convolve(proj_ref, rows, cols, first, outs):
+def convolve(proj_ref, shift_ref, rows, cols, first, outs, rotated=0):
     group = proj_ref.shape[1] // SCAN_BLOCK - 1
+    batch = min(16, group)
+    high = 32
     lags = range(1, tap_count)
-    lane = lax.broadcasted_iota(jnp.int32, (16, SCAN_BLOCK), 1)
-    for r in range(0, rows, 16):
+    lane = lax.broadcasted_iota(jnp.int32, (high, SCAN_BLOCK), 1)
+    for r in range(0, rows, high):
         half = [
-            jnp.broadcast_to(cols[first + r : first + r + 16, k : k + 1], (16, SCAN_BLOCK)) for k in range(tap_count + 1)
+            jnp.broadcast_to(cols[first + r : first + r + high, k : k + 1], (high, SCAN_BLOCK))
+            for k in range(tap_count + 1)
         ]
-        ref, at = next((ref, r - low) for ref, low, high in outs if low <= r < high)
-        before = proj_ref[r : r + 16, span(0)]
-        before = [pltpu.roll(before, lag, 1) for lag in lags]
-        for u in range(group):
-            conv_in = proj_ref[r : r + 16, span(u + 1)]
-            now = [pltpu.roll(conv_in, lag, 1) for lag in lags]
-            total = half[tap_count]
-            for lag in reversed(lags):
-                shifted = jnp.where(lane < lag, before[lag - 1], now[lag - 1])
-                total = total + half[tap_count - 1 - lag] * shifted
-            total = total + half[tap_count - 1] * conv_in
-            ref[u, at : at + 16, :] = half_silu(total).astype(bf16)
-            before = now
+        ref, at = next((ref, r - low) for ref, low, end in outs if low <= r < end)
+        if r >= rows - rotated:
+            before = proj_ref[r : r + high, span(0)].astype(f32)
+            before = [pltpu.roll(before, lag, 1) for lag in lags]
+            for u in range(group):
+                conv_in = proj_ref[r : r + high, span(u + 1)].astype(f32)
+                now = [pltpu.roll(conv_in, lag, 1) for lag in lags]
+                total = half[tap_count]
+                for lag in reversed(lags):
+                    shifted = jnp.where(lane < lag, before[lag - 1], now[lag - 1])
+                    total = total + half[tap_count - 1 - lag] * shifted
+                total = total + half[tap_count - 1] * conv_in
+                ref[u, at : at + high, :] = half_silu(total).astype(bf16)
+                before = now
+            continue
+        for b in range(0, group, batch):
+            pairs = [proj_ref[r : r + high, span(u, 2)] for u in range(b, b + batch)]
+            moved = project(jnp.concatenate(pairs, axis=0), shift_ref[...])
+            for i in range(batch):
+                total = half[tap_count]
+                for lag in reversed(range(tap_count)):
+                    total = total + half[tap_count - 1 - lag] * moved[i * high : (i + 1) * high, span(lag)]
+                ref[b + i, at : at + high, :] = half_silu(total).astype(bf16)
     proj_ref[:, span(0)] = proj_ref[:, span(group)]
 
 
-def sequence_kernel(size, me_ref, volume_ref, hid_ref, tail_ref, turn_ref, tile_ref):
+def tail_kernel(size, me_ref, volume_ref, tail_ref, part_ref):
+    model, cells_x, cells_y = volume_ref.shape
+    per = LANES // cells_x
+    last = jnp.where(lax.broadcasted_iota(jnp.int32, (16, cells_y), 1) == cells_y - 1, 1.0, 0.0).astype(bf16)
+    row = contract(last, volume_ref[...].reshape(model * cells_x, cells_y), 1)[0:1]
+    rows = jnp.concatenate([row[:, c * LANES : (c + 1) * LANES] for c in range(model // per)], axis=0)
+    for j in range(per):
+        shift = LANES - (j + 1) * cells_x
+        part_ref[pl.ds(j, model // per, stride=per), :] = pltpu.roll(rows, shift, 1) if shift else rows
+    tail = part_ref[...]
+    tail_ref[...] = jnp.where(me_ref[0] == size - 1, jnp.zeros_like(tail), tail).astype(bf16)
+
+
+def sequence_kernel(volume_ref, hid_ref, turn_ref, tile_ref):
     to_sequence(volume_ref, hid_ref, turn_ref, tile_ref)
-    last = hid_ref[hid_ref.shape[0] - 1]
-    tail_ref[...] = jnp.where(me_ref[0] == size - 1, jnp.zeros_like(last), last)
 
 
 def weights_kernel(
-    in_ref, dt_ref, taps_ref, conv_bias_ref, gain_ref, dt_bias_ref, rate_ref, skip_ref, out_gain_ref, weight_ref, cols_ref
+    in_ref, dt_ref, taps_ref, conv_bias_ref, gain_ref, dt_bias_ref, rate_ref, skip_ref, out_gain_ref, weight_ref, cols_ref,
+    shift_ref,
 ):
     model = in_ref.shape[1]
+    source = lax.broadcasted_iota(jnp.int32, shift_ref.shape, 0) - SCAN_BLOCK
+    target = lax.broadcasted_iota(jnp.int32, shift_ref.shape, 1)
+    shift_ref[...] = jnp.where(source == target % SCAN_BLOCK - target // SCAN_BLOCK, 1.0, 0.0).astype(bf16)
     lanes = cols_ref.shape[1]
     for layer in range(in_ref.shape[0]):
         here = slice(layer, layer + 1)
@@ -227,8 +255,8 @@
 
 
 def state_kernel(
-    layer, heads, group, hid_ref, tail_ref, weight_ref, cols_ref, inner_ref, write_ref, dec_ref, state_ref, total_ref,
-    proj_ref, carry_ref,
+    layer, heads, group, hid_ref, tail_ref, weight_ref, cols_ref, shift_ref, inner_ref, write_ref, dec_ref, state_ref,
+    total_ref, proj_ref, carry_ref,
 ):
     model = weight_ref.shape[2]
     inner = inner_ref.shape[1]
@@ -241,7 +269,7 @@
     gain_col = cols[:model, 5:6]
     head_cols = cols[:8, 6:8]
     carry_ref[...] = jnp.zeros_like(carry_ref)
-    proj_ref[:, span(0)] = rounded(project(weight, normalise(tail_tile(tail_ref, model), gain_col))[:rows])
+    proj_ref[:, span(0)] = project(weight, normalise(tail_tile(tail_ref, model), gain_col))[:rows].astype(bf16)
     lane = lax.broadcasted_iota(jnp.int32, (1, LANES), 1)
     alls = (hid_ref, inner_ref, write_ref, dec_ref, state_ref)
 
@@ -250,7 +278,7 @@
         dt_raw = []
         for q in range(0, group, wide):
             projected = project(weight, normalise(side_by_side(hid_ref, q, wide, model), gain_col))
-            proj_ref[:, span(q + 1, wide)] = rounded(projected[:rows])
+            proj_ref[:, span(q + 1, wide)] = projected[:rows].astype(bf16)
             dt_raw.append(projected[rows : rows + 8])
         step = jnp.concatenate(dt_raw, axis=1) + head_cols[:, 0:1]
         step = jnp.maximum(step, 0.0) + jnp.log1p(jnp.exp(-jnp.abs(step)))
@@ -270,7 +298,7 @@
         for u in range(group):
             dec_ref[u, 0:8, :] = cum[8 * u : 8 * u + 8]
             dec_ref[u, 8:16, :] = step[8 * u : 8 * u + 8]
-        convolve(proj_ref, rows, cols, 0, [(inner_ref, 0, inner), (write_ref, inner, rows)])
+        convolve(proj_ref, shift_ref, rows, cols, 0, [(inner_ref, 0, inner), (write_ref, inner, rows)], 32)
         decay_rows, block_states = [], []
         for u in range(group):
             row = last[8 * u + heads - 1 : 8 * u + heads]
@@ -295,7 +323,8 @@
 
 
 def local_kernel(
-    layer, heads, first, count, group, hid_ref, tail_ref, weight_ref, cols_ref, inner_ref, write_ref, dec_ref, *rest
+    layer, heads, first, count, group, hid_ref, tail_ref, weight_ref, cols_ref, shift_ref, inner_ref, write_ref, dec_ref,
+    *rest
 ):
     local_ref, gate_ref, read_ref, proj_ref, score_ref, weights_ref = rest[-6:]
     model = weight_ref.shape[2]
@@ -308,7 +337,7 @@
     gain_col = cols[:model, 5:6]
     skip_cols = cols[:8, 8:9]
     before = hid_ref[first - 1][:model] if first else tail_tile(tail_ref, model)
-    proj_ref[:, span(0)] = rounded(project(weight[inner:], normalise(before, gain_col)))
+    proj_ref[:, span(0)] = project(weight[inner:], normalise(before, gain_col)).astype(bf16)
     source = lax.broadcasted_iota(jnp.int32, (SCAN_BLOCK, SCAN_BLOCK), 0)
     target = lax.broadcasted_iota(jnp.int32, (SCAN_BLOCK, SCAN_BLOCK), 1)
     causal = source <= target
@@ -320,12 +349,12 @@
             r.at[pl.ds(first + g * group, group)] for r in alls
         )
         for q in range(0, group, wide):
-            projected = rounded(project(weight, normalise(side_by_side(hid_ref, q, wide, model), gain_col)))
+            projected = project(weight, normalise(side_by_side(hid_ref, q, wide, model), gain_col)).astype(bf16)
             proj_ref[:, span(q + 1, wide)] = projected[inner:]
-            gate = half_silu(0.5 * projected[:inner])
+            gate = half_silu(0.5 * projected[:inner].astype(f32))
             for u in range(wide):
                 gate_ref[q + u] = gate[:, span(u)]
-        convolve(proj_ref, state, cols, inner + state, [(read_ref, 0, state)])
+        convolve(proj_ref, shift_ref, state, cols, inner + state, [(read_ref, 0, state)])
         cum = jnp.concatenate([dec_ref[u, 0:8, :] for u in range(group)], axis=0)
         step = jnp.concatenate([dec_ref[u, 8:16, :] for u in range(group)], axis=0)
         source_cols = (cum - jnp.log(step)) * log2e
@@ -399,73 +428,51 @@
     to_planes(tile_ref, out_ref, turn_ref, plane_ref, model, cells_x)
 
 
-def softmax_parts(logits_ref, labels_ref, distance_ref, here):
-    classes = logits_ref.shape[0]
-    logits = logits_ref[:, here, :]
-    peak = jnp.max(logits, axis=0)
-    shifted = jnp.exp(logits - peak[None])
-    partition = jnp.sum(shifted, axis=0)
-    probability = shifted / partition[None]
-    weighted = probability * (distance_ref[:, here, :].astype(f32) * (1.0 / dist_unit))
-    expect = jnp.sum(weighted, axis=0)
-    hot = labels_ref[here, :][None] == lax.broadcasted_iota(jnp.int32, logits.shape, 0)
-    return logits, peak, partition, probability, weighted, expect, hot
-
-
-def tiles_of(count, body):
-    if count <= 32:
-        for z in range(0, count, 8):
-            body(pl.ds(z, 8))
-    else:
-        pl.loop(0, count // 8)(lambda z: body(pl.ds(pl.multiple_of(z * 8, 8), 8)))
-
-
 def head_kernel(
-    layer, heads, group, enter_ref, hid_ref, local_ref, gate_ref, read_ref, dec_ref, state_ref, cols_ref, out_proj_ref,
-    head_ref, bias_ref, labels_ref, distance_ref, after_ref, logits_ref, loss_ref, gated_ref, square_ref, logit_scr,
-    sum_scr,
+    layer, heads, group, size, me_ref, enter_ref, hid_ref, local_ref, gate_ref, read_ref, dec_ref, state_ref, cols_ref,
+    out_proj_ref, head_ref, bias_ref, labels_ref, distance_ref, features_ref, grad_ref, loss_ref, gated_ref, square_ref,
+    after_ref, feature_scr, logit_scr, sum_scr,
 ):
     count = hid_ref.shape[0]
     classes = distance_ref.shape[0]
+    model = out_proj_ref.shape[1]
     inner = local_ref.shape[1]
     alls = (hid_ref, local_ref, gate_ref, read_ref, dec_ref, state_ref)
     enter = unpack(enter_ref[...], heads)
     out_gain = cols_ref[layer, :inner, 9:10]
     bias = columns(bias_ref[...])[:classes, 0:1]
+    sum_scr[...] = jnp.zeros_like(sum_scr)
 
     def step_group(g):
         def take(u, result):
-            after_ref[g * group + u] = result
-            logit_scr[pl.ds(u, classes, stride=group), :] = project(head_ref[...], result) + bias
+            after_ref[u] = result
+            feature_scr[pl.ds(u, model, stride=group), :] = result.astype(f32)
 
         refs = tuple(r.at[pl.ds(g * group, group)] for r in alls)
         finish_group(heads, enter, refs, out_gain, out_proj_ref[layer], gated_ref, square_ref, take)
+        for q in range(0, group, wide):
+            logits = project(head_ref[...], side_by_side(after_ref, q, wide)) + bias
+            for u in range(wide):
+                logit_scr[pl.ds(q + u, classes, stride=group), :] = logits[:, span(u)]
         at = g * group if isinstance(g, int) else pl.multiple_of(g * group, group)
-        logits_ref[:, pl.ds(at, group), :] = logit_scr[...].reshape(classes, group, SCAN_BLOCK)
+        features_ref[:, pl.ds(at, group), :] = feature_scr[...].reshape(model, group, SCAN_BLOCK).astype(bf16)
+        for z in range(0, group, 8):
+            here = pl.ds(at + z, 8)
+            logits = jnp.stack([logit_scr[c * group + z : c * group + z + 8, :] for c in range(classes)], axis=0)
+            peak = jnp.max(logits, axis=0)
+            shifted = jnp.exp(logits - peak[None])
+            partition = jnp.sum(shifted, axis=0)
+            probability = shifted / partition[None]
+            weighted = probability * (distance_ref[:, here, :].astype(f32) * (1.0 / dist_unit))
+            expect = jnp.sum(weighted, axis=0)
+            hot = labels_ref[here, :][None] == lax.broadcasted_iota(jnp.int32, logits.shape, 0)
+            chosen = jnp.sum(jnp.where(hot, logits, 0.0), axis=0)
+            grad_ref[:, here, :] = probability - jnp.where(hot, 1.0, 0.0) + weighted - probability * expect[None]
+            sum_scr[...] += peak + jnp.log(partition) - chosen + expect
 
     repeat(count // group, step_group)
-    sum_scr[...] = jnp.zeros_like(sum_scr)
-
-    def losses(here):
-        logits, peak, partition, _, _, expect, hot = softmax_parts(logits_ref, labels_ref, distance_ref, here)
-        chosen = jnp.sum(jnp.where(hot, logits, 0.0), axis=0)
-        sum_scr[...] += peak + jnp.log(partition) - chosen + expect
-
-    tiles_of(count, losses)
-    loss_ref[...] = jnp.broadcast_to(jnp.sum(sum_scr[...], axis=0, keepdims=True), loss_ref.shape)
-
-
-def gradient_kernel(after_ref, logits_ref, labels_ref, distance_ref, features_ref, grad_ref, feature_scr):
-    count, model, _ = after_ref.shape
-    for u in range(count):
-        feature_scr[pl.ds(u, model, stride=count), :] = after_ref[u].astype(f32)
-    features_ref[...] = feature_scr[...].reshape(model, count, SCAN_BLOCK).astype(bf16)
-
-    def gradients(here):
-        _, _, _, probability, weighted, expect, hot = softmax_parts(logits_ref, labels_ref, distance_ref, here)
-        grad_ref[:, here, :] = probability - jnp.where(hot, 1.0, 0.0) + weighted - probability * expect[None]
-
-    tiles_of(count, gradients)
+    weight = 1.0 + 3.0 * me_ref[0].astype(f32) / (size - 1.0)
+    loss_ref[...] = jnp.broadcast_to(jnp.sum(sum_scr[...], axis=0, keepdims=True) * weight, loss_ref.shape)
 
 
 def params(size=vmem_bytes):
@@ -544,14 +551,28 @@
     return jax.ShapeDtypeStruct((count, rows, SCAN_BLOCK), kind)
 
 
-def call_sequence(me, size, volume):
+def call_tail(me, size, volume):
+    model = volume.shape[0]
+    return pl.pallas_call(
+        functools.partial(tail_kernel, size),
+        in_specs=[pl.BlockSpec(memory_space=pltpu.SMEM), vmem],
+        out_specs=vmem,
+        out_shape=jax.ShapeDtypeStruct((model, SCAN_BLOCK), bf16),
+        scratch_shapes=[pltpu.VMEM((model, LANES), f32)],
+        compiler_params=params(4 * 1024 * 1024),
+        cost_estimate=cost(2),
+        name="tail",
+    )(me, volume)
+
+
+def call_sequence(volume):
     model, cells_x, cells_y = volume.shape
     count = cells_x * cells_y // SCAN_BLOCK
     return pl.pallas_call(
-        functools.partial(sequence_kernel, size),
-        in_specs=[pl.BlockSpec(memory_space=pltpu.SMEM), vmem],
-        out_specs=[vmem] * 2,
-        out_shape=[tile(count, model, bf16), jax.ShapeDtypeStruct((model, SCAN_BLOCK), bf16)],
+        sequence_kernel,
+        in_specs=[vmem],
+        out_specs=vmem,
+        out_shape=tile(count, model, bf16),
         scratch_shapes=[
             pltpu.VMEM((model * cells_x // LANES, cells_y, LANES), f32),
             pltpu.VMEM((count * model, LANES), f32),
@@ -559,7 +580,7 @@
         compiler_params=params(),
         cost_estimate=cost(8),
         name="sequence",
-    )(me, volume)
+    )(volume)
 
 
 def call_weights(norm_gain, in_proj, dt_proj, dt_bias, decay_rate, conv_weight, conv_bias, skip_gain, out_gain):
@@ -567,10 +588,11 @@
     return pl.pallas_call(
         weights_kernel,
         in_specs=[vmem] * 9,
-        out_specs=[vmem] * 2,
+        out_specs=[vmem] * 3,
         out_shape=[
             jax.ShapeDtypeStruct((layers, projected + 16, model), bf16),
             jax.ShapeDtypeStruct((layers, -(-conv_bias.shape[1] // LANES) * LANES, 16), f32),
+            jax.ShapeDtypeStruct((2 * SCAN_BLOCK, tap_count * SCAN_BLOCK), bf16),
         ],
         compiler_params=params(4 * 1024 * 1024),
         name="weights",
@@ -586,7 +608,7 @@
     group = min(32, count)
     return pl.pallas_call(
         functools.partial(state_kernel, layer, heads, group),
-        in_specs=[vmem] * 4,
+        in_specs=[vmem] * 5,
         out_specs=[vmem] * 5,
         out_shape=[
             tile(count, inner, bf16),
@@ -596,12 +618,12 @@
             jax.ShapeDtypeStruct((state * inner // LANES + 8, LANES), f32),
         ],
         scratch_shapes=[
-            pltpu.VMEM((inner + state, (group + 1) * SCAN_BLOCK), f32),
+            pltpu.VMEM((inner + state, (group + 1) * SCAN_BLOCK), bf16),
             pltpu.VMEM((state + 8, LANES), f32),
         ],
         compiler_params=params(),
         name="states",
-    )(hidden, tail, weights["rows"], weights["cols"])
+    )(hidden, tail, weights["rows"], weights["cols"], weights["shift"])
 
 
 def call_local(layer, first, count, held, done, weights):
@@ -612,18 +634,18 @@
     taken = [] if done is None else list(done)
     return pl.pallas_call(
         functools.partial(local_kernel, layer, heads, first, count, group),
-        in_specs=[vmem] * (7 + len(taken)),
+        in_specs=[vmem] * (8 + len(taken)),
         out_specs=[vmem] * 3,
         out_shape=[tile(total, inner, f32), tile(total, inner, f32), tile(total, state, bf16)],
-        input_output_aliases={7 + i: i for i in range(len(taken))},
+        input_output_aliases={8 + i: i for i in range(len(taken))},
         scratch_shapes=[
-            pltpu.VMEM((state, (group + 1) * SCAN_BLOCK), f32),
+            pltpu.VMEM((state, (group + 1) * SCAN_BLOCK), bf16),
             pltpu.VMEM((group, SCAN_BLOCK, SCAN_BLOCK), f32),
             pltpu.VMEM((group, heads, SCAN_BLOCK, SCAN_BLOCK), bf16),
         ],
         compiler_params=params(),
         name="local",
-    )(hidden, tail, weights["rows"], weights["cols"], inner_values, write, dec, *taken)
+    )(hidden, tail, weights["rows"], weights["cols"], weights["shift"], inner_values, write, dec, *taken)
 
 
 def layer_start(layer, me, hidden, tail, weights):
@@ -663,41 +685,29 @@
     )(*parts)
 
 
-def call_heads(size, parts, weights, head_weight, head_bias, labels, distance):
+def call_heads(me, size, parts, weights, head_weight, head_bias, labels, distance):
     classes, model = head_weight.shape
     count = parts[1].shape[0]
     group = min(32, count)
     return pl.pallas_call(
-        functools.partial(head_kernel, 1, weights["heads"], group),
-        in_specs=[vmem] * (len(parts) + 4),
+        functools.partial(head_kernel, 1, weights["heads"], group, size),
+        in_specs=[pl.BlockSpec(memory_space=pltpu.SMEM)] + [vmem] * (len(parts) + 4),
         out_specs=[vmem] * 3,
         out_shape=[
-            tile(count, model, bf16),
+            jax.ShapeDtypeStruct((model, count, SCAN_BLOCK), bf16),
             jax.ShapeDtypeStruct((classes, count, SCAN_BLOCK), f32),
             jax.ShapeDtypeStruct((size, SCAN_BLOCK), f32),
         ],
         scratch_shapes=finish_scratch(group, weights)
-        + [pltpu.VMEM((classes * group, SCAN_BLOCK), f32), pltpu.VMEM((8, SCAN_BLOCK), f32)],
+        + [
+            pltpu.VMEM((group, model, SCAN_BLOCK), bf16),
+            pltpu.VMEM((model * group, SCAN_BLOCK), f32),
+            pltpu.VMEM((classes * group, SCAN_BLOCK), f32),
+            pltpu.VMEM((8, SCAN_BLOCK), f32),
+        ],
         compiler_params=params(),
         name="heads",
-    )(*parts, head_weight, head_bias, labels, distance)
-
-
-def call_gradient(after, logits, labels, distance):
-    count, model, _ = after.shape
-    return pl.pallas_call(
-        gradient_kernel,
-        in_specs=[vmem] * 4,
-        out_specs=[vmem] * 2,
-        out_shape=[
-            jax.ShapeDtypeStruct((model, count, SCAN_BLOCK), bf16),
-            jax.ShapeDtypeStruct(logits.shape, f32),
-        ],
-        scratch_shapes=[pltpu.VMEM((model * count, SCAN_BLOCK), f32)],
-        compiler_params=params(),
-        cost_estimate=cost(4),
-        name="gradient",
-    )(after, logits, labels, distance)
+    )(me, *parts, head_weight, head_bias, labels, distance)
 
 
 def per_device(
@@ -711,8 +721,10 @@
     heads = decay_rate.shape[1]
     weights = dict(heads=heads, inner=inner, state=(in_proj.shape[1] - 2 * inner) // 2, model=model)
     me = lax.axis_index(axes).astype(jnp.int32).reshape(1)
-    hidden, tail = call_sequence(me, size, jnp.swapaxes(volume[:, 0], 1, 2))
-    weights["rows"], weights["cols"] = call_weights(
+    plane = jnp.swapaxes(volume[:, 0], 1, 2)
+    tail = call_tail(me, size, plane)
+    hidden = call_sequence(plane)
+    weights["rows"], weights["cols"], weights["shift"] = call_weights(
         norm_gain, in_proj, dt_proj, dt_bias, decay_rate, conv_weight, conv_bias, skip_gain, out_gain
     )
     weights["out_proj"] = out_proj
@@ -723,12 +735,11 @@
     count = hidden.shape[0]
     parts = layer_start(1, me, hidden, hidden, weights)
     labels, distance = labels.reshape(count, SCAN_BLOCK), distance.reshape(classes, count, SCAN_BLOCK)
-    after, logits, loss = call_heads(size, parts, weights, head_weight, head_bias[None, :], labels, distance)
+    features, grad, loss = call_heads(
+        me, size, parts, weights, head_weight, head_bias[None, :], labels, distance
+    )
     shared = lax.all_to_all(loss, axes, 0, 0, tiled=True)
-    features, grad = call_gradient(after, logits, labels, distance)
-    shared, features, grad = lax.optimization_barrier((shared, features, grad))
-    voxel_weight = 1.0 + 3.0 * jnp.arange(size, dtype=f32) / (size - 1.0)
-    total_loss = jnp.sum(voxel_weight[:, None] * shared) / (2.5 * count * SCAN_BLOCK * size)
+    total_loss = jnp.sum(shared) / (2.5 * count * SCAN_BLOCK * size)
     return (
         features.reshape(model, 1, count, SCAN_BLOCK),
         grad.reshape(classes, 1, count, SCAN_BLOCK),

time: 80.4 us -> 76.5 us (0.951)
  blocking collectives: 17.8 us -> 28 us
  waiting for transfers between devices: 16.8 us -> 10 us
  starting transfers between devices: 18.8 us -> 14.9 us
  Pallas kernels: 22.4 us -> 18.8 us
    all_to_all x0 -> x1, blocking collectives: none -> 9.8 us  [per_device(): shared = lax.all_to_all(loss, axes, 0, 0, tiled=True)]
    all_to_all x1 -> x0, waiting for transfers between devices: 5.45 us -> none  [per_device(): shared = lax.all_to_all(loss, axes, 0, 0, tiled=True)]
    all_to_all x1 -> x0, starting transfers between devices: 4.06 us -> none  [per_device(): shared = lax.all_to_all(loss, axes, 0, 0, tiled=True)]
    pallas_call x4, Pallas kernels: 8.89 us -> 7.13 us  [call_local(): pl.pallas_call(functools.partial(local_kernel, layer, heads, first, count...]
    pallas_call x4, Pallas kernels: 5.59 us -> 4.28 us  [the longest x1 2.72 us: call_heads(): pl.pallas_call(functools.partial(head_kernel, 1, weights['heads'], group,...]
    ppermute x1, waiting for transfers between devices: 7.04 us -> 5.8 us  [per_device(): tail = lax.ppermute(tail, axes, [(i, (i + 1) % size) for i in range(size)])]
  transfers between devices with their start and end apart: 16 -> 15, of which waited for: 7 -> 7; matrix products, arithmetic and copies ran while one was open for 0% -> 0% of each run, Pallas kernels for 13% -> 11%
where the time goes in v4:
time: 76.5 us; the launch traced here: 76.3 us
  blocking collectives  28 us (37%)
  Pallas kernels  18.8 us (25%)
  starting transfers between devices  14.9 us (19%)
  waiting for transfers between devices  10 us (13%)
  between operations  2.73 us (4%)
  local copies, waits for them, and re-layouts  1.21 us (2%)
    all_to_all x1, blocking collectives, per_device(): lax.all_to_all(planes, axes, split_axis=0, concat_axis=0, tiled=True)  18.2 us
    ppermute x14, starting transfers between devices, prefix_state(): lax.ppermute(total, axes, [(k, k ^ (step * reach | 1)) for k in range(siz...  14.4 us
    all_to_all x1, blocking collectives, per_device(): shared = lax.all_to_all(loss, axes, 0, 0, tiled=True)  9.8 us
    pallas_call x4, Pallas kernels, call_local(): pl.pallas_call(functools.partial(local_kernel, layer, heads, first, count...  7.13 us
    ppermute x1, waiting for transfers between devices, per_device(): tail = lax.ppermute(tail, axes, [(i, (i + 1) % size) for i in range(size)])  5.8 us
    pallas_call x2, Pallas kernels, call_states(): pl.pallas_call(functools.partial(state_kernel, layer, heads, group), in_s...  5.48 us
    ppermute x14, waiting for transfers between devices, prefix_state(): lax.ppermute(total, axes, [(k, k ^ (step * reach | 1)) for k in range(siz...  4.25 us
    pallas_call x1, Pallas kernels, call_heads(): pl.pallas_call(functools.partial(head_kernel, 1, weights['heads'], group,...  2.72 us
  transfers between devices with their start and end apart: 15, of which 7 were waited for; matrix products, arithmetic and copies ran while one was open for 0% of the time, Pallas kernels for 11%

profile of v4, /device:TPU:0, one launch (start us, length us, event | category | flops | bytes accessed | tf_op | source)
XLA Modules:
  0.0 76.3 jit_solution(2097832447139618257)
XLA Ops:
  0.6 1.0 %copy-done.14 = bf16[48,1,128,32]{2,3,1,0:T(8,128)(2,1)S(1)} copy-done((bf16[48,1,128,32]{2,3,1,0:T(8,128)(2,1)S(1)}, bf16[48,1,128,32]{2,3,1,0:T(8,128)(2,1)}, u32[]{:S(2)}) %copy-start.14) | copy-done | bytes 393240
  1.6 0.3 tail.1
  2.0 0.5 collective-permute-start
  2.5 0.1 copy-done.15
  2.6 1.1 %sequence.1.hid_ref = bf16[32,48,128]{2,1,0:T(8,128)(2,1)S(1)} custom-call(bf16[48,32,128]{2,1,0:T(8,128)(2,1)S(1)} %bitcast.27), custom_call_target="tpu_custom_call" | custom-call | flops 8000000000 | bytes 28000000 | tf_op jit(solution)/shard_map/sequence/pallas_call | solution.py:571
  3.8 0.2 weights.1
  4.0 5.8 %collective-permute-done.tail_ref = bf16[48,128]{1,0:T(8,128)(2,1)S(1)} collective-permute-done((bf16[48,128]{1,0:T(8,128)(2,1)S(1)}, bf16[48,128]{1,0:T(8,128)(2,1)S(1)}, u32[]{:S(2)}, u32[]{:S(2)}) %collective-permute-start) | collective-permute-done | bytes 12320 | tf_op jit(solution)/shard_map/ppermute | solution.py:731
  9.8 2.7 %states.2 = (bf16[32,96,128]{2,1,0:T(8,128)(2,1)S(1)}, bf16[32,64,128]{2,1,0:T(8,128)(2,1)S(1)}, f32[32,16,128]{2,1,0:T(8,128)S(1)}, f32[32,72,128]{2,1,0:T(8,128)S(1)}, f32[56,128]{1,0:T(8,128)S(1)}) custom-call(bf16[32,48,128]{2,1,0:T(8,128)(2,1)S(1)} %sequence.1.hid_ref, bf16[48,128]{1,0:T(8,128)(2,1)S(1)} %collective-permute-done.tail_ref, ...), custom_call_target="tpu_custom_call" | custom-call | tf_op jit(solution)/shard_map/states/pallas_call | solution.py:609
  12.6 1.2 %collective-permute-done.1.refs_1_ = f32[56,128]{1,0:T(8,128)S(1)} collective-permute-done((f32[56,128]{1,0:T(8,128)S(1)}, f32[56,128]{1,0:T(8,128)S(1)}, u32[]{:S(2)}, u32[]{:S(2)}) %collective-permute-start.1) | collective-permute-done | bytes 28704 | tf_op jit(solution)/shard_map/ppermute | solution.py:533
  13.9 2.9 %collective-permute-start.2 = (f32[56,128]{1,0:T(8,128)S(1)}, f32[56,128]{1,0:T(8,128)S(1)}, u32[]{:S(2)}, u32[]{:S(2)}) collective-permute-start(f32[56,128]{1,0:T(8,128)S(1)} %get-tuple-element.96.refs_0_), channel_id=1, source_target_pairs={{0,3},{1,2},{2,1},{3,0},{4,7},{5,6},{6,5},{7,4},{8,11},{9,10},{10,... | collective-permute-start | bytes 86024 | tf_op jit(solution)/shard_map/ppermute | solution.py:533
  16.8 1.8 %local.4 = (f32[32,96,128]{2,1,0:T(8,128)S(1)}, f32[32,96,128]{2,1,0:T(8,128)S(1)}, bf16[32,64,128]{2,1,0:T(8,128)(2,1)S(1)}) custom-call(bf16[32,48,128]{2,1,0:T(8,128)(2,1)S(1)} %sequence.1.hid_ref, bf16[48,128]{1,0:T(8,128)(2,1)S(1)} %collective-permute-done.tail_ref, bf16[2,336,48]{2,1,0:T(8,128)(2,1)S(1)} %get-tuple-element.87.weight_ref, ...), custom_call_target="tpu_custom_call" | custom-call | tf_op jit(solution)/shard_map/local/pallas_call | solution.py:635
  18.7 2.2 %collective-permute-start.7 = (f32[56,128]{1,0:T(8,128)S(1)}, f32[56,128]{1,0:T(8,128)S(1)}, u32[]{:S(2)}, u32[]{:S(2)}) collective-permute-start(f32[56,128]{1,0:T(8,128)S(1)} %get-tuple-element.110.refs_0_), channel_id=1, source_target_pairs={{0,25},{1,24},{2,27},{3,26},{4,29},{5,28},{6,31},{7,30},{8,17},{9,... | collective-permute-start | bytes 86024 | tf_op jit(solution)/shard_map/ppermute | solution.py:533
  20.9 1.9 %collective-permute-start.5 = (f32[56,128]{1,0:T(8,128)S(1)}, f32[56,128]{1,0:T(8,128)S(1)}, u32[]{:S(2)}, u32[]{:S(2)}) collective-permute-start(f32[56,128]{1,0:T(8,128)S(1)} %get-tuple-element.110.refs_0_), channel_id=1, source_target_pairs={{0,9},{1,8},{2,11},{3,10},{4,13},{5,12},{6,15},{7,14},{8,1},{9,0},... | collective-permute-start | bytes 86024 | tf_op jit(solution)/shard_map/ppermute | solution.py:533
  22.8 1.8 %local.5 = (f32[32,96,128]{2,1,0:T(8,128)S(1)}, f32[32,96,128]{2,1,0:T(8,128)S(1)}, bf16[32,64,128]{2,1,0:T(8,128)(2,1)S(1)}) custom-call(bf16[32,48,128]{2,1,0:T(8,128)(2,1)S(1)} %sequence.1.hid_ref, bf16[48,128]{1,0:T(8,128)(2,1)S(1)} %collective-permute-done.tail_ref, ...), custom_call_target="tpu_custom_call", output_to_operand_aliasing={{0}: (8, {}), {1}: (9, {}), {2}: (10, {})} | custom-call | tf_op jit(solution)/shard_map/local/pallas_call | solution.py:635
  24.6 0.6 collective-permute-done.6.refs_2_
  25.2 1.8 %finish.1 = bf16[32,56,128]{2,1,0:T(8,128)(2,1)S(1)} custom-call(f32[56,128]{1,0:T(8,128)S(1)} %join.8.enter_ref, bf16[32,48,128]{2,1,0:T(8,128)(2,1)S(1)} %sequence.1.hid_ref, f32[32,96,128]{2,1,0:T(8,128)S(1)} %get-tuple-element.125.local_ref, f32[32,96,128]{2,1,0:T(8,128)S(1)} %get-tuple-element.126.gate_ref, ...), custom_call_target="tpu_custom_call" | custom-call | tf_op jit(solution)/shard_map/finish/pallas_call | solution.py:672
  27.0 18.2 %all_to_all.14.hid_ref.tail_ref = bf16[32,56,128]{2,1,0:T(8,128)(2,1)S(1)} all-to-all(bf16[32,56,128]{2,1,0:T(8,128)(2,1)S(1)} %finish.1), channel_id=1, replica_groups=mesh['row'=8,'col'=4] {'row','col'}, dimensions={0} | all-to-all | bytes 917504 | tf_op jit(solution)/shard_map/all_to_all | solution.py:734
  45.2 2.8 %states.3 = (bf16[32,96,128]{2,1,0:T(8,128)(2,1)S(1)}, bf16[32,64,128]{2,1,0:T(8,128)(2,1)S(1)}, f32[32,16,128]{2,1,0:T(8,128)S(1)}, f32[32,72,128]{2,1,0:T(8,128)S(1)}, f32[56,128]{1,0:T(8,128)S(1)}) custom-call(bf16[32,56,128]{2,1,0:T(8,128)(2,1)S(1)} %all_to_all.14.hid_ref.tail_ref, bf16[32,56,128]{2,1,0:T(8,128)(2,1)S(1)} %all_to_all.14.hid_ref.tail_ref, ...), custom_call_target="tpu_custom_call" | custom-call | tf_op jit(solution)/shard_map/states/pallas_call | solution.py:609
  47.9 1.2 %collective-permute-done.8.refs_1_ = f32[56,128]{1,0:T(8,128)S(1)} collective-permute-done((f32[56,128]{1,0:T(8,128)S(1)}, f32[56,128]{1,0:T(8,128)S(1)}, u32[]{:S(2)}, u32[]{:S(2)}) %collective-permute-start.8) | collective-permute-done | bytes 28704 | tf_op jit(solution)/shard_map/ppermute | solution.py:533
  49.1 1.5 %collective-permute-start.11 = (f32[56,128]{1,0:T(8,128)S(1)}, f32[56,128]{1,0:T(8,128)S(1)}, u32[]{:S(2)}, u32[]{:S(2)}) collective-permute-start(f32[56,128]{1,0:T(8,128)S(1)} %get-tuple-element.135.refs_0_), channel_id=1, source_target_pairs={{0,7},{1,6},{2,5},{3,4},{4,3},{5,2},{6,1},{7,0},{8,15},{9,14},{10,... | collective-permute-start | bytes 86024 | tf_op jit(solution)/shard_map/ppermute | solution.py:533
  50.6 0.6 collective-permute-start.10
  51.2 1.0 %collective-permute-start.9 = (f32[56,128]{1,0:T(8,128)S(1)}, f32[56,128]{1,0:T(8,128)S(1)}, u32[]{:S(2)}, u32[]{:S(2)}) collective-permute-start(f32[56,128]{1,0:T(8,128)S(1)} %get-tuple-element.135.refs_0_), channel_id=1, source_target_pairs={{0,3},{1,2},{2,1},{3,0},{4,7},{5,6},{6,5},{7,4},{8,11},{9,10},{10,... | collective-permute-start | bytes 86024 | tf_op jit(solution)/shard_map/ppermute | solution.py:533
  52.2 1.8 %local.6 = (f32[32,96,128]{2,1,0:T(8,128)S(1)}, f32[32,96,128]{2,1,0:T(8,128)S(1)}, bf16[32,64,128]{2,1,0:T(8,128)(2,1)S(1)}) custom-call(bf16[32,56,128]{2,1,0:T(8,128)(2,1)S(1)} %all_to_all.14.hid_ref.tail_ref, bf16[32,56,128]{2,1,0:T(8,128)(2,1)S(1)} %all_to_all.14.hid_ref.tail_ref, bf16[2,336,48]{2,1,0:T(8,128)(2,1)S(1)} %get-tuple-element.87.weight_ref, ...), custom_call_target="tpu_custom_call" | custom-call | tf_op jit(solution)/shard_map/local/pallas_call | solution.py:635
  54.1 0.4 collective-permute-done.9.refs_1_
  54.6 1.2 %collective-permute-start.14 = (f32[56,128]{1,0:T(8,128)S(1)}, f32[56,128]{1,0:T(8,128)S(1)}, u32[]{:S(2)}, u32[]{:S(2)}) collective-permute-start(f32[56,128]{1,0:T(8,128)S(1)} %get-tuple-element.149.refs_0_), channel_id=1, source_target_pairs={{0,25},{1,24},{2,27},{3,26},{4,29},{5,28},{6,31},{7,30},{8,17},{9,... | collective-permute-start | bytes 86024 | tf_op jit(solution)/shard_map/ppermute | solution.py:533
  55.8 0.8 %collective-permute-start.13 = (f32[56,128]{1,0:T(8,128)S(1)}, f32[56,128]{1,0:T(8,128)S(1)}, u32[]{:S(2)}, u32[]{:S(2)}) collective-permute-start(f32[56,128]{1,0:T(8,128)S(1)} %get-tuple-element.149.refs_0_), channel_id=1, source_target_pairs={{0,17},{1,16},{2,19},{3,18},{4,21},{5,20},{6,23},{7,22},{8,25},{9,... | collective-permute-start | bytes 86024 | tf_op jit(solution)/shard_map/ppermute | solution.py:533
  56.5 2.2 %collective-permute-start.12 = (f32[56,128]{1,0:T(8,128)S(1)}, f32[56,128]{1,0:T(8,128)S(1)}, u32[]{:S(2)}, u32[]{:S(2)}) collective-permute-start(f32[56,128]{1,0:T(8,128)S(1)} %get-tuple-element.149.refs_0_), channel_id=1, source_target_pairs={{0,9},{1,8},{2,11},{3,10},{4,13},{5,12},{6,15},{7,14},{8,1},{9,0},... | collective-permute-start | bytes 86024 | tf_op jit(solution)/shard_map/ppermute | solution.py:533
  58.7 1.8 %local.7 = (f32[32,96,128]{2,1,0:T(8,128)S(1)}, f32[32,96,128]{2,1,0:T(8,128)S(1)}, bf16[32,64,128]{2,1,0:T(8,128)(2,1)S(1)}) custom-call(bf16[32,56,128]{2,1,0:T(8,128)(2,1)S(1)} %all_to_all.14.hid_ref.tail_ref, bf16[32,56,128]{2,1,0:T(8,128)(2,1)S(1)} %all_to_all.14.hid_ref.tail_ref, ...), custom_call_target="tpu_custom_call", output_to_operand_aliasing={{0}: (8, {}), {1}: (9, {}), {2}: (10, {})} | custom-call | tf_op jit(solution)/shard_map/local/pallas_call | solution.py:635
  60.5 0.8 %collective-permute-done.13.refs_2_ = f32[56,128]{1,0:T(8,128)S(1)} collective-permute-done((f32[56,128]{1,0:T(8,128)S(1)}, f32[56,128]{1,0:T(8,128)S(1)}, u32[]{:S(2)}, u32[]{:S(2)}) %collective-permute-start.13) | collective-permute-done | bytes 28704 | tf_op jit(solution)/shard_map/ppermute | solution.py:533
  61.4 2.7 %heads.1 = (bf16[48,32,128]{2,1,0:T(8,128)(2,1)}, f32[14,32,128]{2,1,0:T(8,128)}, f32[32,128]{1,0:T(8,128)S(1)}) custom-call(s32[1]{0:T(128)} %bitcast.me_ref, f32[56,128]{1,0:T(8,128)S(1)} %join.11.enter_ref, bf16[32,56,128]{2,1,0:T(8,128)(2,1)S(1)} %all_to_all.14.hid_ref.tail_ref, f32[32,96,128]{2,1,0:T(8,128)S(1)} %get-tuple-element.164.local_ref, ...), custom_call_target="tpu_custom_call" | custom-call | tf_op jit(solution)/shard_map/heads/pallas_call | solution.py:692
  64.1 9.8 %all_to_all.15 = f32[32,1,128]{2,1,0:T(1,128)S(1)} all-to-all(f32[32,1,128]{2,1,0:T(1,128)S(1)} %bitcast.22), channel_id=1, replica_groups=mesh['row'=8,'col'=4] {'row','col'}, dimensions={0} | all-to-all | bytes 32768 | tf_op jit(solution)/shard_map/all_to_all | solution.py:741
  73.9 0.6 reduce_sum.9
  (51 shorter events, 0.6 us)
Async XLA Ops:
  0.6 1.0 %copy-start.14 = (bf16[48,1,128,32]{2,3,1,0:T(8,128)(2,1)S(1)}, bf16[48,1,128,32]{2,3,1,0:T(8,128)(2,1)}, u32[]{:S(2)}) copy-start(bf16[48,1,128,32]{2,3,1,0:T(8,128)(2,1)} %param.15) | copy-start | bytes 1179652
  1.6 1.0 %copy-start.15 = (bf16[48,1,128,32]{2,3,1,0:T(8,128)(2,1)S(1)}, bf16[48,1,128,32]{2,3,1,0:T(8,128)(2,1)}, u32[]{:S(2)}) copy-start(bf16[48,1,128,32]{2,3,1,0:T(8,128)(2,1)} %param.15) | copy-start | bytes 1179652
  1.9 1.8 %copy-start.2 = (bf16[2,320,48]{1,2,0:T(8,128)(2,1)S(1)}, bf16[2,320,48]{1,2,0:T(8,128)(2,1)}, u32[]{:S(2)}) copy-start(bf16[2,320,48]{1,2,0:T(8,128)(2,1)} %param.17) | copy-start | bytes 184324
  1.9 1.8 %copy-start.4 = (f32[2,224,4]{1,2,0:T(4,128)S(1)}, f32[2,224,4]{1,2,0:T(4,128)}, u32[]{:S(2)}) copy-start(f32[2,224,4]{1,2,0:T(4,128)} %param.21) | copy-start | bytes 21508
  1.9 1.8 %copy-start.6 = (f32[2,224]{1,0:T(2,128)S(1)}, f32[2,224]{1,0:T(2,128)}, u32[]{:S(2)}) copy-start(f32[2,224]{1,0:T(2,128)} %conv_bias_ref.1) | copy-start | bytes 5380
  1.9 1.8 %copy-start.7 = (bf16[2,3,48]{2,0,1:T(2,128)(2,1)S(1)}, bf16[2,3,48]{2,0,1:T(2,128)(2,1)}, u32[]{:S(2)}) copy-start(bf16[2,3,48]{2,0,1:T(2,128)(2,1)} %param.18) | copy-start | bytes 1732
  1.9 1.8 %copy-start.8 = (f32[2,48]{1,0:T(2,128)S(1)}, f32[2,48]{1,0:T(2,128)}, u32[]{:S(2)}) copy-start(f32[2,48]{1,0:T(2,128)} %gain_ref.1) | copy-start | bytes 1156
  2.0 1.8 %copy-start.9 = (f32[2,3]{1,0:T(2,128)S(1)}, f32[2,3]{1,0:T(2,128)}, u32[]{:S(2)}) copy-start(f32[2,3]{1,0:T(2,128)} %dt_bias_ref.1) | copy-start | bytes 76
  2.0 1.8 %copy-start.10 = (f32[2,3]{1,0:T(2,128)S(1)}, f32[2,3]{1,0:T(2,128)}, u32[]{:S(2)}) copy-start(f32[2,3]{1,0:T(2,128)} %rate_ref.1) | copy-start | bytes 76
  2.0 1.8 %copy-start.11 = (f32[2,3]{1,0:T(2,128)S(1)}, f32[2,3]{1,0:T(2,128)}, u32[]{:S(2)}) copy-start(f32[2,3]{1,0:T(2,128)} %skip_ref.1) | copy-start | bytes 76
  2.0 1.8 %copy-start.12 = (f32[2,96]{1,0:T(2,128)S(1)}, f32[2,96]{1,0:T(2,128)}, u32[]{:S(2)}) copy-start(f32[2,96]{1,0:T(2,128)} %out_gain_ref.1) | copy-start | bytes 2308
  2.0 7.8 %collective-permute-start = (bf16[48,128]{1,0:T(8,128)(2,1)S(1)}, bf16[48,128]{1,0:T(8,128)(2,1)S(1)}, u32[]{:S(2)}, u32[]{:S(2)}) collective-permute-start(bf16[48,128]{1,0:T(8,128)(2,1)S(1)} %tail.1), channel_id=1, source_target_pairs={{0,1},{1,2},{2,3},{3,4},{4,5},{5,6},{6,7},{7,8},{8,9},{9,10},{10,1... | collective-permute-start | bytes 36872 | tf_op jit(solution)/shard_map/ppermute | solution.py:731
  12.5 1.2 %collective-permute-start.1 = (f32[56,128]{1,0:T(8,128)S(1)}, f32[56,128]{1,0:T(8,128)S(1)}, u32[]{:S(2)}, u32[]{:S(2)}) collective-permute-start(f32[56,128]{1,0:T(8,128)S(1)} %get-tuple-element.90.refs_0_), channel_id=1, source_target_pairs={{0,1},{1,0},{2,3},{3,2},{4,5},{5,4},{6,7},{7,6},{8,9},{9,8},{10,11... | collective-permute-start | bytes 86024 | tf_op jit(solution)/shard_map/ppermute | solution.py:533
  13.8 4.8 %collective-permute-start.4 = (f32[56,128]{1,0:T(8,128)S(1)}, f32[56,128]{1,0:T(8,128)S(1)}, u32[]{:S(2)}, u32[]{:S(2)}) collective-permute-start(f32[56,128]{1,0:T(8,128)S(1)} %get-tuple-element.96.refs_0_), channel_id=1, source_target_pairs={{0,7},{1,6},{2,5},{3,4},{4,3},{5,2},{6,1},{7,0},{8,15},{9,14},{10,... | collective-permute-start | bytes 86024 | tf_op jit(solution)/shard_map/ppermute | solution.py:533
  13.9 4.8 %collective-permute-start.3 = (f32[56,128]{1,0:T(8,128)S(1)}, f32[56,128]{1,0:T(8,128)S(1)}, u32[]{:S(2)}, u32[]{:S(2)}) collective-permute-start(f32[56,128]{1,0:T(8,128)S(1)} %get-tuple-element.96.refs_0_), channel_id=1, source_target_pairs={{0,5},{1,4},{2,7},{3,6},{4,1},{5,0},{6,3},{7,2},{8,13},{9,12},{10,... | collective-permute-start | bytes 86024 | tf_op jit(solution)/shard_map/ppermute | solution.py:533
  13.9 4.7 %collective-permute-start.2 = (f32[56,128]{1,0:T(8,128)S(1)}, f32[56,128]{1,0:T(8,128)S(1)}, u32[]{:S(2)}, u32[]{:S(2)}) collective-permute-start(f32[56,128]{1,0:T(8,128)S(1)} %get-tuple-element.96.refs_0_), channel_id=1, source_target_pairs={{0,3},{1,2},{2,1},{3,0},{4,7},{5,6},{6,5},{7,4},{8,11},{9,10},{10,... | collective-permute-start | bytes 86024 | tf_op jit(solution)/shard_map/ppermute | solution.py:533
  18.7 6.5 %copy-start.1 = (bf16[2,48,96]{2,1,0:T(8,128)(2,1)S(1)}, bf16[2,48,96]{2,1,0:T(8,128)(2,1)}, u32[]{:S(2)}) copy-start(bf16[2,48,96]{2,1,0:T(8,128)(2,1)} %out_proj_ref.3) | copy-start | bytes 55300
  18.7 5.9 %collective-permute-start.7 = (f32[56,128]{1,0:T(8,128)S(1)}, f32[56,128]{1,0:T(8,128)S(1)}, u32[]{:S(2)}, u32[]{:S(2)}) collective-permute-start(f32[56,128]{1,0:T(8,128)S(1)} %get-tuple-element.110.refs_0_), channel_id=1, source_target_pairs={{0,25},{1,24},{2,27},{3,26},{4,29},{5,28},{6,31},{7,30},{8,17},{9,... | collective-permute-start | bytes 86024 | tf_op jit(solution)/shard_map/ppermute | solution.py:533
  20.9 4.2 %collective-permute-start.6 = (f32[56,128]{1,0:T(8,128)S(1)}, f32[56,128]{1,0:T(8,128)S(1)}, u32[]{:S(2)}, u32[]{:S(2)}) collective-permute-start(f32[56,128]{1,0:T(8,128)S(1)} %get-tuple-element.110.refs_0_), channel_id=1, source_target_pairs={{0,17},{1,16},{2,19},{3,18},{4,21},{5,20},{6,23},{7,22},{8,25},{9,... | collective-permute-start | bytes 86024 | tf_op jit(solution)/shard_map/ppermute | solution.py:533
  20.9 4.2 %collective-permute-start.5 = (f32[56,128]{1,0:T(8,128)S(1)}, f32[56,128]{1,0:T(8,128)S(1)}, u32[]{:S(2)}, u32[]{:S(2)}) collective-permute-start(f32[56,128]{1,0:T(8,128)S(1)} %get-tuple-element.110.refs_0_), channel_id=1, source_target_pairs={{0,9},{1,8},{2,11},{3,10},{4,13},{5,12},{6,15},{7,14},{8,1},{9,0},... | collective-permute-start | bytes 86024 | tf_op jit(solution)/shard_map/ppermute | solution.py:533
  47.9 1.2 %collective-permute-start.8 = (f32[56,128]{1,0:T(8,128)S(1)}, f32[56,128]{1,0:T(8,128)S(1)}, u32[]{:S(2)}, u32[]{:S(2)}) collective-permute-start(f32[56,128]{1,0:T(8,128)S(1)} %get-tuple-element.129.refs_0_), channel_id=1, source_target_pairs={{0,1},{1,0},{2,3},{3,2},{4,5},{5,4},{6,7},{7,6},{8,9},{9,8},{10,11... | collective-permute-start | bytes 86024 | tf_op jit(solution)/shard_map/ppermute | solution.py:533
  49.1 4.8 %collective-permute-start.11 = (f32[56,128]{1,0:T(8,128)S(1)}, f32[56,128]{1,0:T(8,128)S(1)}, u32[]{:S(2)}, u32[]{:S(2)}) collective-permute-start(f32[56,128]{1,0:T(8,128)S(1)} %get-tuple-element.135.refs_0_), channel_id=1, source_target_pairs={{0,7},{1,6},{2,5},{3,4},{4,3},{5,2},{6,1},{7,0},{8,15},{9,14},{10,... | collective-permute-start | bytes 86024 | tf_op jit(solution)/shard_map/ppermute | solution.py:533
  50.6 3.4 %collective-permute-start.10 = (f32[56,128]{1,0:T(8,128)S(1)}, f32[56,128]{1,0:T(8,128)S(1)}, u32[]{:S(2)}, u32[]{:S(2)}) collective-permute-start(f32[56,128]{1,0:T(8,128)S(1)} %get-tuple-element.135.refs_0_), channel_id=1, source_target_pairs={{0,5},{1,4},{2,7},{3,6},{4,1},{5,0},{6,3},{7,2},{8,13},{9,12},{10,... | collective-permute-start | bytes 86024 | tf_op jit(solution)/shard_map/ppermute | solution.py:533
  51.2 3.3 %collective-permute-start.9 = (f32[56,128]{1,0:T(8,128)S(1)}, f32[56,128]{1,0:T(8,128)S(1)}, u32[]{:S(2)}, u32[]{:S(2)}) collective-permute-start(f32[56,128]{1,0:T(8,128)S(1)} %get-tuple-element.135.refs_0_), channel_id=1, source_target_pairs={{0,3},{1,2},{2,1},{3,0},{4,7},{5,6},{6,5},{7,4},{8,11},{9,10},{10,... | collective-permute-start | bytes 86024 | tf_op jit(solution)/shard_map/ppermute | solution.py:533
  54.5 6.8 %copy-start = (s32[14,1,32,128]{3,2,1,0:T(8,128)S(1)}, s32[14,1,32,128]{3,2,1,0:T(8,128)}, u32[]{:S(2)}) copy-start(s32[14,1,32,128]{3,2,1,0:T(8,128)} %param.29) | copy-start | bytes 688132
  54.5 6.8 %copy-start.3 = (s32[1,32,128]{2,1,0:T(8,128)S(1)}, s32[1,32,128]{2,1,0:T(8,128)}, u32[]{:S(2)}) copy-start(s32[1,32,128]{2,1,0:T(8,128)} %param.28) | copy-start | bytes 49156
  54.6 6.8 %copy-start.5 = (bf16[14,48]{1,0:T(8,128)(2,1)S(1)}, bf16[14,48]{1,0:T(8,128)(2,1)}, u32[]{:S(2)}) copy-start(bf16[14,48]{1,0:T(8,128)(2,1)} %head_ref.1) | copy-start | bytes 4036
  54.6 6.8 %copy-start.13 = (f32[14]{0:T(128)S(1)}, f32[14]{0:T(128)}, u32[]{:S(2)}) copy-start(f32[14]{0:T(128)} %param.27) | copy-start | bytes 172
  54.6 5.9 %collective-permute-start.14 = (f32[56,128]{1,0:T(8,128)S(1)}, f32[56,128]{1,0:T(8,128)S(1)}, u32[]{:S(2)}, u32[]{:S(2)}) collective-permute-start(f32[56,128]{1,0:T(8,128)S(1)} %get-tuple-element.149.refs_0_), channel_id=1, source_target_pairs={{0,25},{1,24},{2,27},{3,26},{4,29},{5,28},{6,31},{7,30},{8,17},{9,... | collective-permute-start | bytes 86024 | tf_op jit(solution)/shard_map/ppermute | solution.py:533
  55.8 5.5 %collective-permute-start.13 = (f32[56,128]{1,0:T(8,128)S(1)}, f32[56,128]{1,0:T(8,128)S(1)}, u32[]{:S(2)}, u32[]{:S(2)}) collective-permute-start(f32[56,128]{1,0:T(8,128)S(1)} %get-tuple-element.149.refs_0_), channel_id=1, source_target_pairs={{0,17},{1,16},{2,19},{3,18},{4,21},{5,20},{6,23},{7,22},{8,25},{9,... | collective-permute-start | bytes 86024 | tf_op jit(solution)/shard_map/ppermute | solution.py:533
  56.5 4.7 %collective-permute-start.12 = (f32[56,128]{1,0:T(8,128)S(1)}, f32[56,128]{1,0:T(8,128)S(1)}, u32[]{:S(2)}, u32[]{:S(2)}) collective-permute-start(f32[56,128]{1,0:T(8,128)S(1)} %get-tuple-element.149.refs_0_), channel_id=1, source_target_pairs={{0,9},{1,8},{2,11},{3,10},{4,13},{5,12},{6,15},{7,14},{8,1},{9,0},... | collective-permute-start | bytes 86024 | tf_op jit(solution)/shard_map/ppermute | solution.py:533

commit v5 on v4

--- a/solution.py
+++ b/solution.py
@@ -223,7 +223,7 @@
     for j in range(per):
         shift = LANES - (j + 1) * cells_x
         part_ref[pl.ds(j, model // per, stride=per), :] = pltpu.roll(rows, shift, 1) if shift else rows
-    tail = part_ref[...]
+    tail = part_ref[0:model, :]
     tail_ref[...] = jnp.where(me_ref[0] == size - 1, jnp.zeros_like(tail), tail).astype(bf16)
 
 
@@ -553,12 +553,13 @@
 
 def call_tail(me, size, volume):
     model = volume.shape[0]
+    per = LANES // volume.shape[1]
     return pl.pallas_call(
         functools.partial(tail_kernel, size),
         in_specs=[pl.BlockSpec(memory_space=pltpu.SMEM), vmem],
         out_specs=vmem,
         out_shape=jax.ShapeDtypeStruct((model, SCAN_BLOCK), bf16),
-        scratch_shapes=[pltpu.VMEM((model, LANES), f32)],
+        scratch_shapes=[pltpu.VMEM((-(-model // (8 * per)) * 8 * per, LANES), f32)],
         compiler_params=params(4 * 1024 * 1024),
         cost_estimate=cost(2),
         name="tail",
@@ -702,7 +703,7 @@
         + [
             pltpu.VMEM((group, model, SCAN_BLOCK), bf16),
             pltpu.VMEM((model * group, SCAN_BLOCK), f32),
-            pltpu.VMEM((classes * group, SCAN_BLOCK), f32),
+            pltpu.VMEM((-(-classes // 8) * 8 * group, SCAN_BLOCK), f32),
             pltpu.VMEM((8, SCAN_BLOCK), f32),
         ],
         compiler_params=params(),

time: 76.5 us -> 76.5 us (level)
  no operation moved by 1% of the time
where the time goes in v5:
time: 76.5 us; the launch traced here: 76.3 us
  blocking collectives  28 us (37%)
  Pallas kernels  18.8 us (25%)
  starting transfers between devices  14.9 us (19%)
  waiting for transfers between devices  10 us (13%)
  between operations  2.73 us (4%)
  local copies, waits for them, and re-layouts  1.21 us (2%)
    all_to_all x1, blocking collectives, per_device(): lax.all_to_all(planes, axes, split_axis=0, concat_axis=0, tiled=True)  18.2 us
    ppermute x14, starting transfers between devices, prefix_state(): lax.ppermute(total, axes, [(k, k ^ (step * reach | 1)) for k in range(siz...  14.4 us
    all_to_all x1, blocking collectives, per_device(): shared = lax.all_to_all(loss, axes, 0, 0, tiled=True)  9.8 us
    pallas_call x4, Pallas kernels, call_local(): pl.pallas_call(functools.partial(local_kernel, layer, heads, first, count...  7.13 us
    ppermute x1, waiting for transfers between devices, per_device(): tail = lax.ppermute(tail, axes, [(i, (i + 1) % size) for i in range(size)])  5.8 us
    pallas_call x2, Pallas kernels, call_states(): pl.pallas_call(functools.partial(state_kernel, layer, heads, group), in_s...  5.48 us
    ppermute x14, waiting for transfers between devices, prefix_state(): lax.ppermute(total, axes, [(k, k ^ (step * reach | 1)) for k in range(siz...  4.25 us
    pallas_call x1, Pallas kernels, call_heads(): pl.pallas_call(functools.partial(head_kernel, 1, weights['heads'], group,...  2.72 us
  transfers between devices with their start and end apart: 15, of which 7 were waited for; matrix products, arithmetic and copies ran while one was open for 0% of the time, Pallas kernels for 11%

profile of v5, /device:TPU:0, one launch (start us, length us, event | category | flops | bytes accessed | tf_op | source)
XLA Modules:
  0.0 76.3 jit_solution(4219630669005889292)
XLA Ops:
  0.6 1.0 %copy-done.14 = bf16[48,1,128,32]{2,3,1,0:T(8,128)(2,1)S(1)} copy-done((bf16[48,1,128,32]{2,3,1,0:T(8,128)(2,1)S(1)}, bf16[48,1,128,32]{2,3,1,0:T(8,128)(2,1)}, u32[]{:S(2)}) %copy-start.14) | copy-done | bytes 393240
  1.6 0.3 tail.1
  2.0 0.5 collective-permute-start
  2.5 0.1 copy-done.15
  2.6 1.1 %sequence.1.hid_ref = bf16[32,48,128]{2,1,0:T(8,128)(2,1)S(1)} custom-call(bf16[48,32,128]{2,1,0:T(8,128)(2,1)S(1)} %bitcast.27), custom_call_target="tpu_custom_call" | custom-call | flops 8000000000 | bytes 28000000 | tf_op jit(solution)/shard_map/sequence/pallas_call | solution.py:572
  3.8 0.2 weights.1
  4.0 5.8 %collective-permute-done.tail_ref = bf16[48,128]{1,0:T(8,128)(2,1)S(1)} collective-permute-done((bf16[48,128]{1,0:T(8,128)(2,1)S(1)}, bf16[48,128]{1,0:T(8,128)(2,1)S(1)}, u32[]{:S(2)}, u32[]{:S(2)}) %collective-permute-start) | collective-permute-done | bytes 12320 | tf_op jit(solution)/shard_map/ppermute | solution.py:732
  9.8 2.7 %states.2 = (bf16[32,96,128]{2,1,0:T(8,128)(2,1)S(1)}, bf16[32,64,128]{2,1,0:T(8,128)(2,1)S(1)}, f32[32,16,128]{2,1,0:T(8,128)S(1)}, f32[32,72,128]{2,1,0:T(8,128)S(1)}, f32[56,128]{1,0:T(8,128)S(1)}) custom-call(bf16[32,48,128]{2,1,0:T(8,128)(2,1)S(1)} %sequence.1.hid_ref, bf16[48,128]{1,0:T(8,128)(2,1)S(1)} %collective-permute-done.tail_ref, ...), custom_call_target="tpu_custom_call" | custom-call | tf_op jit(solution)/shard_map/states/pallas_call | solution.py:610
  12.6 1.2 %collective-permute-done.1.refs_1_ = f32[56,128]{1,0:T(8,128)S(1)} collective-permute-done((f32[56,128]{1,0:T(8,128)S(1)}, f32[56,128]{1,0:T(8,128)S(1)}, u32[]{:S(2)}, u32[]{:S(2)}) %collective-permute-start.1) | collective-permute-done | bytes 28704 | tf_op jit(solution)/shard_map/ppermute | solution.py:533
  13.9 2.9 %collective-permute-start.2 = (f32[56,128]{1,0:T(8,128)S(1)}, f32[56,128]{1,0:T(8,128)S(1)}, u32[]{:S(2)}, u32[]{:S(2)}) collective-permute-start(f32[56,128]{1,0:T(8,128)S(1)} %get-tuple-element.96.refs_0_), channel_id=1, source_target_pairs={{0,3},{1,2},{2,1},{3,0},{4,7},{5,6},{6,5},{7,4},{8,11},{9,10},{10,... | collective-permute-start | bytes 86024 | tf_op jit(solution)/shard_map/ppermute | solution.py:533
  16.8 1.8 %local.4 = (f32[32,96,128]{2,1,0:T(8,128)S(1)}, f32[32,96,128]{2,1,0:T(8,128)S(1)}, bf16[32,64,128]{2,1,0:T(8,128)(2,1)S(1)}) custom-call(bf16[32,48,128]{2,1,0:T(8,128)(2,1)S(1)} %sequence.1.hid_ref, bf16[48,128]{1,0:T(8,128)(2,1)S(1)} %collective-permute-done.tail_ref, bf16[2,336,48]{2,1,0:T(8,128)(2,1)S(1)} %get-tuple-element.87.weight_ref, ...), custom_call_target="tpu_custom_call" | custom-call | tf_op jit(solution)/shard_map/local/pallas_call | solution.py:636
  18.7 2.2 %collective-permute-start.7 = (f32[56,128]{1,0:T(8,128)S(1)}, f32[56,128]{1,0:T(8,128)S(1)}, u32[]{:S(2)}, u32[]{:S(2)}) collective-permute-start(f32[56,128]{1,0:T(8,128)S(1)} %get-tuple-element.110.refs_0_), channel_id=1, source_target_pairs={{0,25},{1,24},{2,27},{3,26},{4,29},{5,28},{6,31},{7,30},{8,17},{9,... | collective-permute-start | bytes 86024 | tf_op jit(solution)/shard_map/ppermute | solution.py:533
  20.9 1.9 %collective-permute-start.5 = (f32[56,128]{1,0:T(8,128)S(1)}, f32[56,128]{1,0:T(8,128)S(1)}, u32[]{:S(2)}, u32[]{:S(2)}) collective-permute-start(f32[56,128]{1,0:T(8,128)S(1)} %get-tuple-element.110.refs_0_), channel_id=1, source_target_pairs={{0,9},{1,8},{2,11},{3,10},{4,13},{5,12},{6,15},{7,14},{8,1},{9,0},... | collective-permute-start | bytes 86024 | tf_op jit(solution)/shard_map/ppermute | solution.py:533
  22.8 1.8 %local.5 = (f32[32,96,128]{2,1,0:T(8,128)S(1)}, f32[32,96,128]{2,1,0:T(8,128)S(1)}, bf16[32,64,128]{2,1,0:T(8,128)(2,1)S(1)}) custom-call(bf16[32,48,128]{2,1,0:T(8,128)(2,1)S(1)} %sequence.1.hid_ref, bf16[48,128]{1,0:T(8,128)(2,1)S(1)} %collective-permute-done.tail_ref, ...), custom_call_target="tpu_custom_call", output_to_operand_aliasing={{0}: (8, {}), {1}: (9, {}), {2}: (10, {})} | custom-call | tf_op jit(solution)/shard_map/local/pallas_call | solution.py:636
  24.6 0.6 collective-permute-done.6.refs_2_
  25.2 1.8 %finish.1 = bf16[32,56,128]{2,1,0:T(8,128)(2,1)S(1)} custom-call(f32[56,128]{1,0:T(8,128)S(1)} %join.8.enter_ref, bf16[32,48,128]{2,1,0:T(8,128)(2,1)S(1)} %sequence.1.hid_ref, f32[32,96,128]{2,1,0:T(8,128)S(1)} %get-tuple-element.125.local_ref, f32[32,96,128]{2,1,0:T(8,128)S(1)} %get-tuple-element.126.gate_ref, ...), custom_call_target="tpu_custom_call" | custom-call | tf_op jit(solution)/shard_map/finish/pallas_call | solution.py:673
  27.0 18.2 %all_to_all.14.hid_ref.tail_ref = bf16[32,56,128]{2,1,0:T(8,128)(2,1)S(1)} all-to-all(bf16[32,56,128]{2,1,0:T(8,128)(2,1)S(1)} %finish.1), channel_id=1, replica_groups=mesh['row'=8,'col'=4] {'row','col'}, dimensions={0} | all-to-all | bytes 917504 | tf_op jit(solution)/shard_map/all_to_all | solution.py:735
  45.2 2.8 %states.3 = (bf16[32,96,128]{2,1,0:T(8,128)(2,1)S(1)}, bf16[32,64,128]{2,1,0:T(8,128)(2,1)S(1)}, f32[32,16,128]{2,1,0:T(8,128)S(1)}, f32[32,72,128]{2,1,0:T(8,128)S(1)}, f32[56,128]{1,0:T(8,128)S(1)}) custom-call(bf16[32,56,128]{2,1,0:T(8,128)(2,1)S(1)} %all_to_all.14.hid_ref.tail_ref, bf16[32,56,128]{2,1,0:T(8,128)(2,1)S(1)} %all_to_all.14.hid_ref.tail_ref, ...), custom_call_target="tpu_custom_call" | custom-call | tf_op jit(solution)/shard_map/states/pallas_call | solution.py:610
  47.9 1.2 %collective-permute-done.8.refs_1_ = f32[56,128]{1,0:T(8,128)S(1)} collective-permute-done((f32[56,128]{1,0:T(8,128)S(1)}, f32[56,128]{1,0:T(8,128)S(1)}, u32[]{:S(2)}, u32[]{:S(2)}) %collective-permute-start.8) | collective-permute-done | bytes 28704 | tf_op jit(solution)/shard_map/ppermute | solution.py:533
  49.1 1.5 %collective-permute-start.11 = (f32[56,128]{1,0:T(8,128)S(1)}, f32[56,128]{1,0:T(8,128)S(1)}, u32[]{:S(2)}, u32[]{:S(2)}) collective-permute-start(f32[56,128]{1,0:T(8,128)S(1)} %get-tuple-element.135.refs_0_), channel_id=1, source_target_pairs={{0,7},{1,6},{2,5},{3,4},{4,3},{5,2},{6,1},{7,0},{8,15},{9,14},{10,... | collective-permute-start | bytes 86024 | tf_op jit(solution)/shard_map/ppermute | solution.py:533
  50.6 0.6 collective-permute-start.10
  51.2 1.0 %collective-permute-start.9 = (f32[56,128]{1,0:T(8,128)S(1)}, f32[56,128]{1,0:T(8,128)S(1)}, u32[]{:S(2)}, u32[]{:S(2)}) collective-permute-start(f32[56,128]{1,0:T(8,128)S(1)} %get-tuple-element.135.refs_0_), channel_id=1, source_target_pairs={{0,3},{1,2},{2,1},{3,0},{4,7},{5,6},{6,5},{7,4},{8,11},{9,10},{10,... | collective-permute-start | bytes 86024 | tf_op jit(solution)/shard_map/ppermute | solution.py:533
  52.2 1.8 %local.6 = (f32[32,96,128]{2,1,0:T(8,128)S(1)}, f32[32,96,128]{2,1,0:T(8,128)S(1)}, bf16[32,64,128]{2,1,0:T(8,128)(2,1)S(1)}) custom-call(bf16[32,56,128]{2,1,0:T(8,128)(2,1)S(1)} %all_to_all.14.hid_ref.tail_ref, bf16[32,56,128]{2,1,0:T(8,128)(2,1)S(1)} %all_to_all.14.hid_ref.tail_ref, bf16[2,336,48]{2,1,0:T(8,128)(2,1)S(1)} %get-tuple-element.87.weight_ref, ...), custom_call_target="tpu_custom_call" | custom-call | tf_op jit(solution)/shard_map/local/pallas_call | solution.py:636
  54.1 0.4 collective-permute-done.9.refs_1_
  54.6 1.2 %collective-permute-start.14 = (f32[56,128]{1,0:T(8,128)S(1)}, f32[56,128]{1,0:T(8,128)S(1)}, u32[]{:S(2)}, u32[]{:S(2)}) collective-permute-start(f32[56,128]{1,0:T(8,128)S(1)} %get-tuple-element.149.refs_0_), channel_id=1, source_target_pairs={{0,25},{1,24},{2,27},{3,26},{4,29},{5,28},{6,31},{7,30},{8,17},{9,... | collective-permute-start | bytes 86024 | tf_op jit(solution)/shard_map/ppermute | solution.py:533
  55.8 0.8 %collective-permute-start.13 = (f32[56,128]{1,0:T(8,128)S(1)}, f32[56,128]{1,0:T(8,128)S(1)}, u32[]{:S(2)}, u32[]{:S(2)}) collective-permute-start(f32[56,128]{1,0:T(8,128)S(1)} %get-tuple-element.149.refs_0_), channel_id=1, source_target_pairs={{0,17},{1,16},{2,19},{3,18},{4,21},{5,20},{6,23},{7,22},{8,25},{9,... | collective-permute-start | bytes 86024 | tf_op jit(solution)/shard_map/ppermute | solution.py:533
  56.5 2.2 %collective-permute-start.12 = (f32[56,128]{1,0:T(8,128)S(1)}, f32[56,128]{1,0:T(8,128)S(1)}, u32[]{:S(2)}, u32[]{:S(2)}) collective-permute-start(f32[56,128]{1,0:T(8,128)S(1)} %get-tuple-element.149.refs_0_), channel_id=1, source_target_pairs={{0,9},{1,8},{2,11},{3,10},{4,13},{5,12},{6,15},{7,14},{8,1},{9,0},... | collective-permute-start | bytes 86024 | tf_op jit(solution)/shard_map/ppermute | solution.py:533
  58.7 1.8 %local.7 = (f32[32,96,128]{2,1,0:T(8,128)S(1)}, f32[32,96,128]{2,1,0:T(8,128)S(1)}, bf16[32,64,128]{2,1,0:T(8,128)(2,1)S(1)}) custom-call(bf16[32,56,128]{2,1,0:T(8,128)(2,1)S(1)} %all_to_all.14.hid_ref.tail_ref, bf16[32,56,128]{2,1,0:T(8,128)(2,1)S(1)} %all_to_all.14.hid_ref.tail_ref, ...), custom_call_target="tpu_custom_call", output_to_operand_aliasing={{0}: (8, {}), {1}: (9, {}), {2}: (10, {})} | custom-call | tf_op jit(solution)/shard_map/local/pallas_call | solution.py:636
  60.5 0.8 %collective-permute-done.13.refs_2_ = f32[56,128]{1,0:T(8,128)S(1)} collective-permute-done((f32[56,128]{1,0:T(8,128)S(1)}, f32[56,128]{1,0:T(8,128)S(1)}, u32[]{:S(2)}, u32[]{:S(2)}) %collective-permute-start.13) | collective-permute-done | bytes 28704 | tf_op jit(solution)/shard_map/ppermute | solution.py:533
  61.4 2.7 %heads.1 = (bf16[48,32,128]{2,1,0:T(8,128)(2,1)}, f32[14,32,128]{2,1,0:T(8,128)}, f32[32,128]{1,0:T(8,128)S(1)}) custom-call(s32[1]{0:T(128)} %bitcast.me_ref, f32[56,128]{1,0:T(8,128)S(1)} %join.11.enter_ref, bf16[32,56,128]{2,1,0:T(8,128)(2,1)S(1)} %all_to_all.14.hid_ref.tail_ref, f32[32,96,128]{2,1,0:T(8,128)S(1)} %get-tuple-element.164.local_ref, ...), custom_call_target="tpu_custom_call" | custom-call | tf_op jit(solution)/shard_map/heads/pallas_call | solution.py:693
  64.1 9.8 %all_to_all.15 = f32[32,1,128]{2,1,0:T(1,128)S(1)} all-to-all(f32[32,1,128]{2,1,0:T(1,128)S(1)} %bitcast.22), channel_id=1, replica_groups=mesh['row'=8,'col'=4] {'row','col'}, dimensions={0} | all-to-all | bytes 32768 | tf_op jit(solution)/shard_map/all_to_all | solution.py:742
  73.9 0.6 reduce_sum.9
  (51 shorter events, 0.6 us)
Async XLA Ops:
  0.6 1.0 %copy-start.14 = (bf16[48,1,128,32]{2,3,1,0:T(8,128)(2,1)S(1)}, bf16[48,1,128,32]{2,3,1,0:T(8,128)(2,1)}, u32[]{:S(2)}) copy-start(bf16[48,1,128,32]{2,3,1,0:T(8,128)(2,1)} %param.15) | copy-start | bytes 1179652
  1.6 1.0 %copy-start.15 = (bf16[48,1,128,32]{2,3,1,0:T(8,128)(2,1)S(1)}, bf16[48,1,128,32]{2,3,1,0:T(8,128)(2,1)}, u32[]{:S(2)}) copy-start(bf16[48,1,128,32]{2,3,1,0:T(8,128)(2,1)} %param.15) | copy-start | bytes 1179652
  1.9 1.8 %copy-start.2 = (bf16[2,320,48]{1,2,0:T(8,128)(2,1)S(1)}, bf16[2,320,48]{1,2,0:T(8,128)(2,1)}, u32[]{:S(2)}) copy-start(bf16[2,320,48]{1,2,0:T(8,128)(2,1)} %param.17) | copy-start | bytes 184324
  1.9 1.8 %copy-start.4 = (f32[2,224,4]{1,2,0:T(4,128)S(1)}, f32[2,224,4]{1,2,0:T(4,128)}, u32[]{:S(2)}) copy-start(f32[2,224,4]{1,2,0:T(4,128)} %param.21) | copy-start | bytes 21508
  1.9 1.8 %copy-start.6 = (f32[2,224]{1,0:T(2,128)S(1)}, f32[2,224]{1,0:T(2,128)}, u32[]{:S(2)}) copy-start(f32[2,224]{1,0:T(2,128)} %conv_bias_ref.1) | copy-start | bytes 5380
  1.9 1.8 %copy-start.7 = (bf16[2,3,48]{2,0,1:T(2,128)(2,1)S(1)}, bf16[2,3,48]{2,0,1:T(2,128)(2,1)}, u32[]{:S(2)}) copy-start(bf16[2,3,48]{2,0,1:T(2,128)(2,1)} %param.18) | copy-start | bytes 1732
  1.9 1.8 %copy-start.8 = (f32[2,48]{1,0:T(2,128)S(1)}, f32[2,48]{1,0:T(2,128)}, u32[]{:S(2)}) copy-start(f32[2,48]{1,0:T(2,128)} %gain_ref.1) | copy-start | bytes 1156
  2.0 1.8 %copy-start.9 = (f32[2,3]{1,0:T(2,128)S(1)}, f32[2,3]{1,0:T(2,128)}, u32[]{:S(2)}) copy-start(f32[2,3]{1,0:T(2,128)} %dt_bias_ref.1) | copy-start | bytes 76
  2.0 1.8 %copy-start.10 = (f32[2,3]{1,0:T(2,128)S(1)}, f32[2,3]{1,0:T(2,128)}, u32[]{:S(2)}) copy-start(f32[2,3]{1,0:T(2,128)} %rate_ref.1) | copy-start | bytes 76
  2.0 1.8 %copy-start.11 = (f32[2,3]{1,0:T(2,128)S(1)}, f32[2,3]{1,0:T(2,128)}, u32[]{:S(2)}) copy-start(f32[2,3]{1,0:T(2,128)} %skip_ref.1) | copy-start | bytes 76
  2.0 1.8 %copy-start.12 = (f32[2,96]{1,0:T(2,128)S(1)}, f32[2,96]{1,0:T(2,128)}, u32[]{:S(2)}) copy-start(f32[2,96]{1,0:T(2,128)} %out_gain_ref.1) | copy-start | bytes 2308
  2.0 7.8 %collective-permute-start = (bf16[48,128]{1,0:T(8,128)(2,1)S(1)}, bf16[48,128]{1,0:T(8,128)(2,1)S(1)}, u32[]{:S(2)}, u32[]{:S(2)}) collective-permute-start(bf16[48,128]{1,0:T(8,128)(2,1)S(1)} %tail.1), channel_id=1, source_target_pairs={{0,1},{1,2},{2,3},{3,4},{4,5},{5,6},{6,7},{7,8},{8,9},{9,10},{10,1... | collective-permute-start | bytes 36872 | tf_op jit(solution)/shard_map/ppermute | solution.py:732
  12.5 1.2 %collective-permute-start.1 = (f32[56,128]{1,0:T(8,128)S(1)}, f32[56,128]{1,0:T(8,128)S(1)}, u32[]{:S(2)}, u32[]{:S(2)}) collective-permute-start(f32[56,128]{1,0:T(8,128)S(1)} %get-tuple-element.90.refs_0_), channel_id=1, source_target_pairs={{0,1},{1,0},{2,3},{3,2},{4,5},{5,4},{6,7},{7,6},{8,9},{9,8},{10,11... | collective-permute-start | bytes 86024 | tf_op jit(solution)/shard_map/ppermute | solution.py:533
  13.8 4.8 %collective-permute-start.4 = (f32[56,128]{1,0:T(8,128)S(1)}, f32[56,128]{1,0:T(8,128)S(1)}, u32[]{:S(2)}, u32[]{:S(2)}) collective-permute-start(f32[56,128]{1,0:T(8,128)S(1)} %get-tuple-element.96.refs_0_), channel_id=1, source_target_pairs={{0,7},{1,6},{2,5},{3,4},{4,3},{5,2},{6,1},{7,0},{8,15},{9,14},{10,... | collective-permute-start | bytes 86024 | tf_op jit(solution)/shard_map/ppermute | solution.py:533
  13.9 4.8 %collective-permute-start.3 = (f32[56,128]{1,0:T(8,128)S(1)}, f32[56,128]{1,0:T(8,128)S(1)}, u32[]{:S(2)}, u32[]{:S(2)}) collective-permute-start(f32[56,128]{1,0:T(8,128)S(1)} %get-tuple-element.96.refs_0_), channel_id=1, source_target_pairs={{0,5},{1,4},{2,7},{3,6},{4,1},{5,0},{6,3},{7,2},{8,13},{9,12},{10,... | collective-permute-start | bytes 86024 | tf_op jit(solution)/shard_map/ppermute | solution.py:533
  13.9 4.7 %collective-permute-start.2 = (f32[56,128]{1,0:T(8,128)S(1)}, f32[56,128]{1,0:T(8,128)S(1)}, u32[]{:S(2)}, u32[]{:S(2)}) collective-permute-start(f32[56,128]{1,0:T(8,128)S(1)} %get-tuple-element.96.refs_0_), channel_id=1, source_target_pairs={{0,3},{1,2},{2,1},{3,0},{4,7},{5,6},{6,5},{7,4},{8,11},{9,10},{10,... | collective-permute-start | bytes 86024 | tf_op jit(solution)/shard_map/ppermute | solution.py:533
  18.7 6.5 %copy-start.1 = (bf16[2,48,96]{2,1,0:T(8,128)(2,1)S(1)}, bf16[2,48,96]{2,1,0:T(8,128)(2,1)}, u32[]{:S(2)}) copy-start(bf16[2,48,96]{2,1,0:T(8,128)(2,1)} %out_proj_ref.3) | copy-start | bytes 55300
  18.7 5.9 %collective-permute-start.7 = (f32[56,128]{1,0:T(8,128)S(1)}, f32[56,128]{1,0:T(8,128)S(1)}, u32[]{:S(2)}, u32[]{:S(2)}) collective-permute-start(f32[56,128]{1,0:T(8,128)S(1)} %get-tuple-element.110.refs_0_), channel_id=1, source_target_pairs={{0,25},{1,24},{2,27},{3,26},{4,29},{5,28},{6,31},{7,30},{8,17},{9,... | collective-permute-start | bytes 86024 | tf_op jit(solution)/shard_map/ppermute | solution.py:533
  20.9 4.2 %collective-permute-start.6 = (f32[56,128]{1,0:T(8,128)S(1)}, f32[56,128]{1,0:T(8,128)S(1)}, u32[]{:S(2)}, u32[]{:S(2)}) collective-permute-start(f32[56,128]{1,0:T(8,128)S(1)} %get-tuple-element.110.refs_0_), channel_id=1, source_target_pairs={{0,17},{1,16},{2,19},{3,18},{4,21},{5,20},{6,23},{7,22},{8,25},{9,... | collective-permute-start | bytes 86024 | tf_op jit(solution)/shard_map/ppermute | solution.py:533
  20.9 4.2 %collective-permute-start.5 = (f32[56,128]{1,0:T(8,128)S(1)}, f32[56,128]{1,0:T(8,128)S(1)}, u32[]{:S(2)}, u32[]{:S(2)}) collective-permute-start(f32[56,128]{1,0:T(8,128)S(1)} %get-tuple-element.110.refs_0_), channel_id=1, source_target_pairs={{0,9},{1,8},{2,11},{3,10},{4,13},{5,12},{6,15},{7,14},{8,1},{9,0},... | collective-permute-start | bytes 86024 | tf_op jit(solution)/shard_map/ppermute | solution.py:533
  47.9 1.2 %collective-permute-start.8 = (f32[56,128]{1,0:T(8,128)S(1)}, f32[56,128]{1,0:T(8,128)S(1)}, u32[]{:S(2)}, u32[]{:S(2)}) collective-permute-start(f32[56,128]{1,0:T(8,128)S(1)} %get-tuple-element.129.refs_0_), channel_id=1, source_target_pairs={{0,1},{1,0},{2,3},{3,2},{4,5},{5,4},{6,7},{7,6},{8,9},{9,8},{10,11... | collective-permute-start | bytes 86024 | tf_op jit(solution)/shard_map/ppermute | solution.py:533
  49.1 4.8 %collective-permute-start.11 = (f32[56,128]{1,0:T(8,128)S(1)}, f32[56,128]{1,0:T(8,128)S(1)}, u32[]{:S(2)}, u32[]{:S(2)}) collective-permute-start(f32[56,128]{1,0:T(8,128)S(1)} %get-tuple-element.135.refs_0_), channel_id=1, source_target_pairs={{0,7},{1,6},{2,5},{3,4},{4,3},{5,2},{6,1},{7,0},{8,15},{9,14},{10,... | collective-permute-start | bytes 86024 | tf_op jit(solution)/shard_map/ppermute | solution.py:533
  50.6 3.4 %collective-permute-start.10 = (f32[56,128]{1,0:T(8,128)S(1)}, f32[56,128]{1,0:T(8,128)S(1)}, u32[]{:S(2)}, u32[]{:S(2)}) collective-permute-start(f32[56,128]{1,0:T(8,128)S(1)} %get-tuple-element.135.refs_0_), channel_id=1, source_target_pairs={{0,5},{1,4},{2,7},{3,6},{4,1},{5,0},{6,3},{7,2},{8,13},{9,12},{10,... | collective-permute-start | bytes 86024 | tf_op jit(solution)/shard_map/ppermute | solution.py:533
  51.2 3.3 %collective-permute-start.9 = (f32[56,128]{1,0:T(8,128)S(1)}, f32[56,128]{1,0:T(8,128)S(1)}, u32[]{:S(2)}, u32[]{:S(2)}) collective-permute-start(f32[56,128]{1,0:T(8,128)S(1)} %get-tuple-element.135.refs_0_), channel_id=1, source_target_pairs={{0,3},{1,2},{2,1},{3,0},{4,7},{5,6},{6,5},{7,4},{8,11},{9,10},{10,... | collective-permute-start | bytes 86024 | tf_op jit(solution)/shard_map/ppermute | solution.py:533
  54.5 6.8 %copy-start = (s32[14,1,32,128]{3,2,1,0:T(8,128)S(1)}, s32[14,1,32,128]{3,2,1,0:T(8,128)}, u32[]{:S(2)}) copy-start(s32[14,1,32,128]{3,2,1,0:T(8,128)} %param.29) | copy-start | bytes 688132
  54.5 6.8 %copy-start.3 = (s32[1,32,128]{2,1,0:T(8,128)S(1)}, s32[1,32,128]{2,1,0:T(8,128)}, u32[]{:S(2)}) copy-start(s32[1,32,128]{2,1,0:T(8,128)} %param.28) | copy-start | bytes 49156
  54.6 6.8 %copy-start.5 = (bf16[14,48]{1,0:T(8,128)(2,1)S(1)}, bf16[14,48]{1,0:T(8,128)(2,1)}, u32[]{:S(2)}) copy-start(bf16[14,48]{1,0:T(8,128)(2,1)} %head_ref.1) | copy-start | bytes 4036
  54.6 6.8 %copy-start.13 = (f32[14]{0:T(128)S(1)}, f32[14]{0:T(128)}, u32[]{:S(2)}) copy-start(f32[14]{0:T(128)} %param.27) | copy-start | bytes 172
  54.6 5.9 %collective-permute-start.14 = (f32[56,128]{1,0:T(8,128)S(1)}, f32[56,128]{1,0:T(8,128)S(1)}, u32[]{:S(2)}, u32[]{:S(2)}) collective-permute-start(f32[56,128]{1,0:T(8,128)S(1)} %get-tuple-element.149.refs_0_), channel_id=1, source_target_pairs={{0,25},{1,24},{2,27},{3,26},{4,29},{5,28},{6,31},{7,30},{8,17},{9,... | collective-permute-start | bytes 86024 | tf_op jit(solution)/shard_map/ppermute | solution.py:533
  55.8 5.5 %collective-permute-start.13 = (f32[56,128]{1,0:T(8,128)S(1)}, f32[56,128]{1,0:T(8,128)S(1)}, u32[]{:S(2)}, u32[]{:S(2)}) collective-permute-start(f32[56,128]{1,0:T(8,128)S(1)} %get-tuple-element.149.refs_0_), channel_id=1, source_target_pairs={{0,17},{1,16},{2,19},{3,18},{4,21},{5,20},{6,23},{7,22},{8,25},{9,... | collective-permute-start | bytes 86024 | tf_op jit(solution)/shard_map/ppermute | solution.py:533
  56.5 4.7 %collective-permute-start.12 = (f32[56,128]{1,0:T(8,128)S(1)}, f32[56,128]{1,0:T(8,128)S(1)}, u32[]{:S(2)}, u32[]{:S(2)}) collective-permute-start(f32[56,128]{1,0:T(8,128)S(1)} %get-tuple-element.149.refs_0_), channel_id=1, source_target_pairs={{0,9},{1,8},{2,11},{3,10},{4,13},{5,12},{6,15},{7,14},{8,1},{9,0},... | collective-permute-start | bytes 86024 | tf_op jit(solution)/shard_map/ppermute | solution.py:533
